TPU v7x, 32 devices: a whole 2x2x4 slice. The times are simulated.
32 devices in a mesh: ops: 8 (over y, x, core), sec: 4 (over z).
Axes of the slice: x: 2, y: 2, z: 4, core: 2. Of those that a mesh axis runs over, the one named last changes fastest.
Arguments:
- wavefunction: float32 [8, 128, 128], P('sec'), may hold values from -6 to 6
- hamiltonian_diag: float32 [8, 128, 128], P('sec'), may hold values from -6 to 6
- mirror_coupling: float32 [8], P('sec'), may hold values from 0.5 to 1.5, as said below
- left_env: float32 [192, 8, 128, 128], P('ops', 'sec'), as said below
- right_env: float32 [192, 128, 128], P('ops'), as said below
- term_source: int32 [192, 8], P('ops', 'sec'), may hold values from -1 to 7, as said below
Outputs:
- new_wave: float32 [8, 128, 128], P('sec', 'ops')
- new_sigma: float32 [8, 128, 128], P('sec', 'ops')
- energy: float32 [1], replicated
Inputs may be any that keep to these rules, and one draw needn't show every extreme that they name: `term_source`: for each term the non-negative entries over the 8 target sectors are distinct; terms 0 and 1 have a block for every sector; for even k, term k + 1 maps sector t into sector s exactly where term k maps s into t. For even k and term_source[k, s] = t >= 0, left_env[k + 1, t] is the transpose of left_env[k, s]. For even k, right_env[k + 1] is the transpose of right_env[k]. mirror_coupling[s] equals mirror_coupling[s + 4].
All inputs are finite; a program needn't handle non-finite values.
Results may differ from a plain program's by a relative error of at most 0.0003.
Values sent between devices are 32-bit elements; how exact they have to be, the bound alone decides.
No kernel may reach another device: no remote copies, remote signals or barrier semaphores. Data moves between devices by JAX's collectives and lax.ppermute only.
A program may use at most 64 MiB of HBM per device.

v0:
```python
import jax
import jax.numpy as jnp
from jax import lax
from jax.sharding import PartitionSpec as P

HIGH = lax.Precision.HIGHEST


def full_blocks(vector):
    return lax.all_gather(vector, "sec", axis=0, tiled=True)


def contract_terms(vector, left_env, right_env, term_source):
    whole = full_blocks(vector)
    picked = whole[jnp.maximum(term_source, 0)]
    picked = jnp.where((term_source >= 0)[:, :, None, None], picked, jnp.zeros_like(picked))
    inner = jnp.einsum("ksij,ksjl->ksil", left_env, picked, precision=HIGH)
    return (jnp.einsum("ksil,kml->sim", inner, right_env, precision=HIGH), whole)


def mirror_term(vector, whole, mirror_coupling):
    sectors = whole.shape[0]
    owned = vector.shape[0]
    start = (lax.axis_index("sec") * owned + sectors // 2) % sectors
    partner = lax.dynamic_slice_in_dim(whole, start, owned, 0)
    return mirror_coupling[:, None, None] * jnp.swapaxes(partner, 1, 2)


def sector_sums(values):
    return lax.psum(values, "sec")


def summed_whole(partial_sigma):
    return lax.psum(partial_sigma, "ops")


def correction_step(wave, sigma, diag, reducer):
    norm_sq, correlation = reducer((jnp.sum(wave * wave), jnp.sum(wave * sigma)))
    scale = jnp.sqrt(norm_sq)
    unit = wave / scale
    rayleigh = correlation / norm_sq
    resid = sigma / scale - rayleigh * unit
    offset = diag - rayleigh
    correction = resid / (1.0 + offset * offset)
    along = reducer(jnp.sum(unit * correction))
    correction = correction - along * unit
    corr_sq = reducer(jnp.sum(correction * correction))
    direction = correction / jnp.sqrt(corr_sq)
    return (scale, rayleigh, resid, direction)


def ritz_pair(rayleigh, coupling, curvature):
    half_gap = 0.5 * (curvature - rayleigh)
    energy = 0.5 * (rayleigh + curvature) - jnp.sqrt(half_gap * half_gap + coupling * coupling)
    angle = 0.5 * jnp.arctan2(-coupling, half_gap)
    return (energy, jnp.cos(angle), jnp.sin(angle))


def body(wavefunction, hamiltonian_diag, mirror_coupling, left_env, right_env, term_source):
    rows = wavefunction.shape[1] // lax.axis_size("ops")
    first = lax.axis_index("ops") * rows

    def own_rows(values):
        return lax.dynamic_slice_in_dim(values, first, rows, 1)

    partial_sigma, whole_wave = contract_terms(wavefunction, left_env, right_env, term_source)
    mirrored = mirror_term(wavefunction, whole_wave, mirror_coupling)
    sigma = summed_whole(partial_sigma) + mirrored
    scale, rayleigh, resid, direction = correction_step(
        wavefunction, sigma, hamiltonian_diag, sector_sums
    )
    dir_partial, whole_dir = contract_terms(direction, left_env, right_env, term_source)
    dir_sigma = summed_whole(dir_partial)
    dir_sigma = dir_sigma + mirror_term(direction, whole_dir, mirror_coupling)
    coupling, curvature = sector_sums((jnp.sum(direction * resid), jnp.sum(direction * dir_sigma)))
    energy, cos_part, sin_part = ritz_pair(rayleigh, coupling, curvature)
    new_wave = own_rows(cos_part * wavefunction + sin_part * scale * direction)
    new_sigma = own_rows(cos_part * sigma + sin_part * scale * dir_sigma)
    return (new_wave, new_sigma, jnp.reshape(energy, (1,)))


def solution(mesh):
    placed = (
        P("sec", None, None),
        P("sec", None, None),
        P("sec"),
        P("ops", "sec", None, None),
        P("ops", None, None),
        P("ops", "sec"),
    )
    return jax.shard_map(
        body,
        mesh=mesh,
        in_specs=placed,
        out_specs=(P("sec", "ops", None), P("sec", "ops", None), P()),
        check_vma=False,
    )
```

profile of v0, /device:TPU:0, one launch (start us, length us, event | category | flops | bytes accessed | tf_op | source)
XLA Modules:
  0.0 258.8 jit_solution(4616902309543094478)
XLA Ops:
  7.2 0.0 all-reduce.5.cloned.1.call-start
  7.2 0.8 broadcast_compare_fusion
  8.1 0.8 broadcast_maximum_fusion
  8.8 0.1 copy.17
  8.9 0.1 reshape.14
  9.0 19.3 %all_gather.6 = f32[8,128,128]{2,1,0:T(8,128)} all-gather(f32[2,128,128]{2,1,0:T(8,128)} %param.6), channel_id=1, replica_groups=mesh['ops'=8,'sec'=4] {'sec'}, dimensions={0}, use_global_device_ids=true | all-gather | bytes 655360 | tf_op jit(solution)/shard_map/all_gather | solution.py:10
  28.3 3.5 %gather_fusion = f32[48,128,128]{2,1,0:T(8,128)} fusion(f32[8,128,128]{2,1,0:T(8,128)} %all_gather.6, s32[1024]{0:T(1024)S(1)} %pad_clamp_fusion), kind=kCustom, calls=%fused_computation | custom fusion | bytes 6291648 | tf_op jit(solution)/shard_map/gather | solution.py:15
  31.7 3.6 %copy.18 = f32[24,2,128,128]{2,3,0,1:T(8,128)} copy(f32[24,2,128,128]{3,2,1,0:T(8,128)} %bitcast.35) | data formatting | bytes 6291456 | tf_op jit(solution)/shard_map/gather | solution.py:15
  35.3 8.9 %fusion.6 = f32[24,2,128,128]{3,2,0,1:T(8,128)S(1)} fusion(f32[24,2,128,128]{2,3,0,1:T(8,128)} %copy.18, f32[24,2,128,128]{3,2,1,0:T(8,128)S(1)} %copy-done, pred[24,2]{0,1:T(4,128)(4,1)S(1)} %broadcast_compare_fusion), kind=kOutput, calls=%fused_computation.8 | convolution fusion | flops 1208745984 | bytes 9437232 | tf_op jit(solution)/shard_map/ksij,ksjl->ksil/dot_general | solution.py:17
  44.2 5.8 %fusion.16 = f32[2,128,128]{2,1,0:T(8,128)} fusion(f32[24,128,128]{2,1,0:T(8,128)S(1)} %copy-done.1, f32[24,2,128,128]{3,2,0,1:T(8,128)S(1)} %fusion.6), kind=kOutput, calls=%fused_computation.18 | convolution fusion | flops 1207959552 | bytes 4849664 | tf_op jit(solution)/shard_map/ksil,kml->sim/dot_general | solution.py:18
  50.0 0.0 all-reduce.7.cloned.1.call-start
  50.1 0.9 constant_dynamic-slice_fusion.1
  51.0 0.1 copy.30
  51.1 52.0 %all-reduce.5.cloned.1.call-done = f32[2,128,128]{2,1,0:T(8,128)} async-done(((f32[2,128,128]{2,1,0:T(8,128)}), f32[2,128,128]{2,1,0:T(8,128)}) %all-reduce.5.cloned.1.call-update) | async-done | bytes 131088 | tf_op jit(solution)/shard_map/psum | solution.py:34
  103.1 1.6 multiply_reduce_fusion.5
  104.7 12.3 %all-reduce.1 = (f32[]{:T(128)}, f32[]{:T(128)}) all-reduce(f32[]{:T(128)} %get-tuple-element.6, f32[]{:T(128)} %get-tuple-element.5), channel_id=1, replica_groups=mesh['ops'=8,'sec'=4] {'sec'}, use_global_device_ids=true, to_apply=%region_4.5 | all-reduce | flops 2 | bytes 16 | tf_op jit(solution)/shard_map/psum | solution.py:30
  119.1 1.6 multiply_reduce_fusion.3
  120.6 9.0 %psum.59 = f32[]{:T(128)} all-reduce(f32[]{:T(128)} %get-tuple-element.12), channel_id=1, replica_groups=mesh['ops'=8,'sec'=4] {'sec'}, use_global_device_ids=true, to_apply=%region_6.7 | all-reduce | flops 1 | bytes 8 | tf_op jit(solution)/shard_map/psum | solution.py:30
  129.6 1.3 multiply_reduce_fusion.2
  130.9 11.0 %psum.60 = f32[]{:T(128)} all-reduce(f32[]{:T(128)} %multiply_reduce_fusion.2), channel_id=1, replica_groups=mesh['ops'=8,'sec'=4] {'sec'}, use_global_device_ids=true, to_apply=%region_8.9 | all-reduce | flops 1 | bytes 8 | tf_op jit(solution)/shard_map/psum | solution.py:30
  142.6 1.6 broadcast_divide_fusion
  144.2 15.6 %all_gather.7 = f32[8,128,128]{2,1,0:T(8,128)} all-gather(f32[2,128,128]{2,1,0:T(8,128)S(1)} %broadcast_divide_fusion), channel_id=1, replica_groups=mesh['ops'=8,'sec'=4] {'sec'}, dimensions={0}, use_global_device_ids=true | all-gather | bytes 655360 | tf_op jit(solution)/shard_map/all_gather | solution.py:10
  159.8 3.5 %gather_fusion.1 = f32[48,128,128]{2,1,0:T(8,128)} fusion(f32[8,128,128]{2,1,0:T(8,128)} %all_gather.7, s32[1024]{0:T(1024)S(1)} %pad_clamp_fusion), kind=kCustom, calls=%fused_computation.1 | custom fusion | bytes 6291648 | tf_op jit(solution)/shard_map/gather | solution.py:15
  163.2 3.6 %copy.22 = f32[24,2,128,128]{2,3,0,1:T(8,128)} copy(f32[24,2,128,128]{3,2,1,0:T(8,128)} %bitcast.34) | data formatting | bytes 6291456 | tf_op jit(solution)/shard_map/gather | solution.py:15
  166.8 8.9 %fusion.4 = f32[24,2,128,128]{3,2,0,1:T(8,128)S(1)} fusion(f32[24,2,128,128]{2,3,0,1:T(8,128)} %copy.22, f32[24,2,128,128]{3,2,1,0:T(8,128)S(1)} %copy-done, pred[24,2]{0,1:T(4,128)(4,1)S(1)} %broadcast_compare_fusion), kind=kOutput, calls=%fused_computation.6 | convolution fusion | flops 1208745984 | bytes 9437232 | tf_op jit(solution)/shard_map/ksij,ksjl->ksil/dot_general | solution.py:17
  175.7 5.8 %fusion.21 = f32[2,128,128]{2,1,0:T(8,128)} fusion(f32[24,128,128]{2,1,0:T(8,128)S(1)} %copy-done.2, f32[24,2,128,128]{3,2,0,1:T(8,128)S(1)} %fusion.4), kind=kOutput, calls=%fused_computation.19 | convolution fusion | flops 1207959552 | bytes 4849664 | tf_op jit(solution)/shard_map/ksil,kml->sim/dot_general | solution.py:18
  181.5 1.6 constant_dynamic-slice_fusion
  183.0 1.7 copy.31
  184.7 46.7 %all-reduce.7.cloned.1.call-done = f32[2,128,128]{2,1,0:T(8,128)} async-done(((f32[2,128,128]{2,1,0:T(8,128)}), f32[2,128,128]{2,1,0:T(8,128)}) %all-reduce.7.cloned.1.call-update) | async-done | bytes 131088 | tf_op jit(solution)/shard_map/psum | solution.py:34
  231.4 2.3 multiply_reduce_fusion
  233.7 12.3 %all-reduce = (f32[]{:T(128)}, f32[]{:T(128)}) all-reduce(f32[]{:T(128)} %get-tuple-element.4, f32[]{:T(128)} %get-tuple-element.3), channel_id=1, replica_groups=mesh['ops'=8,'sec'=4] {'sec'}, use_global_device_ids=true, to_apply=%region_10.11 | all-reduce | flops 2 | bytes 16 | tf_op jit(solution)/shard_map/psum | solution.py:30
  249.5 1.3 fusion.26
  (15 shorter events, 0.1 us)
Async XLA Ops:
  7.2 28.2 %copy-start = (f32[24,2,128,128]{3,2,1,0:T(8,128)S(1)}, f32[24,2,128,128]{3,2,1,0:T(8,128)}, u32[]{:S(2)}) copy-start(f32[24,2,128,128]{3,2,1,0:T(8,128)} %param.9) | copy-start | bytes 9437188
  7.2 95.9 %all-reduce.5.cloned.1.call-start = ((), (), s32[]{:S(2)}) async-start(), calls=%async_computation | async-start | bytes 262144 | tf_op jit(solution)/shard_map/psum | solution.py:34
  35.3 8.9 %copy-start.1 = (f32[24,128,128]{2,1,0:T(8,128)S(1)}, f32[24,128,128]{2,1,0:T(8,128)}, u32[]{:S(2)}) copy-start(f32[24,128,128]{2,1,0:T(8,128)} %param.10) | copy-start | bytes 4718596
  44.2 58.9 %copy-start.3 = (f32[2,128,128]{2,1,0:T(8,128)S(1)}, f32[2,128,128]{2,1,0:T(8,128)}, u32[]{:S(2)}) copy-start(f32[2,128,128]{2,1,0:T(8,128)} %param.6) | copy-start | bytes 393220
  44.2 58.9 %copy-start.5 = (f32[2]{0:T(128)S(1)}, f32[2]{0:T(128)}, u32[]{:S(2)}) copy-start(f32[2]{0:T(128)} %param.8) | copy-start | bytes 28
  50.0 181.4 %all-reduce.7.cloned.1.call-start = ((), (), s32[]{:S(2)}) async-start(), calls=%async_computation.1 | async-start | bytes 262144 | tf_op jit(solution)/shard_map/psum | solution.py:34
  120.6 21.2 %copy-start.4 = (f32[2,128,128]{2,1,0:T(8,128)}, f32[2,128,128]{2,1,0:T(8,128)S(1)}, u32[]{:S(2)}) copy-start(f32[2,128,128]{2,1,0:T(8,128)S(1)} %get-tuple-element.13) | copy-start | bytes 393220
  166.8 8.9 %copy-start.2 = (f32[24,128,128]{2,1,0:T(8,128)S(1)}, f32[24,128,128]{2,1,0:T(8,128)}, u32[]{:S(2)}) copy-start(f32[24,128,128]{2,1,0:T(8,128)} %param.10) | copy-start | bytes 4718596
Sparse Core Ops, SparseCore 0:
  50.1 52.9 all-reduce.4
  181.6 49.7 all-reduce.6
where the time goes:
time: 259 us
  waiting for transfers between devices  98.7 us (38%)
  blocking collectives  79.4 us (31%)
  matrix products  29.2 us (11%)
  between operations  21.5 us (8%)
  local copies, waits for them, and re-layouts  18.5 us (7%)
  other arithmetic  11.3 us (4%)
    psum x2, waiting for transfers between devices, summed_whole(): return lax.psum(partial_sigma, 'ops')  98.7 us
    psum x4, blocking collectives, sector_sums(): return lax.psum(values, 'sec')  44.5 us
    all_gather x2, blocking collectives, full_blocks(): return lax.all_gather(vector, 'sec', axis=0, tiled=True)  34.9 us
    dot_general x2, matrix products, contract_terms(): inner = jnp.einsum('ksij,ksjl->ksil', left_env, picked, precision=HIGH)  17.7 us
    gather x4, local copies, waits for them, and re-layouts, contract_terms(): picked = whole[jnp.maximum(term_source, 0)]  14.1 us
    dot_general x2, matrix products, contract_terms(): jnp.einsum('ksil,kml->sim', inner, right_env, precision=HIGH)  11.5 us
  transfers between devices with their start and end apart: 2, of which 2 were waited for; matrix products, arithmetic and copies ran while one was open for 2% of the time, Pallas kernels for 0%

commit v1 on v0

v1 whole, which is shorter than its diff:
```python
import functools

import jax
import jax.numpy as jnp
from jax import lax
from jax.experimental import pallas as pl
from jax.experimental.pallas import tpu as pltpu
from jax.sharding import PartitionSpec as P

F32 = jnp.float32
BF16 = jnp.bfloat16
VMEM = pl.BlockSpec(memory_space=pltpu.VMEM)
SMEM = pl.BlockSpec(memory_space=pltpu.SMEM)
PAD = 8
LIMIT = 48 * 1024 * 1024


def call(kernel, out_shape, in_specs, scratch=(), flops=0):
    return pl.pallas_call(
        kernel,
        out_shape=out_shape,
        in_specs=in_specs,
        out_specs=jax.tree.map(lambda _: VMEM, out_shape),
        scratch_shapes=list(scratch),
        compiler_params=pltpu.CompilerParams(vmem_limit_bytes=LIMIT),
        cost_estimate=pl.CostEstimate(flops=flops, bytes_accessed=1 << 20, transcendentals=0),
    )


def split(values):
    high = values.astype(BF16)
    return high, (values - high.astype(F32)).astype(BF16)


def total(values):
    return jnp.sum(values, keepdims=True)


def store_vector(slots, at, block):
    size = block.shape[0]
    high, low = split(block)
    slots[at, :size, :size] = high
    slots[at, :size, size:] = low
    slots[at, size:, :size] = high
    slots[at, size:, size:] = jnp.zeros_like(high)


def apply_terms(source_ref, left_ref, right_ref, slots, stacked, weights, where, empty):
    terms, owned, size, _ = left_ref.shape
    for k in range(terms):
        high, low = split(right_ref[k])
        base = 2 * k * size
        weights[base : base + size, :size] = high
        weights[base : base + size, size:] = low
        weights[base + size : base + 2 * size, :size] = high
        weights[base + size : base + 2 * size, size:] = jnp.zeros_like(high)
    for k in range(terms):
        base = 2 * (k ^ 1) * size
        for s in range(owned):
            t = source_ref[k, s]
            at = jnp.where(t < 0, empty, where(jnp.maximum(t, 0)))
            pair = jnp.concatenate(split(left_ref[k, s]), axis=1)
            both = jnp.dot(pair, slots[at], preferred_element_type=F32)
            high, low = split(both[:, :size] + both[:, size:])
            stacked[s * size : (s + 1) * size, base : base + size] = high
            stacked[s * size : (s + 1) * size, base + size : base + 2 * size] = low
    both = jnp.dot(stacked[...], weights[...], preferred_element_type=F32)
    return both[:, :size] + both[:, size:]


def place(n_sec, core, plane):
    def where(t):
        return jnp.bitwise_xor(t // 2, plane) + n_sec * jnp.bitwise_xor(t % 2, core)

    return where


def first_kernel(n_sec, n_ops, source_ref, at_ref, coupling_ref, left_ref, right_ref, own_ref, other_ref,
                 out_ref, slots, stacked, weights):
    core, plane = at_ref[0], at_ref[1]
    size = own_ref.shape[1]
    where = place(n_sec, core, plane)
    for m in range(n_sec):
        store_vector(slots, m, own_ref[m])
        store_vector(slots, n_sec + m, other_ref[m])
    slots[2 * n_sec] = jnp.zeros_like(slots[2 * n_sec])
    part = apply_terms(source_ref, left_ref, right_ref, slots, stacked, weights, where, 2 * n_sec)
    mirror = jnp.bitwise_xor((plane + n_sec // 2) % n_sec, plane)
    corr = jnp.zeros((1, 1), F32)
    for s in range(2):
        mine = core == s
        partner = jnp.where(mine, own_ref[mirror], other_ref[mirror])
        vec = jnp.where(mine, own_ref[0], other_ref[0])
        block = part[s * size : (s + 1) * size] + (coupling_ref[s] / n_ops) * partner.T
        out_ref[s, :size] = block
        corr += total(vec * block)
    for s in range(2):
        out_ref[s, size:] = jnp.broadcast_to(corr, (PAD, size))


def correction_kernel(n_sec, sums_ref, own_ref, other_ref, diag_ref, out_ref, scalar_ref):
    size = own_ref.shape[1]
    norm_sq = total(own_ref[...] * own_ref[...]).reshape(1, 1) + total(other_ref[...] * other_ref[...]).reshape(1, 1)
    corr = jnp.sum(sums_ref[:, size : size + 1, :1], axis=0)
    scale = jnp.sqrt(norm_sq)
    rayleigh = corr / norm_sq
    for m in range(n_sec):
        sigma = sums_ref[m, :size]
        resid = sigma / scale - rayleigh * (own_ref[m] / scale)
        offset = diag_ref[m] - rayleigh
        out_ref[m] = resid / (1.0 + offset * offset)
    out_ref[n_sec] = sums_ref[0, :size]
    lane = lax.broadcasted_iota(jnp.int32, (PAD, size), 1)
    scalar_ref[...] = jnp.where(lane < size // 2, scale, rayleigh)


def second_kernel(n_sec, n_ops, source_ref, at_ref, coupling_ref, left_ref, right_ref, own_ref, other_ref,
                  mine_ref, theirs_ref, scalar_ref, out_ref, dir_ref, slots, stacked, weights, direction):
    core, plane = at_ref[0], at_ref[1]
    size = own_ref.shape[1]
    where = place(n_sec, core, plane)
    scale = scalar_ref[:1, :1]
    rayleigh = scalar_ref[:1, size // 2 : size // 2 + 1]
    pieces = [(mine_ref, own_ref, m) for m in range(n_sec)] + [(theirs_ref, other_ref, m) for m in range(n_sec)]
    acc = jnp.zeros((size, size), F32)
    for corr_ref, wave_ref, m in pieces:
        acc += corr_ref[m] * wave_ref[m]
    along = total(acc) / scale
    acc = jnp.zeros((size, size), F32)
    for i, (corr_ref, wave_ref, m) in enumerate(pieces):
        rest = corr_ref[m] - along * (wave_ref[m] / scale)
        direction[i] = rest
        acc += rest * rest
    norm = jnp.sqrt(total(acc))
    for i in range(2 * n_sec):
        block = direction[i] / norm
        direction[i] = block
        store_vector(slots, i, block)
    slots[2 * n_sec] = jnp.zeros_like(slots[2 * n_sec])
    part = apply_terms(source_ref, left_ref, right_ref, slots, stacked, weights, where, 2 * n_sec)
    mirror = jnp.bitwise_xor((plane + n_sec // 2) % n_sec, plane)
    curvature = jnp.zeros((1, 1), F32)
    coupling = jnp.zeros((1, 1), F32)
    rows = size // n_ops
    for s in range(2):
        mine = core == s
        at = jnp.where(mine, 0, n_sec)
        vec = direction[at]
        wave = jnp.where(mine, own_ref[0], other_ref[0])
        sigma = jnp.where(mine, mine_ref[n_sec], theirs_ref[n_sec])
        block = part[s * size : (s + 1) * size] + (coupling_ref[s] / n_ops) * direction[at + mirror].T
        dir_ref[s] = vec
        curvature += total(vec * block)
        coupling += total(vec * (sigma / scale - rayleigh * (wave / scale)))
        for o in range(n_ops):
            at_row = ((o // 2) * 2 + s) * rows
            out_ref[o % 2, at_row : at_row + rows] = block[o * rows : (o + 1) * rows]
    lane = lax.broadcasted_iota(jnp.int32, (PAD, size), 1)
    sums = jnp.where(lane < size // 2, curvature, coupling / n_ops)
    for c in range(2):
        out_ref[c, size:] = sums


def ritz_kernel(n_sec, scalar_ref, sums_ref, wave_ref, dir_ref, sigma_ref, dir_sigma_ref, wave_out, sigma_out, energy_out):
    half = scalar_ref.shape[1] // 2
    scale = scalar_ref[:1, :1]
    rayleigh = scalar_ref[:1, half : half + 1]
    sums = jnp.sum(sums_ref[...], axis=0)
    curvature = sums[:1, :1]
    coupling = sums[:1, half : half + 1]
    half_gap = 0.5 * (curvature - rayleigh)
    radius = jnp.sqrt(half_gap * half_gap + coupling * coupling)
    energy = 0.5 * (rayleigh + curvature) - radius
    safe = jnp.where(radius > 0.0, radius, 1.0)
    big = jnp.sqrt(0.5 + 0.5 * (jnp.abs(half_gap) / safe))
    small = (0.5 * (jnp.abs(coupling) / safe)) / big
    ahead = half_gap >= 0.0
    cos_part = jnp.where(radius > 0.0, jnp.where(ahead, big, small), 1.0)
    sin_size = jnp.where(radius > 0.0, jnp.where(ahead, small, big), 0.0)
    sin_part = jnp.where(coupling < 0.0, sin_size, -sin_size)
    lift = sin_part * scale
    wave_out[...] = cos_part * wave_ref[...] + lift * dir_ref[...]
    sigma_out[...] = cos_part * sigma_ref[...] + lift * dir_sigma_ref[...]
    energy_out[...] = jnp.broadcast_to(energy, energy_out.shape)


def body(n_ops, n_sec, wavefunction, hamiltonian_diag, mirror_coupling, left_env, right_env, term_source):
    owned, size, _ = wavefunction.shape
    terms = left_env.shape[0]
    chips = n_ops // 2
    rows = size // n_ops
    me_ops, me_sec = lax.axis_index("ops"), lax.axis_index("sec")
    core, chip = me_ops % 2, me_ops // 2

    def swap(values):
        return lax.ppermute(values, "ops", [(i, i ^ 1) for i in range(n_ops)])

    def to_chip(values, m):
        return lax.ppermute(values, "ops", [(i, i ^ (2 * m)) for i in range(n_ops)])

    def to_plane(values, m):
        return lax.ppermute(values, "sec", [(i, i ^ m) for i in range(n_sec)])

    def gather_planes(values):
        return jnp.stack([values] + [to_plane(values, m) for m in range(1, n_sec)])

    def pick(values, index):
        return lax.dynamic_index_in_dim(values, index, 0, keepdims=False)

    at = jnp.stack([core, me_sec]).astype(jnp.int32)
    matmul_flops = terms * owned * size * size * size * 12
    scratch = [
        pltpu.VMEM((2 * n_sec + 1, 2 * size, 2 * size), BF16),
        pltpu.VMEM((owned * size, 2 * terms * size), BF16),
        pltpu.VMEM((2 * terms * size, 2 * size), BF16),
    ]

    with jax.named_scope("gather_wave"):
        own = gather_planes(pick(wavefunction, core))
        other = jnp.concatenate([pick(wavefunction, 1 - core)[None], swap(own[1:])])
    with jax.named_scope("gather_diag"):
        diag = gather_planes(pick(hamiltonian_diag, core))

    with jax.named_scope("first_apply"):
        part = call(
            functools.partial(first_kernel, n_sec, n_ops),
            jax.ShapeDtypeStruct((owned, size + PAD, size), F32),
            [SMEM, SMEM, SMEM, VMEM, VMEM, VMEM, VMEM],
            scratch,
            matmul_flops,
        )(term_source, at, mirror_coupling, left_env, right_env, own, other)
    with jax.named_scope("reduce_sigma"):
        summed = pick(part, core) + swap(pick(part, 1 - core))
        summed = sum([to_chip(summed, m) for m in range(1, chips)], summed)
    with jax.named_scope("gather_sigma"):
        sums = gather_planes(summed)
    with jax.named_scope("correction"):
        mine, scalars = call(
            functools.partial(correction_kernel, n_sec),
            (jax.ShapeDtypeStruct((n_sec + 1, size, size), F32), jax.ShapeDtypeStruct((PAD, size), F32)),
            [VMEM] * 4,
        )(sums, own, other, diag)
        theirs = swap(mine)
    with jax.named_scope("second_apply"):
        part, direction = call(
            functools.partial(second_kernel, n_sec, n_ops),
            (
                jax.ShapeDtypeStruct((2, size + PAD, size), F32),
                jax.ShapeDtypeStruct((owned, size, size), F32),
            ),
            [SMEM, SMEM, SMEM] + [VMEM] * 7,
            scratch + [pltpu.VMEM((2 * n_sec, size, size), F32)],
            matmul_flops,
        )(term_source, at, mirror_coupling, left_env, right_env, own, other, mine, theirs, scalars)
    with jax.named_scope("reduce_dir_sigma"):
        summed = pick(part, core) + swap(pick(part, 1 - core))
        tail = summed[size:]

        def message(q):
            return jnp.concatenate([lax.dynamic_slice_in_dim(summed, q * (2 * rows), 2 * rows, 0), tail])

        got = sum([to_chip(message(chip ^ m), m) for m in range(1, chips)], message(chip))
        dir_sigma = got[: 2 * rows].reshape(owned, rows, size)
        scalar_sums = gather_planes(got[2 * rows :])
    with jax.named_scope("ritz"):
        sigma = jnp.stack([jnp.where(core == 0, mine[n_sec], theirs[n_sec]), jnp.where(core == 0, theirs[n_sec], mine[n_sec])])

        def own_rows(values):
            return lax.dynamic_slice_in_dim(values, me_ops * rows, rows, 1)

        new_wave, new_sigma, energy = call(
            functools.partial(ritz_kernel, n_sec),
            (
                jax.ShapeDtypeStruct((owned, rows, size), F32),
                jax.ShapeDtypeStruct((owned, rows, size), F32),
                jax.ShapeDtypeStruct((1, size), F32),
            ),
            [VMEM] * 6,
        )(scalars, scalar_sums, own_rows(wavefunction), own_rows(direction), own_rows(sigma), dir_sigma)
    return (new_wave, new_sigma, energy[0, :1])


def solution(mesh):
    placed = (
        P("sec", None, None),
        P("sec", None, None),
        P("sec"),
        P("ops", "sec", None, None),
        P("ops", None, None),
        P("ops", "sec"),
    )
    return jax.shard_map(
        functools.partial(body, mesh.shape["ops"], mesh.shape["sec"]),
        mesh=mesh,
        in_specs=placed,
        out_specs=(P("sec", "ops", None), P("sec", "ops", None), P()),
        check_vma=False,
    )
```

time: 259 us -> 67.3 us (0.26)
  waiting for transfers between devices: 98.7 us -> 18.9 us
  blocking collectives: 79.4 us -> 0 us
  matrix products: 29.2 us -> 0 us
  starting transfers between devices: 0.08 us -> 26.7 us
  between operations: 21.5 us -> 0.83 us
  other arithmetic: 11.3 us -> 1.12 us
  Pallas kernels: 0 us -> 9.19 us
  local copies, waits for them, and re-layouts: 18.5 us -> 10.1 us
    psum x2 -> x0, waiting for transfers between devices: 98.7 us -> none  [summed_whole(): return lax.psum(partial_sigma, 'ops')]
    psum x4 -> x0, blocking collectives: 44.5 us -> none  [sector_sums(): return lax.psum(values, 'sec')]
    all_gather x2 -> x0, blocking collectives: 34.9 us -> none  [full_blocks(): return lax.all_gather(vector, 'sec', axis=0, tiled=True)]
    dot_general x4 -> x0, matrix products: 29.2 us -> none  [the longest x2 17.7 us: contract_terms(): inner = jnp.einsum('ksij,ksjl->ksil', left_env, picked, precision=HIGH)]
    ppermute x0 -> x22, starting transfers between devices: none -> 26.7 us  [the longest x12 19.2 us: to_plane(): return lax.ppermute(values, 'sec', [(i, i ^ m) for i in range(n_sec)])]
    ppermute x0 -> x22, waiting for transfers between devices: none -> 18.9 us  [the longest x12 10.6 us: to_plane(): return lax.ppermute(values, 'sec', [(i, i ^ m) for i in range(n_sec)])]
    gather x4 -> x0, local copies, waits for them, and re-layouts: 14.1 us -> none  [contract_terms(): picked = whole[jnp.maximum(term_source, 0)]]
    pallas_call x0 -> x4, Pallas kernels: none -> 9.19 us  [the longest x1 3.98 us: body(): call(functools.partial(second_kernel, n_sec, n_ops), (jax.ShapeDtypeStruc...]
  transfers between devices with their start and end apart: 2 -> 22, of which waited for: 2 -> 14; matrix products, arithmetic and copies ran while one was open for 2% -> 4% of each run, Pallas kernels for 0% -> 0%
where the time goes in v1:
time: 67.3 us; the launch traced here: 66.9 us
  starting transfers between devices  26.7 us (40%)
  waiting for transfers between devices  18.9 us (28%)
  local copies, waits for them, and re-layouts  10.1 us (15%)
  Pallas kernels  9.19 us (14%)
  other arithmetic  1.12 us (2%)
  between operations  0.83 us (1%)
    ppermute x12, starting transfers between devices, to_plane(): return lax.ppermute(values, 'sec', [(i, i ^ m) for i in range(n_sec)])  19.2 us
    ppermute x12, waiting for transfers between devices, to_plane(): return lax.ppermute(values, 'sec', [(i, i ^ m) for i in range(n_sec)])  10.6 us
    unnamed x23, local copies, waits for them, and re-layouts  8.39 us
    ppermute x6, starting transfers between devices, to_chip(): return lax.ppermute(values, 'ops', [(i, i ^ 2 * m) for i in range(n_ops)])  7.11 us
    ppermute x6, waiting for transfers between devices, to_chip(): return lax.ppermute(values, 'ops', [(i, i ^ 2 * m) for i in range(n_ops)])  5.53 us
    pallas_call x1, Pallas kernels, body(): call(functools.partial(second_kernel, n_sec, n_ops), (jax.ShapeDtypeStruc...  3.98 us
    pallas_call x1, Pallas kernels, body(): call(functools.partial(first_kernel, n_sec, n_ops), jax.ShapeDtypeStruct(...  3.14 us
    ppermute x4, waiting for transfers between devices, swap(): return lax.ppermute(values, 'ops', [(i, i ^ 1) for i in range(n_ops)])  2.82 us
  transfers between devices with their start and end apart: 22, of which 14 were waited for; matrix products, arithmetic and copies ran while one was open for 4% of the time, Pallas kernels for 0%

profile of v1, /device:TPU:0, one launch (start us, length us, event | category | flops | bytes accessed | tf_op | source)
XLA Modules:
  0.0 66.9 jit_solution(15018461916206892960)
XLA Ops:
  0.7 0.9 %constant_dynamic-slice_fusion.7 = (f32[1,128,128]{2,1,0:T(8,128)S(1)}, f32[1,128,128]{2,1,0:T(8,128)S(1)}) fusion(f32[2,128,128]{2,1,0:T(8,128)} %param.6, s32[]{:T(128)S(6)} %select_n.57, s32[]{:T(128)S(6)} %select_n.56), kind=kLoop, calls=%fused_computation.30 | loop fusion | bytes 262152 | tf_op jit(solution)/shard_map/gather_wave/jit(dynamic_index_in_dim)/dynamic_slice | solution.py:208
  1.6 5.1 %collective-permute-start.2 = (f32[128,128]{1,0:T(8,128)S(1)}, f32[128,128]{1,0:T(8,128)S(1)}, u32[]{:S(2)}, u32[]{:S(2)}) collective-permute-start(f32[128,128]{1,0:T(8,128)S(1)} %bitcast.33), channel_id=1, source_target_pairs={{0,3},{1,2},{2,1},{3,0},{4,7},{5,6},{6,5},{7,4},{8,11},{9,10},{10,... | collective-permute-start | bytes 196616 | tf_op jit(solution)/shard_map/gather_wave/ppermute | solution.py:202
  8.1 1.2 %collective-permute-done.2 = f32[128,128]{1,0:T(8,128)S(1)} collective-permute-done((f32[128,128]{1,0:T(8,128)S(1)}, f32[128,128]{1,0:T(8,128)S(1)}, u32[]{:S(2)}, u32[]{:S(2)}) %collective-permute-start.2) | collective-permute-done | bytes 65568 | tf_op jit(solution)/shard_map/gather_wave/ppermute | solution.py:202
  9.3 3.0 %collective-permute-done.1 = f32[128,128]{1,0:T(8,128)S(1)} collective-permute-done((f32[128,128]{1,0:T(8,128)S(1)}, f32[128,128]{1,0:T(8,128)S(1)}, u32[]{:S(2)}, u32[]{:S(2)}) %collective-permute-start.1) | collective-permute-done | bytes 65568 | tf_op jit(solution)/shard_map/gather_wave/ppermute | solution.py:202
  12.5 1.3 %collective-permute-done.3 = f32[3,128,128]{2,1,0:T(8,128)S(1)} collective-permute-done((f32[3,128,128]{2,1,0:T(8,128)S(1)}, f32[3,128,128]{2,1,0:T(8,128)S(1)}, u32[]{:S(2)}, u32[]{:S(2)}) %collective-permute-start.3) | collective-permute-done | bytes 196640 | tf_op jit(solution)/shard_map/gather_wave/ppermute | solution.py:196
  13.9 1.9 %copy-done.1 = f32[24,2,128,128]{3,2,1,0:T(8,128)S(1)} copy-done((f32[24,2,128,128]{3,2,1,0:T(8,128)S(1)}, f32[24,2,128,128]{3,2,1,0:T(8,128)}, u32[]{:S(2)}) %copy-start.1) | copy-done | bytes 3145752
  15.8 1.4 %copy-done.3 = f32[24,128,128]{2,1,0:T(8,128)S(1)} copy-done((f32[24,128,128]{2,1,0:T(8,128)S(1)}, f32[24,128,128]{2,1,0:T(8,128)}, u32[]{:S(2)}) %copy-start.3) | copy-done | bytes 1572888
  17.8 3.1 %first_apply.1 = f32[2,136,128]{2,1,0:T(8,128)S(1)} custom-call(s32[24,2]{1,0:T(8,128)S(1)} %copy.9.source_ref, s32[2]{0:T(128)S(1)} %pad_add_fusion.at_ref, f32[2]{0:T(128)S(1)} %copy-done.7, f32[24,2,128,128]{3,2,1,0:T(8,128)S(1)} %copy-done.1, f32[24,128,128]{2,1,0:T(8,128)S(1)} %copy-done.3, f32[4,128,128]{2,1,0:T(8,128)S(1)} %pad_maximum_fusion.1.own_ref, ...), custom_call_target="tpu_custom_call" | custom-call | flops 1207959552 | bytes 1048576 | tf_op jit(solution)/shard_map/first_apply/pallas_call | solution.py:225
  21.2 2.8 %collective-permute-start.13 = (f32[128,128]{1,0:T(8,128)S(1)}, f32[128,128]{1,0:T(8,128)S(1)}, u32[]{:S(2)}, u32[]{:S(2)}) collective-permute-start(f32[128,128]{1,0:T(8,128)S(1)} %fusion.4), channel_id=1, source_target_pairs={{0,3},{1,2},{2,1},{3,0},{4,7},{5,6},{6,5},{7,4},{8,11},{9,10},{10,... | collective-permute-start | bytes 196616 | tf_op jit(solution)/shard_map/gather_diag/ppermute | solution.py:202
  24.0 2.5 %collective-permute-start.7 = (f32[136,128]{1,0:T(8,128)S(1)}, f32[136,128]{1,0:T(8,128)S(1)}, u32[]{:S(2)}, u32[]{:S(2)}) collective-permute-start(f32[136,128]{1,0:T(8,128)S(1)} %bitcast_add_fusion.1), channel_id=1, source_target_pairs={{0,24},{4,28},{8,16},{12,20},{16,8},{20,12},{24,0},{28,4},{1,25},{... | collective-permute-start | bytes 208904 | tf_op jit(solution)/shard_map/reduce_sigma/ppermute | solution.py:199
  27.6 1.8 %collective-permute-done.7 = f32[136,128]{1,0:T(8,128)S(1)} collective-permute-done((f32[136,128]{1,0:T(8,128)S(1)}, f32[136,128]{1,0:T(8,128)S(1)}, u32[]{:S(2)}, u32[]{:S(2)}) %collective-permute-start.7) | collective-permute-done | bytes 69664 | tf_op jit(solution)/shard_map/reduce_sigma/ppermute | solution.py:199
  29.4 1.7 %collective-permute-start.11 = (f32[128,128]{1,0:T(8,128)S(1)}, f32[128,128]{1,0:T(8,128)S(1)}, u32[]{:S(2)}, u32[]{:S(2)}) collective-permute-start(f32[128,128]{1,0:T(8,128)S(1)} %fusion.4), channel_id=1, source_target_pairs={{0,1},{1,0},{2,3},{3,2},{4,5},{5,4},{6,7},{7,6},{8,9},{9,8},{10,11... | collective-permute-start | bytes 196616 | tf_op jit(solution)/shard_map/gather_diag/ppermute | solution.py:202
  31.4 2.5 %collective-permute-start.10 = (f32[136,128]{1,0:T(8,128)S(1)}, f32[136,128]{1,0:T(8,128)S(1)}, u32[]{:S(2)}, u32[]{:S(2)}) collective-permute-start(f32[136,128]{1,0:T(8,128)S(1)} %add_add_fusion), channel_id=1, source_target_pairs={{0,3},{1,2},{2,1},{3,0},{4,7},{5,6},{6,5},{7,4},{8,11},{9,10},{10,... | collective-permute-start | bytes 208904 | tf_op jit(solution)/shard_map/gather_sigma/ppermute | solution.py:202
  34.6 1.3 %collective-permute-start.8 = (f32[136,128]{1,0:T(8,128)S(1)}, f32[136,128]{1,0:T(8,128)S(1)}, u32[]{:S(2)}, u32[]{:S(2)}) collective-permute-start(f32[136,128]{1,0:T(8,128)S(1)} %add_add_fusion), channel_id=1, source_target_pairs={{0,1},{1,0},{2,3},{3,2},{4,5},{5,4},{6,7},{7,6},{8,9},{9,8},{10,11... | collective-permute-start | bytes 208904 | tf_op jit(solution)/shard_map/gather_sigma/ppermute | solution.py:202
  35.9 2.4 %collective-permute-done.10 = f32[136,128]{1,0:T(8,128)S(1)} collective-permute-done((f32[136,128]{1,0:T(8,128)S(1)}, f32[136,128]{1,0:T(8,128)S(1)}, u32[]{:S(2)}, u32[]{:S(2)}) %collective-permute-start.10) | collective-permute-done | bytes 69664 | tf_op jit(solution)/shard_map/gather_sigma/ppermute | solution.py:202
  38.3 1.8 %collective-permute-done.9 = f32[136,128]{1,0:T(8,128)S(1)} collective-permute-done((f32[136,128]{1,0:T(8,128)S(1)}, f32[136,128]{1,0:T(8,128)S(1)}, u32[]{:S(2)}, u32[]{:S(2)}) %collective-permute-start.9) | collective-permute-done | bytes 69664 | tf_op jit(solution)/shard_map/gather_sigma/ppermute | solution.py:202
  40.1 1.0 %correction.1 = (f32[5,128,128]{2,1,0:T(8,128)}, f32[8,128]{1,0:T(8,128)S(1)}) custom-call(f32[4,136,128]{2,1,0:T(8,128)S(1)} %pad_maximum_fusion.sums_ref, f32[4,128,128]{2,1,0:T(8,128)S(1)} %pad_maximum_fusion.1.own_ref, f32[4,128,128]{2,1,0:T(8,128)S(1)} %pad_maximum_fusion.2.other_ref, f32[4,128,128]{2,1,0:T(8,128)S(1)} %pad_maximum_fusion.3.diag_ref), custom_call_target="tpu_custom_call" | custom-call | bytes 1048576 | tf_op jit(solution)/shard_map/correction/pallas_call | solution.py:238
  41.9 1.2 %collective-permute-done.14.theirs_ref = f32[5,128,128]{2,1,0:T(8,128)} collective-permute-done((f32[5,128,128]{2,1,0:T(8,128)}, f32[5,128,128]{2,1,0:T(8,128)}, u32[]{:S(2)}, u32[]{:S(2)}) %collective-permute-start.14) | collective-permute-done | bytes 327712 | tf_op jit(solution)/shard_map/correction/ppermute | solution.py:196
  43.1 1.4 %copy-done.4 = f32[24,128,128]{2,1,0:T(8,128)S(1)} copy-done((f32[24,128,128]{2,1,0:T(8,128)S(1)}, f32[24,128,128]{2,1,0:T(8,128)}, u32[]{:S(2)}) %copy-start.4) | copy-done | bytes 1572888
  44.5 0.9 %copy-done.6 = f32[4,128,128]{2,1,0:T(8,128)S(1)} copy-done((f32[4,128,128]{2,1,0:T(8,128)S(1)}, f32[4,128,128]{2,1,0:T(8,128)}, u32[]{:S(2)}) %copy-start.6) | copy-done | bytes 262168
  46.8 4.0 %second_apply.1 = (f32[2,136,128]{2,1,0:T(8,128)S(1)}, f32[2,128,128]{2,1,0:T(8,128)S(1)}) custom-call(s32[24,2]{1,0:T(8,128)S(1)} %copy.9.source_ref, s32[2]{0:T(128)S(1)} %copy-done.10, f32[2]{0:T(128)S(1)} %copy-done.8, f32[24,2,128,128]{3,2,1,0:T(8,128)S(1)} %copy-done.2, f32[24,128,128]{2,1,0:T(8,128)S(1)} %copy-done.4, ...), custom_call_target="tpu_custom_call" | custom-call | flops 1207959552 | bytes 1048576 | tf_op jit(solution)/shard_map/second_apply/pallas_call | solution.py:245
  51.0 0.9 %slice_select_fusion = (f32[1,128,128]{2,1,0:T(8,128)S(1)}, f32[1,128,128]{2,1,0:T(8,128)S(1)}) fusion(f32[5,128,128]{2,1,0:T(8,128)} %collective-permute-done.14.theirs_ref, f32[5,128,128]{2,1,0:T(8,128)} %get-tuple-element.11.mine_ref, pred[]{:T(512)S(6)} %eq.6), kind=kLoop, calls=%fused_computation.12 | loop fusion | flops 32768 | bytes 262145 | tf_op jit(solution)/shard_map/ritz/jit(_where)/select_n | solution.py:266
  52.2 2.3 %collective-permute-start.18 = (f32[40,128]{1,0:T(8,128)S(1)}, f32[40,128]{1,0:T(8,128)S(1)}, u32[]{:S(2)}, u32[]{:S(2)}) collective-permute-start(f32[40,128]{1,0:T(8,128)S(1)} %get-tuple-element.29), channel_id=1, source_target_pairs={{0,24},{4,28},{8,16},{12,20},{16,8},{20,12},{24,0},{28,4},{1,25},{... | collective-permute-start | bytes 61448 | tf_op jit(solution)/shard_map/reduce_dir_sigma/ppermute | solution.py:199
  54.5 0.9 %collective-permute-start.17 = (f32[40,128]{1,0:T(8,128)S(1)}, f32[40,128]{1,0:T(8,128)S(1)}, u32[]{:S(2)}, u32[]{:S(2)}) collective-permute-start(f32[40,128]{1,0:T(8,128)S(1)} %get-tuple-element.28), channel_id=1, source_target_pairs={{0,16},{4,20},{8,24},{12,28},{16,0},{20,4},{24,8},{28,12},{1,17},{... | collective-permute-start | bytes 61448 | tf_op jit(solution)/shard_map/reduce_dir_sigma/ppermute | solution.py:199
  55.7 1.2 %collective-permute-done.18 = f32[40,128]{1,0:T(8,128)S(1)} collective-permute-done((f32[40,128]{1,0:T(8,128)S(1)}, f32[40,128]{1,0:T(8,128)S(1)}, u32[]{:S(2)}, u32[]{:S(2)}) %collective-permute-start.18) | collective-permute-done | bytes 20512 | tf_op jit(solution)/shard_map/reduce_dir_sigma/ppermute | solution.py:199
  56.9 1.4 %collective-permute-done.17 = f32[40,128]{1,0:T(8,128)S(1)} collective-permute-done((f32[40,128]{1,0:T(8,128)S(1)}, f32[40,128]{1,0:T(8,128)S(1)}, u32[]{:S(2)}, u32[]{:S(2)}) %collective-permute-start.17) | collective-permute-done | bytes 20512 | tf_op jit(solution)/shard_map/reduce_dir_sigma/ppermute | solution.py:199
  58.3 0.9 %collective-permute-done.16 = f32[40,128]{1,0:T(8,128)S(1)} collective-permute-done((f32[40,128]{1,0:T(8,128)S(1)}, f32[40,128]{1,0:T(8,128)S(1)}, u32[]{:S(2)}, u32[]{:S(2)}) %collective-permute-start.16) | collective-permute-done | bytes 20512 | tf_op jit(solution)/shard_map/reduce_dir_sigma/ppermute | solution.py:199
  59.2 2.1 %collective-permute-start.21 = (f32[8,128]{1,0:T(8,128)S(1)}, f32[8,128]{1,0:T(8,128)S(1)}, u32[]{:S(2)}, u32[]{:S(2)}) collective-permute-start(f32[8,128]{1,0:T(8,128)S(1)} %get-tuple-element.26), channel_id=1, source_target_pairs={{0,3},{1,2},{2,1},{3,0},{4,7},{5,6},{6,5},{7,4},{8,11},{9,10},{10,... | collective-permute-start | bytes 12296 | tf_op jit(solution)/shard_map/reduce_dir_sigma/ppermute | solution.py:202
  61.4 2.3 %collective-permute-start.19 = (f32[8,128]{1,0:T(8,128)S(1)}, f32[8,128]{1,0:T(8,128)S(1)}, u32[]{:S(2)}, u32[]{:S(2)}) collective-permute-start(f32[8,128]{1,0:T(8,128)S(1)} %get-tuple-element.26), channel_id=1, source_target_pairs={{0,1},{1,0},{2,3},{3,2},{4,5},{5,4},{6,7},{7,6},{8,9},{9,8},{10,11... | collective-permute-start | bytes 12296 | tf_op jit(solution)/shard_map/reduce_dir_sigma/ppermute | solution.py:202
  63.7 1.0 %collective-permute-done.21 = f32[8,128]{1,0:T(8,128)S(1)} collective-permute-done((f32[8,128]{1,0:T(8,128)S(1)}, f32[8,128]{1,0:T(8,128)S(1)}, u32[]{:S(2)}, u32[]{:S(2)}) %collective-permute-start.21) | collective-permute-done | bytes 4128 | tf_op jit(solution)/shard_map/reduce_dir_sigma/ppermute | solution.py:202
  64.7 1.2 %collective-permute-done.20 = f32[8,128]{1,0:T(8,128)S(1)} collective-permute-done((f32[8,128]{1,0:T(8,128)S(1)}, f32[8,128]{1,0:T(8,128)S(1)}, u32[]{:S(2)}, u32[]{:S(2)}) %collective-permute-start.20) | collective-permute-done | bytes 4128 | tf_op jit(solution)/shard_map/reduce_dir_sigma/ppermute | solution.py:202
  65.9 1.0 %ritz.1 = (f32[2,16,128]{2,1,0:T(8,128)}, f32[2,16,128]{2,1,0:T(8,128)}, f32[1,128]{1,0:T(1,128)}) custom-call(f32[8,128]{1,0:T(8,128)S(1)} %get-tuple-element.10.scalar_ref, f32[4,8,128]{2,1,0:T(8,128)S(1)} %pad_maximum_fusion.9.sums_ref, f32[2,16,128]{2,1,0:T(8,128)S(1)} %constant_dynamic-slice_fusion.1.wave_ref, ...), custom_call_target="tpu_custom_call" | custom-call | bytes 1048576 | tf_op jit(solution)/shard_map/ritz/pallas_call | solution.py:271
  (64 shorter events, 7.6 us)
Async XLA Ops:
  0.6 20.6 %copy-start = (f32[2,128,128]{2,1,0:T(8,128)S(1)}, f32[2,128,128]{2,1,0:T(8,128)}, u32[]{:S(2)}) copy-start(f32[2,128,128]{2,1,0:T(8,128)} %param.7) | copy-start | bytes 393220
  1.6 7.7 %collective-permute-start.2 = (f32[128,128]{1,0:T(8,128)S(1)}, f32[128,128]{1,0:T(8,128)S(1)}, u32[]{:S(2)}, u32[]{:S(2)}) collective-permute-start(f32[128,128]{1,0:T(8,128)S(1)} %bitcast.33), channel_id=1, source_target_pairs={{0,3},{1,2},{2,1},{3,0},{4,7},{5,6},{6,5},{7,4},{8,11},{9,10},{10,... | collective-permute-start | bytes 196616 | tf_op jit(solution)/shard_map/gather_wave/ppermute | solution.py:202
  6.7 5.6 %collective-permute-start.1 = (f32[128,128]{1,0:T(8,128)S(1)}, f32[128,128]{1,0:T(8,128)S(1)}, u32[]{:S(2)}, u32[]{:S(2)}) collective-permute-start(f32[128,128]{1,0:T(8,128)S(1)} %bitcast.34), channel_id=1, source_target_pairs={{0,2},{1,3},{2,0},{3,1},{4,6},{5,7},{6,4},{7,5},{8,10},{9,11},{10,... | collective-permute-start | bytes 196616 | tf_op jit(solution)/shard_map/gather_wave/ppermute | solution.py:202
  6.7 5.6 %collective-permute-start = (f32[128,128]{1,0:T(8,128)S(1)}, f32[128,128]{1,0:T(8,128)S(1)}, u32[]{:S(2)}, u32[]{:S(2)}) collective-permute-start(f32[128,128]{1,0:T(8,128)S(1)} %bitcast.35), channel_id=1, source_target_pairs={{0,1},{1,0},{2,3},{3,2},{4,5},{5,4},{6,7},{7,6},{8,9},{9,8},{10,11... | collective-permute-start | bytes 196616 | tf_op jit(solution)/shard_map/gather_wave/ppermute | solution.py:202
  12.3 1.5 %collective-permute-start.3 = (f32[3,128,128]{2,1,0:T(8,128)S(1)}, f32[3,128,128]{2,1,0:T(8,128)S(1)}, u32[]{:S(2)}, u32[]{:S(2)}) collective-permute-start(f32[3,128,128]{2,1,0:T(8,128)S(1)} %pad_maximum_fusion.4), channel_id=1, source_target_pairs={{0,4},{4,0},{8,12},{12,8},{16,20},{20,16},{24,28},{28,24},{1,5},{5... | collective-permute-start | bytes 589832 | tf_op jit(solution)/shard_map/gather_wave/ppermute | solution.py:196
  12.5 8.5 %copy-start.9 = (s32[2]{0:T(128)}, s32[2]{0:T(128)S(1)}, u32[]{:S(2)}) copy-start(s32[2]{0:T(128)S(1)} %pad_add_fusion.at_ref) | copy-start | bytes 28
  13.9 1.9 %copy-start.1 = (f32[24,2,128,128]{3,2,1,0:T(8,128)S(1)}, f32[24,2,128,128]{3,2,1,0:T(8,128)}, u32[]{:S(2)}) copy-start(f32[24,2,128,128]{3,2,1,0:T(8,128)} %left_ref.3) | copy-start | bytes 9437188
  15.8 1.4 %copy-start.3 = (f32[24,128,128]{2,1,0:T(8,128)S(1)}, f32[24,128,128]{2,1,0:T(8,128)}, u32[]{:S(2)}) copy-start(f32[24,128,128]{2,1,0:T(8,128)} %right_ref.3) | copy-start | bytes 4718596
  17.2 0.7 copy-start.7
  17.8 22.3 %copy-start.5 = (f32[4,128,128]{2,1,0:T(8,128)}, f32[4,128,128]{2,1,0:T(8,128)S(1)}, u32[]{:S(2)}) copy-start(f32[4,128,128]{2,1,0:T(8,128)S(1)} %pad_maximum_fusion.2.other_ref) | copy-start | bytes 786436
  17.8 25.3 %copy-start.2 = (f32[24,2,128,128]{3,2,1,0:T(8,128)S(1)}, f32[24,2,128,128]{3,2,1,0:T(8,128)}, u32[]{:S(2)}) copy-start(f32[24,2,128,128]{3,2,1,0:T(8,128)} %left_ref.3) | copy-start | bytes 9437188
  21.0 3.0 %collective-permute-start.4 = (f32[136,128]{1,0:T(8,128)S(1)}, f32[136,128]{1,0:T(8,128)S(1)}, u32[]{:S(2)}, u32[]{:S(2)}) collective-permute-start(f32[136,128]{1,0:T(8,128)S(1)} %dynamic-slice_bitcast_fusion.1), channel_id=1, source_target_pairs={{0,4},{4,0},{8,12},{12,8},{16,20},{20,16},{24,28},{28,24},{1,5},{5... | collective-permute-start | bytes 208904 | tf_op jit(solution)/shard_map/reduce_sigma/ppermute | solution.py:196
  21.2 13.4 %collective-permute-start.13 = (f32[128,128]{1,0:T(8,128)S(1)}, f32[128,128]{1,0:T(8,128)S(1)}, u32[]{:S(2)}, u32[]{:S(2)}) collective-permute-start(f32[128,128]{1,0:T(8,128)S(1)} %fusion.4), channel_id=1, source_target_pairs={{0,3},{1,2},{2,1},{3,0},{4,7},{5,6},{6,5},{7,4},{8,11},{9,10},{10,... | collective-permute-start | bytes 196616 | tf_op jit(solution)/shard_map/gather_diag/ppermute | solution.py:202
  24.0 11.8 %collective-permute-start.12 = (f32[128,128]{1,0:T(8,128)S(1)}, f32[128,128]{1,0:T(8,128)S(1)}, u32[]{:S(2)}, u32[]{:S(2)}) collective-permute-start(f32[128,128]{1,0:T(8,128)S(1)} %fusion.4), channel_id=1, source_target_pairs={{0,2},{1,3},{2,0},{3,1},{4,6},{5,7},{6,4},{7,5},{8,10},{9,11},{10,... | collective-permute-start | bytes 196616 | tf_op jit(solution)/shard_map/gather_diag/ppermute | solution.py:202
  24.0 5.3 %collective-permute-start.7 = (f32[136,128]{1,0:T(8,128)S(1)}, f32[136,128]{1,0:T(8,128)S(1)}, u32[]{:S(2)}, u32[]{:S(2)}) collective-permute-start(f32[136,128]{1,0:T(8,128)S(1)} %bitcast_add_fusion.1), channel_id=1, source_target_pairs={{0,24},{4,28},{8,16},{12,20},{16,8},{20,12},{24,0},{28,4},{1,25},{... | collective-permute-start | bytes 208904 | tf_op jit(solution)/shard_map/reduce_sigma/ppermute | solution.py:199
  26.6 4.5 %collective-permute-start.6 = (f32[136,128]{1,0:T(8,128)S(1)}, f32[136,128]{1,0:T(8,128)S(1)}, u32[]{:S(2)}, u32[]{:S(2)}) collective-permute-start(f32[136,128]{1,0:T(8,128)S(1)} %bitcast_add_fusion.1), channel_id=1, source_target_pairs={{0,16},{4,20},{8,24},{12,28},{16,0},{20,4},{24,8},{28,12},{1,17},{... | collective-permute-start | bytes 208904 | tf_op jit(solution)/shard_map/reduce_sigma/ppermute | solution.py:199
  27.1 4.3 %collective-permute-start.5 = (f32[136,128]{1,0:T(8,128)S(1)}, f32[136,128]{1,0:T(8,128)S(1)}, u32[]{:S(2)}, u32[]{:S(2)}) collective-permute-start(f32[136,128]{1,0:T(8,128)S(1)} %bitcast_add_fusion.1), channel_id=1, source_target_pairs={{0,8},{4,12},{8,0},{12,4},{16,24},{20,28},{24,16},{28,20},{1,9},{5... | collective-permute-start | bytes 208904 | tf_op jit(solution)/shard_map/reduce_sigma/ppermute | solution.py:199
  29.4 6.5 %collective-permute-start.11 = (f32[128,128]{1,0:T(8,128)S(1)}, f32[128,128]{1,0:T(8,128)S(1)}, u32[]{:S(2)}, u32[]{:S(2)}) collective-permute-start(f32[128,128]{1,0:T(8,128)S(1)} %fusion.4), channel_id=1, source_target_pairs={{0,1},{1,0},{2,3},{3,2},{4,5},{5,4},{6,7},{7,6},{8,9},{9,8},{10,11... | collective-permute-start | bytes 196616 | tf_op jit(solution)/shard_map/gather_diag/ppermute | solution.py:202
  31.4 6.9 %collective-permute-start.10 = (f32[136,128]{1,0:T(8,128)S(1)}, f32[136,128]{1,0:T(8,128)S(1)}, u32[]{:S(2)}, u32[]{:S(2)}) collective-permute-start(f32[136,128]{1,0:T(8,128)S(1)} %add_add_fusion), channel_id=1, source_target_pairs={{0,3},{1,2},{2,1},{3,0},{4,7},{5,6},{6,5},{7,4},{8,11},{9,10},{10,... | collective-permute-start | bytes 208904 | tf_op jit(solution)/shard_map/gather_sigma/ppermute | solution.py:202
  33.9 6.2 %collective-permute-start.9 = (f32[136,128]{1,0:T(8,128)S(1)}, f32[136,128]{1,0:T(8,128)S(1)}, u32[]{:S(2)}, u32[]{:S(2)}) collective-permute-start(f32[136,128]{1,0:T(8,128)S(1)} %add_add_fusion), channel_id=1, source_target_pairs={{0,2},{1,3},{2,0},{3,1},{4,6},{5,7},{6,4},{7,5},{8,10},{9,11},{10,... | collective-permute-start | bytes 208904 | tf_op jit(solution)/shard_map/gather_sigma/ppermute | solution.py:202
  34.6 5.5 %collective-permute-start.8 = (f32[136,128]{1,0:T(8,128)S(1)}, f32[136,128]{1,0:T(8,128)S(1)}, u32[]{:S(2)}, u32[]{:S(2)}) collective-permute-start(f32[136,128]{1,0:T(8,128)S(1)} %add_add_fusion), channel_id=1, source_target_pairs={{0,1},{1,0},{2,3},{3,2},{4,5},{5,4},{6,7},{7,6},{8,9},{9,8},{10,11... | collective-permute-start | bytes 208904 | tf_op jit(solution)/shard_map/gather_sigma/ppermute | solution.py:202
  41.1 2.0 %collective-permute-start.14 = (f32[5,128,128]{2,1,0:T(8,128)}, f32[5,128,128]{2,1,0:T(8,128)}, u32[]{:S(2)}, u32[]{:S(2)}) collective-permute-start(f32[5,128,128]{2,1,0:T(8,128)} %get-tuple-element.11.mine_ref), channel_id=1, source_target_pairs={{0,4},{4,0},{8,12},{12,8},{16,20},{20,16},{24,28},{28,24},{1,5},{5... | collective-permute-start | bytes 983048 | tf_op jit(solution)/shard_map/correction/ppermute | solution.py:196
  43.1 1.4 %copy-start.4 = (f32[24,128,128]{2,1,0:T(8,128)S(1)}, f32[24,128,128]{2,1,0:T(8,128)}, u32[]{:S(2)}) copy-start(f32[24,128,128]{2,1,0:T(8,128)} %right_ref.3) | copy-start | bytes 4718596
  44.5 0.9 %copy-start.6 = (f32[4,128,128]{2,1,0:T(8,128)S(1)}, f32[4,128,128]{2,1,0:T(8,128)}, u32[]{:S(2)}) copy-start(f32[4,128,128]{2,1,0:T(8,128)} %copy-done.5) | copy-start | bytes 786436
  46.1 0.7 copy-start.10
  50.8 1.3 %collective-permute-start.15 = (f32[136,128]{1,0:T(8,128)S(1)}, f32[136,128]{1,0:T(8,128)S(1)}, u32[]{:S(2)}, u32[]{:S(2)}) collective-permute-start(f32[136,128]{1,0:T(8,128)S(1)} %dynamic-slice_bitcast_fusion), channel_id=1, source_target_pairs={{0,4},{4,0},{8,12},{12,8},{16,20},{20,16},{24,28},{28,24},{1,5},{5... | collective-permute-start | bytes 208904 | tf_op jit(solution)/shard_map/reduce_dir_sigma/ppermute | solution.py:196
  52.2 4.7 %collective-permute-start.18 = (f32[40,128]{1,0:T(8,128)S(1)}, f32[40,128]{1,0:T(8,128)S(1)}, u32[]{:S(2)}, u32[]{:S(2)}) collective-permute-start(f32[40,128]{1,0:T(8,128)S(1)} %get-tuple-element.29), channel_id=1, source_target_pairs={{0,24},{4,28},{8,16},{12,20},{16,8},{20,12},{24,0},{28,4},{1,25},{... | collective-permute-start | bytes 61448 | tf_op jit(solution)/shard_map/reduce_dir_sigma/ppermute | solution.py:199
  54.5 3.8 %collective-permute-start.17 = (f32[40,128]{1,0:T(8,128)S(1)}, f32[40,128]{1,0:T(8,128)S(1)}, u32[]{:S(2)}, u32[]{:S(2)}) collective-permute-start(f32[40,128]{1,0:T(8,128)S(1)} %get-tuple-element.28), channel_id=1, source_target_pairs={{0,16},{4,20},{8,24},{12,28},{16,0},{20,4},{24,8},{28,12},{1,17},{... | collective-permute-start | bytes 61448 | tf_op jit(solution)/shard_map/reduce_dir_sigma/ppermute | solution.py:199
  55.4 3.8 %collective-permute-start.16 = (f32[40,128]{1,0:T(8,128)S(1)}, f32[40,128]{1,0:T(8,128)S(1)}, u32[]{:S(2)}, u32[]{:S(2)}) collective-permute-start(f32[40,128]{1,0:T(8,128)S(1)} %get-tuple-element.27), channel_id=1, source_target_pairs={{0,8},{4,12},{8,0},{12,4},{16,24},{20,28},{24,16},{28,20},{1,9},{5... | collective-permute-start | bytes 61448 | tf_op jit(solution)/shard_map/reduce_dir_sigma/ppermute | solution.py:199
  59.2 5.5 %collective-permute-start.21 = (f32[8,128]{1,0:T(8,128)S(1)}, f32[8,128]{1,0:T(8,128)S(1)}, u32[]{:S(2)}, u32[]{:S(2)}) collective-permute-start(f32[8,128]{1,0:T(8,128)S(1)} %get-tuple-element.26), channel_id=1, source_target_pairs={{0,3},{1,2},{2,1},{3,0},{4,7},{5,6},{6,5},{7,4},{8,11},{9,10},{10,... | collective-permute-start | bytes 12296 | tf_op jit(solution)/shard_map/reduce_dir_sigma/ppermute | solution.py:202
  61.4 4.5 %collective-permute-start.20 = (f32[8,128]{1,0:T(8,128)S(1)}, f32[8,128]{1,0:T(8,128)S(1)}, u32[]{:S(2)}, u32[]{:S(2)}) collective-permute-start(f32[8,128]{1,0:T(8,128)S(1)} %get-tuple-element.26), channel_id=1, source_target_pairs={{0,2},{1,3},{2,0},{3,1},{4,6},{5,7},{6,4},{7,5},{8,10},{9,11},{10,... | collective-permute-start | bytes 12296 | tf_op jit(solution)/shard_map/reduce_dir_sigma/ppermute | solution.py:202
  61.4 4.5 %collective-permute-start.19 = (f32[8,128]{1,0:T(8,128)S(1)}, f32[8,128]{1,0:T(8,128)S(1)}, u32[]{:S(2)}, u32[]{:S(2)}) collective-permute-start(f32[8,128]{1,0:T(8,128)S(1)} %get-tuple-element.26), channel_id=1, source_target_pairs={{0,1},{1,0},{2,3},{3,2},{4,5},{5,4},{6,7},{7,6},{8,9},{9,8},{10,11... | collective-permute-start | bytes 12296 | tf_op jit(solution)/shard_map/reduce_dir_sigma/ppermute | solution.py:202
  (1 other events, 0.7 us)

commit v2 on v1

v2 whole, which is shorter than its diff:
```python
import functools

import jax
import jax.numpy as jnp
from jax import lax
from jax.experimental import pallas as pl
from jax.experimental.pallas import tpu as pltpu
from jax.sharding import PartitionSpec as P

F32 = jnp.float32
BF16 = jnp.bfloat16
VMEM = pl.BlockSpec(memory_space=pltpu.VMEM)
HBM = pl.BlockSpec(memory_space=pltpu.HBM)
SMEM = pl.BlockSpec(memory_space=pltpu.SMEM)
PAD = 8
LIMIT = 32 * 1024 * 1024
SMALL = 16 * 1024 * 1024


def call(kernel, out_shape, in_specs, scratch=(), flops=0, limit=LIMIT):
    return pl.pallas_call(
        kernel,
        out_shape=out_shape,
        in_specs=in_specs,
        out_specs=jax.tree.map(lambda _: VMEM, out_shape),
        scratch_shapes=list(scratch),
        compiler_params=pltpu.CompilerParams(vmem_limit_bytes=limit),
        cost_estimate=pl.CostEstimate(flops=flops, bytes_accessed=1 << 20, transcendentals=0),
    )


def split(values):
    high = values.astype(BF16)
    return high, (values - high.astype(F32)).astype(BF16)


def total(values):
    return jnp.sum(values, keepdims=True)


def spread(value, size):
    return jnp.broadcast_to(value, (1, size))


def load_kernel(count, *refs):
    sources, targets, sems = refs[:count], refs[count : 2 * count], refs[2 * count]
    copies = [pltpu.make_async_copy(source, target, sems.at[i]) for i, (source, target) in enumerate(zip(sources, targets))]
    for copy in copies:
        copy.start()
    for copy in copies:
        copy.wait()


def pack_kernel(wave_ref, diag_ref, packed_ref, own_diag_ref, sems):
    size = wave_ref.shape[1]
    share = packed_ref.shape[0] - size
    ops = lax.axis_index("ops")
    core, chip = ops % 2, ops // 2
    first = pl.multiple_of(chip * share, share)
    copies = [
        pltpu.make_async_copy(wave_ref.at[core], packed_ref.at[pl.ds(0, size)], sems.at[0]),
        pltpu.make_async_copy(diag_ref.at[core, pl.ds(first, share)], packed_ref.at[pl.ds(size, share)], sems.at[1]),
        pltpu.make_async_copy(diag_ref.at[core], own_diag_ref, sems.at[2]),
    ]
    for copy in copies:
        copy.start()
    for copy in copies:
        copy.wait()


def store_vector(slots, at, block):
    size = block.shape[0]
    high, low = split(block)
    slots[at, :size, :size] = high
    slots[at, :size, size:] = low
    slots[at, size:, :size] = high
    slots[at, size:, size:] = jnp.zeros_like(high)


def apply_terms(n_sec, source_ref, left_ref, right_ref, slots, stacked, weights):
    terms, owned, size, _ = left_ref.shape
    plane = lax.axis_index("sec")
    slots[2 * n_sec] = jnp.zeros_like(slots[2 * n_sec])
    for k in range(terms):
        base = 2 * (k ^ 1) * size
        for s in range(owned):
            source = source_ref[s, k]
            at = 2 * jnp.bitwise_xor(source // 2, plane) + jnp.bitwise_and(source, 1)
            pair = jnp.concatenate(split(left_ref[k, s]), axis=1)
            inner = jnp.dot(pair, slots[jnp.where(source < 0, 2 * n_sec, at)], preferred_element_type=F32)
            high, low = split(inner[:, :size] + inner[:, size:])
            stacked[s * size : (s + 1) * size, base : base + size] = high
            stacked[s * size : (s + 1) * size, base + size : base + 2 * size] = low
    for k in range(terms):
        base = 2 * k * size
        high, low = split(right_ref[k])
        weights[base : base + size, :size] = high
        weights[base : base + size, size:] = low
        weights[base + size : base + 2 * size, :size] = high
        weights[base + size : base + 2 * size, size:] = jnp.zeros_like(high)
    both = jnp.dot(stacked[...], weights[...], preferred_element_type=F32)
    return both[:, :size] + both[:, size:]


def join_kernel(keep_ref, got_ref, packed_refs, out_ref):
    rows = keep_ref.shape[0]
    out_ref[:rows] = keep_ref[...] + got_ref[...]
    share = (out_ref.shape[0] - rows) // max(len(packed_refs), 1)
    for i, ref in enumerate(packed_refs):
        out_ref[rows + i * share : rows + (i + 1) * share] = ref[ref.shape[0] - share :]


def plane_kernel(part_refs, own_diag_ref, near_ref, far_ref, diag_refs):
    rows = far_ref.shape[0]
    size = own_diag_ref.shape[0]
    summed = part_refs[0][:rows]
    for ref in part_refs[1:]:
        summed += ref[:rows]
    far_ref[...] = summed
    near_ref[:rows] = summed
    near_ref[rows:] = own_diag_ref[...]
    chip = lax.axis_index("ops") // 2
    share = size // len(part_refs)
    for m, ref in enumerate(part_refs):
        first = pl.multiple_of(jnp.bitwise_xor(chip, m) * share, share)
        for i, diag_ref in enumerate(diag_refs):
            diag_ref[pl.ds(first, share)] = ref[rows + i * share : rows + (i + 1) * share]


def first_kernel(n_sec, n_ops, source_ref, coupling_ref, left_ref, right_ref, local_ref, near_ref, mine_refs, theirs_refs,
                 keep_ref, send_ref, norm_ref, slots, stacked, weights):
    size = local_ref.shape[1]
    core = lax.axis_index("ops") % 2
    acc = jnp.zeros((size, size), F32)
    for m in range(n_sec):
        for s in range(2):
            if m < 2:
                at, block = 2 * m + s, (local_ref, near_ref)[m][s]
            else:
                at, block = 2 * m + (core if s == 0 else 1 - core), (mine_refs, theirs_refs)[s][m - 2][:size]
            acc += block * block
            store_vector(slots, at, block)
    norm_ref[...] = jnp.broadcast_to(total(acc), norm_ref.shape)
    part = apply_terms(n_sec, source_ref, left_ref, right_ref, slots, stacked, weights)
    corr = jnp.zeros((1, 1), F32)
    mirror = n_sec // 2
    blocks = []
    for s in range(2):
        if mirror < 2:
            partner = near_ref[s]
        else:
            partner = jnp.where(core == s, mine_refs[mirror - 2][:size], theirs_refs[mirror - 2][:size])
        blocks.append(part[s * size : (s + 1) * size] + (coupling_ref[0, s] / n_ops) * partner.T)
        corr += total(local_ref[s] * blocks[s])
    keep_ref[:size] = jnp.where(core == 0, blocks[0], blocks[1])
    send_ref[:size] = jnp.where(core == 0, blocks[1], blocks[0])
    keep_ref[size:] = jnp.broadcast_to(corr, (PAD, size))
    send_ref[size:] = jnp.broadcast_to(corr, (PAD, size))


def correction_kernel(n_sec, norm_ref, local_ref, near_ref, mine_refs, sum_refs, own_diag_ref, diag_refs, out_ref):
    size = local_ref.shape[1]
    core = lax.axis_index("ops") % 2
    norm_sq = norm_ref[:1, :1]
    corr = sum_refs[0][size : size + 1, :1]
    for ref in sum_refs[1:]:
        corr += ref[size : size + 1, :1]
    scale = jnp.sqrt(norm_sq)
    inverse = 1.0 / scale
    rayleigh = corr / norm_sq
    sums = [jnp.zeros((size, size), F32) for _ in range(5)]
    for m in range(n_sec):
        wave = local_ref[core] if m == 0 else near_ref[core] if m == 1 else mine_refs[m - 2][:size]
        sigma = sum_refs[m][:size]
        resid = sigma * inverse - rayleigh * (wave * inverse)
        diag = own_diag_ref[...] if m == 0 else sum_refs[1][size + PAD :] if m == 1 else diag_refs[m - 2][...]
        offset = diag - rayleigh
        corrected = resid / (1.0 + offset * offset)
        out_ref[m * size : (m + 1) * size] = corrected
        for i, factor in enumerate((wave, corrected, resid, sigma)):
            sums[i] += corrected * factor
        sums[4] += wave * resid
    out_ref[n_sec * size : (n_sec + 1) * size] = sum_refs[0][:size]
    tail = [spread(scale, size), spread(rayleigh, size)] + [spread(total(values), size) for values in sums]
    for i, row in enumerate(tail):
        out_ref[(n_sec + 1) * size + i : (n_sec + 1) * size + i + 1] = row
    for i in range(len(tail), PAD):
        out_ref[(n_sec + 1) * size + i : (n_sec + 1) * size + i + 1] = jnp.zeros((1, size), F32)


def second_kernel(n_sec, n_ops, source_ref, coupling_ref, left_ref, right_ref, mine_ref, theirs_ref,
                  keep_ref, send_ref, own_ref, scalar_ref, slots, stacked, weights):
    size = left_ref.shape[2]
    core = lax.axis_index("ops") % 2
    for m in range(n_sec):
        span = pl.ds(m * size, size)
        store_vector(slots, 2 * m + core, mine_ref[span])
        store_vector(slots, 2 * m + 1 - core, theirs_ref[span])
    part = apply_terms(n_sec, source_ref, left_ref, right_ref, slots, stacked, weights)
    curvature = jnp.zeros((1, 1), F32)
    rows = size // n_ops
    mirror = pl.ds(n_sec // 2 * size, size)
    kept = pl.ds(n_sec * size, size)
    for s in range(2):
        mine = core == s
        vec = jnp.where(mine, mine_ref[:size], theirs_ref[:size])
        partner = jnp.where(mine, mine_ref[mirror], theirs_ref[mirror])
        block = part[s * size : (s + 1) * size] + (coupling_ref[0, s] / n_ops) * partner.T
        own_ref[s] = vec
        own_ref[2 + s] = jnp.where(mine, mine_ref[kept], theirs_ref[kept])
        curvature += total(vec * block)
        for q in range(n_ops // 2):
            at_row = (q * 2 + s) * rows
            even = block[2 * q * rows : (2 * q + 1) * rows]
            odd = block[(2 * q + 1) * rows : (2 * q + 2) * rows]
            keep_ref[at_row : at_row + rows] = jnp.where(core == 0, even, odd)
            send_ref[at_row : at_row + rows] = jnp.where(core == 0, odd, even)
    keep_ref[size:] = jnp.broadcast_to(curvature, (PAD, size))
    send_ref[size:] = jnp.broadcast_to(curvature, (PAD, size))
    tail = pl.ds((n_sec + 1) * size, PAD)
    row = lax.broadcasted_iota(jnp.int32, (PAD, size), 0)
    scalar_ref[...] = mine_ref[tail] + jnp.where(row < 2, 0.0, theirs_ref[tail])


def ritz_kernel(scalar_ref, wave_ref, own_ref, applied_ref, sum_refs, wave_out, sigma_out, energy_out):
    scale, rayleigh, wave_corr, corr_sq, corr_resid, corr_sigma, wave_resid = (scalar_ref[i : i + 1, :1] for i in range(7))
    curve = sum_refs[0][:1, :1]
    for ref in sum_refs[1:]:
        curve += ref[:1, :1]
    along = wave_corr / scale
    lift = along / scale
    norm_sq = corr_sq - along * along
    norm = jnp.sqrt(norm_sq)
    coupling = (corr_resid - lift * wave_resid) / norm
    curvature = (curve - 2.0 * lift * corr_sigma + along * along * rayleigh) / norm_sq
    half_gap = 0.5 * (curvature - rayleigh)
    radius = jnp.sqrt(half_gap * half_gap + coupling * coupling)
    energy = 0.5 * (rayleigh + curvature) - radius
    safe = jnp.where(radius > 0.0, radius, 1.0)
    big = jnp.sqrt(0.5 + 0.5 * (jnp.abs(half_gap) / safe))
    small = (0.5 * (jnp.abs(coupling) / safe)) / big
    ahead = half_gap >= 0.0
    cos_part = jnp.where(radius > 0.0, jnp.where(ahead, big, small), 1.0)
    sin_size = jnp.where(radius > 0.0, jnp.where(ahead, small, big), 0.0)
    sin_part = jnp.where(coupling < 0.0, sin_size, -sin_size)
    factor = sin_part * scale / norm
    wave_out[...] = cos_part * wave_ref[...] + factor * (own_ref[:2] - lift * wave_ref[...])
    sigma_out[...] = cos_part * own_ref[2:] + factor * (applied_ref[...] - lift * own_ref[2:])
    energy_out[...] = jnp.broadcast_to(energy, energy_out.shape)


def body(n_ops, n_sec, wavefunction, hamiltonian_diag, mirror_coupling, left_env, right_env, term_source):
    owned, size, _ = wavefunction.shape
    terms = left_env.shape[0]
    half = terms // 4 * 2
    chips = n_ops // 2
    rows = size // n_ops
    me_ops, me_sec = lax.axis_index("ops"), lax.axis_index("sec")
    core, chip = me_ops % 2, me_ops // 2
    shape = jax.ShapeDtypeStruct

    def swap(values):
        return lax.ppermute(values, "ops", [(i, i ^ 1) for i in range(n_ops)])

    def to_chip(values, m):
        return lax.ppermute(values, "ops", [(i, i ^ (2 * m)) for i in range(n_ops)])

    def to_plane(values, m):
        return lax.ppermute(values, "sec", [(i, i ^ m) for i in range(n_sec)])

    def gather_planes(values):
        return [values] + [to_plane(values, m) for m in range(1, n_sec)]

    def pick(values, index):
        return lax.dynamic_index_in_dim(values, index, 0, keepdims=False)

    matmul_flops = terms * owned * size * size * size * 12
    scratch = [
        pltpu.VMEM((2 * n_sec + 1, 2 * size, 2 * size), BF16),
        pltpu.VMEM((owned * size, 2 * terms * size), BF16),
        pltpu.VMEM((2 * terms * size, 2 * size), BF16),
    ]
    message_shape = shape((size + PAD, size), F32)
    scalar_shape = shape((PAD, size), F32)

    def in_hbm(values):
        return pltpu.with_memory_space_constraint(values, pltpu.HBM)

    with jax.named_scope("gather_wave"):
        near = to_plane(wavefunction, 1)
        packed, own_diag = call(
            pack_kernel,
            (shape((size + size // chips, size), F32), shape((size, size), F32)),
            [HBM] * 2,
            [pltpu.SemaphoreType.DMA((3,))],
            limit=SMALL,
        )(in_hbm(wavefunction), in_hbm(hamiltonian_diag))
        mine = [to_plane(packed, m) for m in range(2, n_sec)]
    with jax.named_scope("load"):
        held = [left_env, right_env, wavefunction, term_source.T, mirror_coupling[None]]
        loaded = call(
            functools.partial(load_kernel, len(held)),
            tuple(shape(values.shape, values.dtype) for values in held),
            [HBM] * len(held),
            [pltpu.SemaphoreType.DMA((len(held),))],
            limit=SMALL,
        )(*[in_hbm(values) for values in held])
        loaded, mine = lax.optimization_barrier((loaded, mine))
        left, right, local, source, coupling = loaded
    with jax.named_scope("swap_wave"):
        theirs = [swap(values) for values in mine]
    with jax.named_scope("first_apply"):
        keep, send, norm = call(
            functools.partial(first_kernel, n_sec, n_ops),
            (message_shape, message_shape, scalar_shape),
            [SMEM, SMEM] + [VMEM] * 4 + [[VMEM] * (n_sec - 2)] * 2,
            scratch,
            matmul_flops,
        )(source, coupling, left, right, local, near, mine, theirs)
    with jax.named_scope("reduce_sigma"):
        share = size // chips
        joined = call(
            join_kernel,
            shape((size + PAD + (n_sec - 2) * share, size), F32),
            [VMEM, VMEM, [VMEM] * (n_sec - 2)],
            limit=SMALL,
        )(keep, swap(send), mine)
        near_sum, far_sum, diag = call(
            plane_kernel,
            (shape((2 * size + PAD, size), F32), message_shape, [shape((size, size), F32)] * (n_sec - 2)),
            [[VMEM] * chips, VMEM],
            limit=SMALL,
        )([joined] + [to_chip(joined, m) for m in range(1, chips)], own_diag)
    with jax.named_scope("gather_sigma"):
        sums = [far_sum, to_plane(near_sum, 1)] + [to_plane(far_sum, m) for m in range(2, n_sec)]
    with jax.named_scope("correction"):
        found = call(
            functools.partial(correction_kernel, n_sec),
            shape(((n_sec + 1) * size + PAD, size), F32),
            [VMEM] * 3 + [[VMEM] * (n_sec - 2), [VMEM] * n_sec, VMEM, [VMEM] * (n_sec - 2)],
            limit=SMALL,
        )(norm, local, near, mine, sums, own_diag, diag)
        other = swap(found)
    with jax.named_scope("second_apply"):
        keep, send, kept, scalars = call(
            functools.partial(second_kernel, n_sec, n_ops),
            (message_shape, message_shape, shape((2 * owned, size, size), F32), scalar_shape),
            [SMEM, SMEM] + [VMEM] * 4,
            scratch,
            matmul_flops,
        )(source, coupling, left, right, found, other)
    with jax.named_scope("reduce_dir_sigma"):
        summed = keep + swap(send)
        tail = summed[size:]

        def message(q):
            return jnp.concatenate([lax.dynamic_slice_in_dim(summed, q * (2 * rows), 2 * rows, 0), tail])

        got = sum([to_chip(message(chip ^ m), m) for m in range(1, chips)], message(chip))
        applied = got[: 2 * rows].reshape(owned, rows, size)
        curves = gather_planes(got[2 * rows :])
    with jax.named_scope("ritz"):

        def own_rows(values):
            return lax.dynamic_slice_in_dim(values, me_ops * rows, rows, 1)

        new_wave, new_sigma, energy = call(
            ritz_kernel,
            (shape((owned, rows, size), F32), shape((owned, rows, size), F32), shape((1, size), F32)),
            [VMEM] * 4 + [[VMEM] * n_sec],
        )(scalars, own_rows(local), own_rows(kept), applied, curves)
    return (new_wave, new_sigma, energy[0, :1])


def solution(mesh):
    placed = (
        P("sec", None, None),
        P("sec", None, None),
        P("sec"),
        P("ops", "sec", None, None),
        P("ops", None, None),
        P("ops", "sec"),
    )
    return jax.shard_map(
        functools.partial(body, mesh.shape["ops"], mesh.shape["sec"]),
        mesh=mesh,
        in_specs=placed,
        out_specs=(P("sec", "ops", None), P("sec", "ops", None), P()),
        check_vma=False,
    )
```

time: 67.3 us -> 60 us (0.89)
  local copies, waits for them, and re-layouts: 10.1 us -> 0.03 us
  waiting for transfers between devices: 18.9 us -> 25.2 us
  starting transfers between devices: 26.7 us -> 23.2 us
  Pallas kernels: 9.19 us -> 10.6 us
  other arithmetic: 1.12 us -> 0.03 us
    unnamed x23 -> x0, local copies, waits for them, and re-layouts: 8.39 us -> none
    ppermute x12 -> x9, starting transfers between devices: 19.2 us -> 14.8 us  [to_plane(): return lax.ppermute(values, 'sec', [(i, i ^ m) for i in range(n_sec)])]
    ppermute x6, waiting for transfers between devices: 5.53 us -> 8.77 us  [to_chip(): return lax.ppermute(values, 'ops', [(i, i ^ 2 * m) for i in range(n_ops)])]
    ppermute x12 -> x9, waiting for transfers between devices: 10.6 us -> 12.6 us  [to_plane(): return lax.ppermute(values, 'sec', [(i, i ^ m) for i in range(n_sec)])]
    pallas_call x4 -> x8, Pallas kernels: 9.19 us -> 10.6 us  [the longest x1 3.04 us: body(): call(functools.partial(second_kernel, n_sec, n_ops), (message_shape, mess...]
    ppermute x4 -> x5, waiting for transfers between devices: 2.82 us -> 3.86 us  [swap(): return lax.ppermute(values, 'ops', [(i, i ^ 1) for i in range(n_ops)])]
    dynamic_slice x2 -> x0, local copies, waits for them, and re-layouts: 0.92 us -> none  [pick(): return lax.dynamic_index_in_dim(values, index, 0, keepdims=False)]
    select_n x1 -> x0, other arithmetic: 0.88 us -> none  [body(): jnp.where(core == 0, theirs[n_sec], mine[n_sec])]
  transfers between devices with their start and end apart: 22 -> 20, of which waited for: 14 -> 17; matrix products, arithmetic and copies ran while one was open for 4% -> 0% of each run, Pallas kernels for 0% -> 4%
where the time goes in v2:
time: 60 us; the launch traced here: 59.8 us
  waiting for transfers between devices  25.2 us (42%)
  starting transfers between devices  23.2 us (39%)
  Pallas kernels  10.6 us (18%)
  between operations  0.74 us (1%)
    ppermute x9, starting transfers between devices, to_plane(): return lax.ppermute(values, 'sec', [(i, i ^ m) for i in range(n_sec)])  14.8 us
    ppermute x9, waiting for transfers between devices, to_plane(): return lax.ppermute(values, 'sec', [(i, i ^ m) for i in range(n_sec)])  12.6 us
    ppermute x6, waiting for transfers between devices, to_chip(): return lax.ppermute(values, 'ops', [(i, i ^ 2 * m) for i in range(n_ops)])  8.77 us
    ppermute x6, starting transfers between devices, to_chip(): return lax.ppermute(values, 'ops', [(i, i ^ 2 * m) for i in range(n_ops)])  7.17 us
    ppermute x5, waiting for transfers between devices, swap(): return lax.ppermute(values, 'ops', [(i, i ^ 1) for i in range(n_ops)])  3.86 us
    pallas_call x1, Pallas kernels, body(): call(functools.partial(second_kernel, n_sec, n_ops), (message_shape, mess...  3.04 us
    pallas_call x1, Pallas kernels, body(): call(functools.partial(first_kernel, n_sec, n_ops), (message_shape, messa...  3.03 us
    pallas_call x1, Pallas kernels, body(): call(functools.partial(load_kernel, len(held)), tuple((shape(values.shape...  2.4 us
  transfers between devices with their start and end apart: 20, of which 17 were waited for; matrix products, arithmetic and copies ran while one was open for 0% of the time, Pallas kernels for 4%

profile of v2, /device:TPU:0, one launch (start us, length us, event | category | flops | bytes accessed | tf_op | source)
XLA Modules:
  0.0 59.8 jit_solution(8273860873212099022)
XLA Ops:
  0.6 1.0 %gather_wave.1 = (f32[160,128]{1,0:T(8,128)S(1)}, f32[128,128]{1,0:T(8,128)S(1)}) custom-call(f32[2,128,128]{2,1,0:T(8,128)} %wave_ref.1, f32[2,128,128]{2,1,0:T(8,128)} %diag_ref.1), custom_call_target="tpu_custom_call" | custom-call | bytes 1048576 | tf_op jit(solution)/shard_map/gather_wave/pallas_call | solution.py:291
  1.6 4.1 %collective-permute-start = (f32[160,128]{1,0:T(8,128)S(1)}, f32[160,128]{1,0:T(8,128)S(1)}, u32[]{:S(2)}, u32[]{:S(2)}) collective-permute-start(f32[160,128]{1,0:T(8,128)S(1)} %get-tuple-element.36), channel_id=1, source_target_pairs={{0,2},{1,3},{2,0},{3,1},{4,6},{5,7},{6,4},{7,5},{8,10},{9,11},{10,... | collective-permute-start | bytes 245768 | tf_op jit(solution)/shard_map/gather_wave/ppermute | solution.py:269
  5.7 1.3 %collective-permute-start.1 = (f32[160,128]{1,0:T(8,128)S(1)}, f32[160,128]{1,0:T(8,128)S(1)}, u32[]{:S(2)}, u32[]{:S(2)}) collective-permute-start(f32[160,128]{1,0:T(8,128)S(1)} %get-tuple-element.36), channel_id=1, source_target_pairs={{0,3},{1,2},{2,1},{3,0},{4,7},{5,6},{6,5},{7,4},{8,11},{9,10},{10,... | collective-permute-start | bytes 245768 | tf_op jit(solution)/shard_map/gather_wave/ppermute | solution.py:269
  7.3 2.4 %load.1 = (f32[24,2,128,128]{3,2,1,0:T(8,128)S(1)}, f32[24,128,128]{2,1,0:T(8,128)S(1)}, f32[2,128,128]{2,1,0:T(8,128)S(1)}, s32[2,24]{1,0:T(2,128)S(1)}, f32[1,2]{1,0:T(1,128)S(1)}) custom-call(f32[24,2,128,128]{3,2,1,0:T(8,128)} %refs_0_.1, f32[24,128,128]{2,1,0:T(8,128)} %refs_1_.1, f32[2,128,128]{2,1,0:T(8,128)} %wave_ref.1, s32[2,24]{1,0:T(2,128)} %bitcast.6, ...), custom_call_target="tpu_custom_call" | custom-call | bytes 1048576 | tf_op jit(solution)/shard_map/load/pallas_call | solution.py:301
  9.7 1.5 %collective-permute-done.mine_refs_0_.packed_refs_0_ = f32[160,128]{1,0:T(8,128)S(1)} collective-permute-done((f32[160,128]{1,0:T(8,128)S(1)}, f32[160,128]{1,0:T(8,128)S(1)}, u32[]{:S(2)}, u32[]{:S(2)}) %collective-permute-start) | collective-permute-done | bytes 81952 | tf_op jit(solution)/shard_map/gather_wave/ppermute | solution.py:269
  11.2 1.7 %collective-permute-done.1.mine_refs_1_.packed_refs_1_ = f32[160,128]{1,0:T(8,128)S(1)} collective-permute-done((f32[160,128]{1,0:T(8,128)S(1)}, f32[160,128]{1,0:T(8,128)S(1)}, u32[]{:S(2)}, u32[]{:S(2)}) %collective-permute-start.1) | collective-permute-done | bytes 81952 | tf_op jit(solution)/shard_map/gather_wave/ppermute | solution.py:269
  13.4 0.7 %collective-permute-done.2.near_ref = f32[2,128,128]{2,1,0:T(8,128)S(1)} collective-permute-done((f32[2,128,128]{2,1,0:T(8,128)}, f32[2,128,128]{2,1,0:T(8,128)S(1)}, u32[]{:S(2)}, u32[]{:S(2)}) %collective-permute-start.2) | collective-permute-done | bytes 131104 | tf_op jit(solution)/shard_map/gather_wave/ppermute | solution.py:269
  14.3 3.0 %first_apply.1 = (f32[136,128]{1,0:T(8,128)S(1)}, f32[136,128]{1,0:T(8,128)S(1)}, f32[8,128]{1,0:T(8,128)S(1)}) custom-call(s32[2,24]{1,0:T(2,128)S(1)} %get-tuple-element.37.source_ref, f32[1,2]{1,0:T(1,128)S(1)} %get-tuple-element.38.coupling_ref, f32[24,2,128,128]{3,2,1,0:T(8,128)S(1)} %get-tuple-element.39.left_ref, ...), custom_call_target="tpu_custom_call" | custom-call | flops 1207959552 | bytes 1048576 | tf_op jit(solution)/shard_map/first_apply/pallas_call | solution.py:313
  17.8 0.9 %collective-permute-done.5.got_ref = f32[136,128]{1,0:T(8,128)S(1)} collective-permute-done((f32[136,128]{1,0:T(8,128)S(1)}, f32[136,128]{1,0:T(8,128)S(1)}, u32[]{:S(2)}, u32[]{:S(2)}) %collective-permute-start.5) | collective-permute-done | bytes 69664 | tf_op jit(solution)/shard_map/reduce_sigma/ppermute | solution.py:263
  18.7 1.6 %collective-permute-start.6 = (f32[200,128]{1,0:T(8,128)S(1)}, f32[200,128]{1,0:T(8,128)S(1)}, u32[]{:S(2)}, u32[]{:S(2)}) collective-permute-start(f32[200,128]{1,0:T(8,128)S(1)} %reduce_sigma.2.part_refs_0_), channel_id=1, source_target_pairs={{0,8},{4,12},{8,0},{12,4},{16,24},{20,28},{24,16},{28,20},{1,9},{5... | collective-permute-start | bytes 307208 | tf_op jit(solution)/shard_map/reduce_sigma/ppermute | solution.py:266
  20.3 1.5 %collective-permute-start.7 = (f32[200,128]{1,0:T(8,128)S(1)}, f32[200,128]{1,0:T(8,128)S(1)}, u32[]{:S(2)}, u32[]{:S(2)}) collective-permute-start(f32[200,128]{1,0:T(8,128)S(1)} %reduce_sigma.2.part_refs_0_), channel_id=1, source_target_pairs={{0,16},{4,20},{8,24},{12,28},{16,0},{20,4},{24,8},{28,12},{1,17},{... | collective-permute-start | bytes 307208 | tf_op jit(solution)/shard_map/reduce_sigma/ppermute | solution.py:266
  22.3 1.7 %collective-permute-done.6.part_refs_1_ = f32[200,128]{1,0:T(8,128)S(1)} collective-permute-done((f32[200,128]{1,0:T(8,128)S(1)}, f32[200,128]{1,0:T(8,128)S(1)}, u32[]{:S(2)}, u32[]{:S(2)}) %collective-permute-start.6) | collective-permute-done | bytes 102432 | tf_op jit(solution)/shard_map/reduce_sigma/ppermute | solution.py:266
  23.9 2.4 %collective-permute-done.7.part_refs_2_ = f32[200,128]{1,0:T(8,128)S(1)} collective-permute-done((f32[200,128]{1,0:T(8,128)S(1)}, f32[200,128]{1,0:T(8,128)S(1)}, u32[]{:S(2)}, u32[]{:S(2)}) %collective-permute-start.7) | collective-permute-done | bytes 102432 | tf_op jit(solution)/shard_map/reduce_sigma/ppermute | solution.py:266
  26.4 1.0 %collective-permute-done.8.part_refs_3_ = f32[200,128]{1,0:T(8,128)S(1)} collective-permute-done((f32[200,128]{1,0:T(8,128)S(1)}, f32[200,128]{1,0:T(8,128)S(1)}, u32[]{:S(2)}, u32[]{:S(2)}) %collective-permute-start.8) | collective-permute-done | bytes 102432 | tf_op jit(solution)/shard_map/reduce_sigma/ppermute | solution.py:266
  27.4 1.3 %collective-permute-start.9 = (f32[264,128]{1,0:T(8,128)S(1)}, f32[264,128]{1,0:T(8,128)S(1)}, u32[]{:S(2)}, u32[]{:S(2)}) collective-permute-start(f32[264,128]{1,0:T(8,128)S(1)} %get-tuple-element.49), channel_id=1, source_target_pairs={{0,1},{1,0},{2,3},{3,2},{4,5},{5,4},{6,7},{7,6},{8,9},{9,8},{10,11... | collective-permute-start | bytes 405512 | tf_op jit(solution)/shard_map/gather_sigma/ppermute | solution.py:269
  28.7 2.4 %collective-permute-start.10 = (f32[136,128]{1,0:T(8,128)S(1)}, f32[136,128]{1,0:T(8,128)S(1)}, u32[]{:S(2)}, u32[]{:S(2)}) collective-permute-start(f32[136,128]{1,0:T(8,128)S(1)} %get-tuple-element.48.sum_refs_0_), channel_id=1, source_target_pairs={{0,2},{1,3},{2,0},{3,1},{4,6},{5,7},{6,4},{7,5},{8,10},{9,11},{10,... | collective-permute-start | bytes 208904 | tf_op jit(solution)/shard_map/gather_sigma/ppermute | solution.py:269
  31.1 1.0 %collective-permute-start.11 = (f32[136,128]{1,0:T(8,128)S(1)}, f32[136,128]{1,0:T(8,128)S(1)}, u32[]{:S(2)}, u32[]{:S(2)}) collective-permute-start(f32[136,128]{1,0:T(8,128)S(1)} %get-tuple-element.48.sum_refs_0_), channel_id=1, source_target_pairs={{0,3},{1,2},{2,1},{3,0},{4,7},{5,6},{6,5},{7,4},{8,11},{9,10},{10,... | collective-permute-start | bytes 208904 | tf_op jit(solution)/shard_map/gather_sigma/ppermute | solution.py:269
  32.1 3.7 %collective-permute-done.10.sum_refs_2_ = f32[136,128]{1,0:T(8,128)S(1)} collective-permute-done((f32[136,128]{1,0:T(8,128)S(1)}, f32[136,128]{1,0:T(8,128)S(1)}, u32[]{:S(2)}, u32[]{:S(2)}) %collective-permute-start.10) | collective-permute-done | bytes 69664 | tf_op jit(solution)/shard_map/gather_sigma/ppermute | solution.py:269
  35.8 1.5 %collective-permute-done.11.sum_refs_3_ = f32[136,128]{1,0:T(8,128)S(1)} collective-permute-done((f32[136,128]{1,0:T(8,128)S(1)}, f32[136,128]{1,0:T(8,128)S(1)}, u32[]{:S(2)}, u32[]{:S(2)}) %collective-permute-start.11) | collective-permute-done | bytes 69664 | tf_op jit(solution)/shard_map/gather_sigma/ppermute | solution.py:269
  37.8 1.6 %collective-permute-done.12.theirs_ref = f32[648,128]{1,0:T(8,128)S(1)} collective-permute-done((f32[648,128]{1,0:T(8,128)S(1)}, f32[648,128]{1,0:T(8,128)S(1)}, u32[]{:S(2)}, u32[]{:S(2)}) %collective-permute-start.12) | collective-permute-done | bytes 331808 | tf_op jit(solution)/shard_map/correction/ppermute | solution.py:263
  39.5 3.0 %second_apply.1 = (f32[136,128]{1,0:T(8,128)S(1)}, f32[136,128]{1,0:T(8,128)S(1)}, f32[4,128,128]{2,1,0:T(8,128)S(1)}, f32[8,128]{1,0:T(8,128)S(1)}) custom-call(s32[2,24]{1,0:T(2,128)S(1)} %get-tuple-element.37.source_ref, f32[1,2]{1,0:T(1,128)S(1)} %get-tuple-element.38.coupling_ref, f32[24,2,128,128]{3,2,1,0:T(8,128)S(1)} %get-tuple-element.39.left_ref, ...), custom_call_target="tpu_custom_call" | custom-call | flops 1207959552 | bytes 1048576 | tf_op jit(solution)/shard_map/second_apply/pallas_call | solution.py:345
  42.7 1.1 %collective-permute-done.13 = f32[136,128]{1,0:T(8,128)S(1)} collective-permute-done((f32[136,128]{1,0:T(8,128)S(1)}, f32[136,128]{1,0:T(8,128)S(1)}, u32[]{:S(2)}, u32[]{:S(2)}) %collective-permute-start.13) | collective-permute-done | bytes 69664 | tf_op jit(solution)/shard_map/reduce_dir_sigma/ppermute | solution.py:263
  43.9 2.1 %collective-permute-start.14 = (f32[40,128]{1,0:T(8,128)S(1)}, f32[40,128]{1,0:T(8,128)S(1)}, u32[]{:S(2)}, u32[]{:S(2)}) collective-permute-start(f32[40,128]{1,0:T(8,128)S(1)} %get-tuple-element.63), channel_id=1, source_target_pairs={{0,8},{4,12},{8,0},{12,4},{16,24},{20,28},{24,16},{28,20},{1,9},{5... | collective-permute-start | bytes 61448 | tf_op jit(solution)/shard_map/reduce_dir_sigma/ppermute | solution.py:266
  46.5 1.0 %collective-permute-start.16 = (f32[40,128]{1,0:T(8,128)S(1)}, f32[40,128]{1,0:T(8,128)S(1)}, u32[]{:S(2)}, u32[]{:S(2)}) collective-permute-start(f32[40,128]{1,0:T(8,128)S(1)} %get-tuple-element.65), channel_id=1, source_target_pairs={{0,24},{4,28},{8,16},{12,20},{16,8},{20,12},{24,0},{28,4},{1,25},{... | collective-permute-start | bytes 61448 | tf_op jit(solution)/shard_map/reduce_dir_sigma/ppermute | solution.py:266
  47.8 2.2 %collective-permute-done.15 = f32[40,128]{1,0:T(8,128)S(1)} collective-permute-done((f32[40,128]{1,0:T(8,128)S(1)}, f32[40,128]{1,0:T(8,128)S(1)}, u32[]{:S(2)}, u32[]{:S(2)}) %collective-permute-start.15) | collective-permute-done | bytes 20512 | tf_op jit(solution)/shard_map/reduce_dir_sigma/ppermute | solution.py:266
  50.0 1.2 %collective-permute-done.16 = f32[40,128]{1,0:T(8,128)S(1)} collective-permute-done((f32[40,128]{1,0:T(8,128)S(1)}, f32[40,128]{1,0:T(8,128)S(1)}, u32[]{:S(2)}, u32[]{:S(2)}) %collective-permute-start.16) | collective-permute-done | bytes 20512 | tf_op jit(solution)/shard_map/reduce_dir_sigma/ppermute | solution.py:266
  51.2 1.2 %collective-permute-start.17 = (f32[8,128]{1,0:T(8,128)S(1)}, f32[8,128]{1,0:T(8,128)S(1)}, u32[]{:S(2)}, u32[]{:S(2)}) collective-permute-start(f32[8,128]{1,0:T(8,128)S(1)} %slice.18.sum_refs_0_), channel_id=1, source_target_pairs={{0,1},{1,0},{2,3},{3,2},{4,5},{5,4},{6,7},{7,6},{8,9},{9,8},{10,11... | collective-permute-start | bytes 12296 | tf_op jit(solution)/shard_map/reduce_dir_sigma/ppermute | solution.py:269
  52.4 1.3 %collective-permute-start.18 = (f32[8,128]{1,0:T(8,128)S(1)}, f32[8,128]{1,0:T(8,128)S(1)}, u32[]{:S(2)}, u32[]{:S(2)}) collective-permute-start(f32[8,128]{1,0:T(8,128)S(1)} %slice.18.sum_refs_0_), channel_id=1, source_target_pairs={{0,2},{1,3},{2,0},{3,1},{4,6},{5,7},{6,4},{7,5},{8,10},{9,11},{10,... | collective-permute-start | bytes 12296 | tf_op jit(solution)/shard_map/reduce_dir_sigma/ppermute | solution.py:269
  53.7 2.0 %collective-permute-start.19 = (f32[8,128]{1,0:T(8,128)S(1)}, f32[8,128]{1,0:T(8,128)S(1)}, u32[]{:S(2)}, u32[]{:S(2)}) collective-permute-start(f32[8,128]{1,0:T(8,128)S(1)} %slice.18.sum_refs_0_), channel_id=1, source_target_pairs={{0,3},{1,2},{2,1},{3,0},{4,7},{5,6},{6,5},{7,4},{8,11},{9,10},{10,... | collective-permute-start | bytes 12296 | tf_op jit(solution)/shard_map/reduce_dir_sigma/ppermute | solution.py:269
  55.7 1.2 %collective-permute-done.18.sum_refs_2_ = f32[8,128]{1,0:T(8,128)S(1)} collective-permute-done((f32[8,128]{1,0:T(8,128)S(1)}, f32[8,128]{1,0:T(8,128)S(1)}, u32[]{:S(2)}, u32[]{:S(2)}) %collective-permute-start.18) | collective-permute-done | bytes 4128 | tf_op jit(solution)/shard_map/reduce_dir_sigma/ppermute | solution.py:269
  56.9 2.2 %collective-permute-done.19.sum_refs_3_ = f32[8,128]{1,0:T(8,128)S(1)} collective-permute-done((f32[8,128]{1,0:T(8,128)S(1)}, f32[8,128]{1,0:T(8,128)S(1)}, u32[]{:S(2)}, u32[]{:S(2)}) %collective-permute-start.19) | collective-permute-done | bytes 4128 | tf_op jit(solution)/shard_map/reduce_dir_sigma/ppermute | solution.py:269
  59.1 0.7 %ritz.1 = (f32[2,16,128]{2,1,0:T(8,128)}, f32[2,16,128]{2,1,0:T(8,128)}, f32[1,128]{1,0:T(1,128)}) custom-call(f32[8,128]{1,0:T(8,128)S(1)} %get-tuple-element.52.scalar_ref, f32[2,16,128]{2,1,0:T(8,128)S(1)} %constant_dynamic-slice_fusion.5.wave_ref, f32[4,16,128]{2,1,0:T(8,128)S(1)} %constant_dynamic-slice_fusion.4.own_ref, f32[2,16,128]{2,1,0:T(8,128)S(1)} %bitcast.5, ...), custom_call_target="tpu_custom_call" | custom-call | bytes 1048576 | tf_op jit(solution)/shard_map/ritz/pallas_call | solution.py:367
  (25 shorter events, 3.4 us)
Async XLA Ops:
  1.6 9.6 %collective-permute-start = (f32[160,128]{1,0:T(8,128)S(1)}, f32[160,128]{1,0:T(8,128)S(1)}, u32[]{:S(2)}, u32[]{:S(2)}) collective-permute-start(f32[160,128]{1,0:T(8,128)S(1)} %get-tuple-element.36), channel_id=1, source_target_pairs={{0,2},{1,3},{2,0},{3,1},{4,6},{5,7},{6,4},{7,5},{8,10},{9,11},{10,... | collective-permute-start | bytes 245768 | tf_op jit(solution)/shard_map/gather_wave/ppermute | solution.py:269
  5.7 7.2 %collective-permute-start.1 = (f32[160,128]{1,0:T(8,128)S(1)}, f32[160,128]{1,0:T(8,128)S(1)}, u32[]{:S(2)}, u32[]{:S(2)}) collective-permute-start(f32[160,128]{1,0:T(8,128)S(1)} %get-tuple-element.36), channel_id=1, source_target_pairs={{0,3},{1,2},{2,1},{3,0},{4,7},{5,6},{6,5},{7,4},{8,11},{9,10},{10,... | collective-permute-start | bytes 245768 | tf_op jit(solution)/shard_map/gather_wave/ppermute | solution.py:269
  7.0 7.1 %collective-permute-start.2 = (f32[2,128,128]{2,1,0:T(8,128)}, f32[2,128,128]{2,1,0:T(8,128)S(1)}, u32[]{:S(2)}, u32[]{:S(2)}) collective-permute-start(f32[2,128,128]{2,1,0:T(8,128)} %wave_ref.1), channel_id=1, source_target_pairs={{0,1},{1,0},{2,3},{3,2},{4,5},{5,4},{6,7},{7,6},{8,9},{9,8},{10,11... | collective-permute-start | bytes 393224 | tf_op jit(solution)/shard_map/gather_wave/ppermute | solution.py:269
  12.9 1.3 %collective-permute-start.3 = (f32[160,128]{1,0:T(8,128)S(1)}, f32[160,128]{1,0:T(8,128)S(1)}, u32[]{:S(2)}, u32[]{:S(2)}) collective-permute-start(f32[160,128]{1,0:T(8,128)S(1)} %collective-permute-done.mine_refs_0_.packed_refs_0_), channel_id=1, source_target_pairs={{0,4},{4,0},{8,12},{12,8},{16,20},{20,16},{24,28},{28,24},{1,5},{5... | collective-permute-start | bytes 245768 | tf_op jit(solution)/shard_map/swap_wave/ppermute | solution.py:263
  12.9 1.4 %collective-permute-start.4 = (f32[160,128]{1,0:T(8,128)S(1)}, f32[160,128]{1,0:T(8,128)S(1)}, u32[]{:S(2)}, u32[]{:S(2)}) collective-permute-start(f32[160,128]{1,0:T(8,128)S(1)} %collective-permute-done.1.mine_refs_1_.packed_refs_1_), channel_id=1, source_target_pairs={{0,4},{4,0},{8,12},{12,8},{16,20},{20,16},{24,28},{28,24},{1,5},{5... | collective-permute-start | bytes 245768 | tf_op jit(solution)/shard_map/swap_wave/ppermute | solution.py:263
  17.4 1.3 %collective-permute-start.5 = (f32[136,128]{1,0:T(8,128)S(1)}, f32[136,128]{1,0:T(8,128)S(1)}, u32[]{:S(2)}, u32[]{:S(2)}) collective-permute-start(f32[136,128]{1,0:T(8,128)S(1)} %get-tuple-element.46), channel_id=1, source_target_pairs={{0,4},{4,0},{8,12},{12,8},{16,20},{20,16},{24,28},{28,24},{1,5},{5... | collective-permute-start | bytes 208904 | tf_op jit(solution)/shard_map/reduce_sigma/ppermute | solution.py:263
  18.7 5.2 %collective-permute-start.6 = (f32[200,128]{1,0:T(8,128)S(1)}, f32[200,128]{1,0:T(8,128)S(1)}, u32[]{:S(2)}, u32[]{:S(2)}) collective-permute-start(f32[200,128]{1,0:T(8,128)S(1)} %reduce_sigma.2.part_refs_0_), channel_id=1, source_target_pairs={{0,8},{4,12},{8,0},{12,4},{16,24},{20,28},{24,16},{28,20},{1,9},{5... | collective-permute-start | bytes 307208 | tf_op jit(solution)/shard_map/reduce_sigma/ppermute | solution.py:266
  20.3 6.1 %collective-permute-start.7 = (f32[200,128]{1,0:T(8,128)S(1)}, f32[200,128]{1,0:T(8,128)S(1)}, u32[]{:S(2)}, u32[]{:S(2)}) collective-permute-start(f32[200,128]{1,0:T(8,128)S(1)} %reduce_sigma.2.part_refs_0_), channel_id=1, source_target_pairs={{0,16},{4,20},{8,24},{12,28},{16,0},{20,4},{24,8},{28,12},{1,17},{... | collective-permute-start | bytes 307208 | tf_op jit(solution)/shard_map/reduce_sigma/ppermute | solution.py:266
  21.8 5.6 %collective-permute-start.8 = (f32[200,128]{1,0:T(8,128)S(1)}, f32[200,128]{1,0:T(8,128)S(1)}, u32[]{:S(2)}, u32[]{:S(2)}) collective-permute-start(f32[200,128]{1,0:T(8,128)S(1)} %reduce_sigma.2.part_refs_0_), channel_id=1, source_target_pairs={{0,24},{4,28},{8,16},{12,20},{16,8},{20,12},{24,0},{28,4},{1,25},{... | collective-permute-start | bytes 307208 | tf_op jit(solution)/shard_map/reduce_sigma/ppermute | solution.py:266
  27.4 10.0 %collective-permute-start.9 = (f32[264,128]{1,0:T(8,128)S(1)}, f32[264,128]{1,0:T(8,128)S(1)}, u32[]{:S(2)}, u32[]{:S(2)}) collective-permute-start(f32[264,128]{1,0:T(8,128)S(1)} %get-tuple-element.49), channel_id=1, source_target_pairs={{0,1},{1,0},{2,3},{3,2},{4,5},{5,4},{6,7},{7,6},{8,9},{9,8},{10,11... | collective-permute-start | bytes 405512 | tf_op jit(solution)/shard_map/gather_sigma/ppermute | solution.py:269
  28.7 7.1 %collective-permute-start.10 = (f32[136,128]{1,0:T(8,128)S(1)}, f32[136,128]{1,0:T(8,128)S(1)}, u32[]{:S(2)}, u32[]{:S(2)}) collective-permute-start(f32[136,128]{1,0:T(8,128)S(1)} %get-tuple-element.48.sum_refs_0_), channel_id=1, source_target_pairs={{0,2},{1,3},{2,0},{3,1},{4,6},{5,7},{6,4},{7,5},{8,10},{9,11},{10,... | collective-permute-start | bytes 208904 | tf_op jit(solution)/shard_map/gather_sigma/ppermute | solution.py:269
  31.1 6.3 %collective-permute-start.11 = (f32[136,128]{1,0:T(8,128)S(1)}, f32[136,128]{1,0:T(8,128)S(1)}, u32[]{:S(2)}, u32[]{:S(2)}) collective-permute-start(f32[136,128]{1,0:T(8,128)S(1)} %get-tuple-element.48.sum_refs_0_), channel_id=1, source_target_pairs={{0,3},{1,2},{2,1},{3,0},{4,7},{5,6},{6,5},{7,4},{8,11},{9,10},{10,... | collective-permute-start | bytes 208904 | tf_op jit(solution)/shard_map/gather_sigma/ppermute | solution.py:269
  37.8 1.7 %collective-permute-start.12 = (f32[648,128]{1,0:T(8,128)S(1)}, f32[648,128]{1,0:T(8,128)S(1)}, u32[]{:S(2)}, u32[]{:S(2)}) collective-permute-start(f32[648,128]{1,0:T(8,128)S(1)} %correction.1.mine_ref), channel_id=1, source_target_pairs={{0,4},{4,0},{8,12},{12,8},{16,20},{20,16},{24,28},{28,24},{1,5},{5... | collective-permute-start | bytes 995336 | tf_op jit(solution)/shard_map/correction/ppermute | solution.py:263
  42.5 1.3 %collective-permute-start.13 = (f32[136,128]{1,0:T(8,128)S(1)}, f32[136,128]{1,0:T(8,128)S(1)}, u32[]{:S(2)}, u32[]{:S(2)}) collective-permute-start(f32[136,128]{1,0:T(8,128)S(1)} %get-tuple-element.55), channel_id=1, source_target_pairs={{0,4},{4,0},{8,12},{12,8},{16,20},{20,16},{24,28},{28,24},{1,5},{5... | collective-permute-start | bytes 208904 | tf_op jit(solution)/shard_map/reduce_dir_sigma/ppermute | solution.py:263
  43.9 3.8 %collective-permute-start.14 = (f32[40,128]{1,0:T(8,128)S(1)}, f32[40,128]{1,0:T(8,128)S(1)}, u32[]{:S(2)}, u32[]{:S(2)}) collective-permute-start(f32[40,128]{1,0:T(8,128)S(1)} %get-tuple-element.63), channel_id=1, source_target_pairs={{0,8},{4,12},{8,0},{12,4},{16,24},{20,28},{24,16},{28,20},{1,9},{5... | collective-permute-start | bytes 61448 | tf_op jit(solution)/shard_map/reduce_dir_sigma/ppermute | solution.py:266
  46.0 4.0 %collective-permute-start.15 = (f32[40,128]{1,0:T(8,128)S(1)}, f32[40,128]{1,0:T(8,128)S(1)}, u32[]{:S(2)}, u32[]{:S(2)}) collective-permute-start(f32[40,128]{1,0:T(8,128)S(1)} %get-tuple-element.64), channel_id=1, source_target_pairs={{0,16},{4,20},{8,24},{12,28},{16,0},{20,4},{24,8},{28,12},{1,17},{... | collective-permute-start | bytes 61448 | tf_op jit(solution)/shard_map/reduce_dir_sigma/ppermute | solution.py:266
  46.5 4.7 %collective-permute-start.16 = (f32[40,128]{1,0:T(8,128)S(1)}, f32[40,128]{1,0:T(8,128)S(1)}, u32[]{:S(2)}, u32[]{:S(2)}) collective-permute-start(f32[40,128]{1,0:T(8,128)S(1)} %get-tuple-element.65), channel_id=1, source_target_pairs={{0,24},{4,28},{8,16},{12,20},{16,8},{20,12},{24,0},{28,4},{1,25},{... | collective-permute-start | bytes 61448 | tf_op jit(solution)/shard_map/reduce_dir_sigma/ppermute | solution.py:266
  51.2 4.5 %collective-permute-start.17 = (f32[8,128]{1,0:T(8,128)S(1)}, f32[8,128]{1,0:T(8,128)S(1)}, u32[]{:S(2)}, u32[]{:S(2)}) collective-permute-start(f32[8,128]{1,0:T(8,128)S(1)} %slice.18.sum_refs_0_), channel_id=1, source_target_pairs={{0,1},{1,0},{2,3},{3,2},{4,5},{5,4},{6,7},{7,6},{8,9},{9,8},{10,11... | collective-permute-start | bytes 12296 | tf_op jit(solution)/shard_map/reduce_dir_sigma/ppermute | solution.py:269
  52.4 4.5 %collective-permute-start.18 = (f32[8,128]{1,0:T(8,128)S(1)}, f32[8,128]{1,0:T(8,128)S(1)}, u32[]{:S(2)}, u32[]{:S(2)}) collective-permute-start(f32[8,128]{1,0:T(8,128)S(1)} %slice.18.sum_refs_0_), channel_id=1, source_target_pairs={{0,2},{1,3},{2,0},{3,1},{4,6},{5,7},{6,4},{7,5},{8,10},{9,11},{10,... | collective-permute-start | bytes 12296 | tf_op jit(solution)/shard_map/reduce_dir_sigma/ppermute | solution.py:269
  53.7 5.4 %collective-permute-start.19 = (f32[8,128]{1,0:T(8,128)S(1)}, f32[8,128]{1,0:T(8,128)S(1)}, u32[]{:S(2)}, u32[]{:S(2)}) collective-permute-start(f32[8,128]{1,0:T(8,128)S(1)} %slice.18.sum_refs_0_), channel_id=1, source_target_pairs={{0,3},{1,2},{2,1},{3,0},{4,7},{5,6},{6,5},{7,4},{8,11},{9,10},{10,... | collective-permute-start | bytes 12296 | tf_op jit(solution)/shard_map/reduce_dir_sigma/ppermute | solution.py:269

commit v3 on v2

v3 whole, which is shorter than its diff:
```python
import functools

import jax
import jax.numpy as jnp
from jax import lax
from jax.experimental import pallas as pl
from jax.experimental.pallas import tpu as pltpu
from jax.sharding import PartitionSpec as P

F32 = jnp.float32
BF16 = jnp.bfloat16
VMEM = pl.BlockSpec(memory_space=pltpu.VMEM)
HBM = pl.BlockSpec(memory_space=pltpu.HBM)
SMEM = pl.BlockSpec(memory_space=pltpu.SMEM)
PAD = 8
LIMIT = 16 * 1024 * 1024
SMALL = 16 * 1024 * 1024


def call(kernel, out_shape, in_specs, scratch=(), flops=0, limit=LIMIT):
    return pl.pallas_call(
        kernel,
        out_shape=out_shape,
        in_specs=in_specs,
        out_specs=jax.tree.map(lambda _: VMEM, out_shape),
        scratch_shapes=list(scratch),
        compiler_params=pltpu.CompilerParams(vmem_limit_bytes=limit),
        cost_estimate=pl.CostEstimate(flops=flops, bytes_accessed=1 << 20, transcendentals=0),
    )


def split(values):
    high = values.astype(BF16)
    return high, (values - high.astype(F32)).astype(BF16)


def total(values):
    return jnp.sum(values, keepdims=True)


def spread(value, size):
    return jnp.broadcast_to(value, (1, size))


def position(k, terms):
    return k // 2 + k % 2 * (terms // 2)


def load_kernel(left_ref, right_ref, wave_ref, source_ref, coupling_ref,
                pairs_ref, weights_ref, local_ref, sources_ref, couplings_ref, left_buf, right_buf, sems):
    terms, owned, size, _ = left_ref.shape
    sources = (left_ref, right_ref, wave_ref, source_ref, coupling_ref)
    targets = (left_buf, right_buf, local_ref, sources_ref, couplings_ref)
    copies = [pltpu.make_async_copy(source, target, sems.at[i]) for i, (source, target) in enumerate(zip(sources, targets))]
    for copy in copies:
        copy.start()
    for copy in copies:
        copy.wait()
    for k in range(terms):
        for s in range(owned):
            pairs_ref[k, s, :, :size], pairs_ref[k, s, :, size:] = split(left_buf[k, s])
        base = 2 * size * position(k, terms)
        high, low = split(right_buf[k ^ 1])
        weights_ref[base : base + size, :size] = high
        weights_ref[base : base + size, size:] = low
        weights_ref[base + size : base + 2 * size, :size] = high
        weights_ref[base + size : base + 2 * size, size:] = jnp.zeros_like(high)


def pack_kernel(wave_ref, diag_ref, packed_ref, near_ref, own_diag_ref, sems):
    owned, size, _ = wave_ref.shape
    share = packed_ref.shape[0] - size
    ops = lax.axis_index("ops")
    core, chip = ops % 2, ops // 2
    rows = pl.ds(pl.multiple_of(chip * share, share), share)
    moves = [
        (wave_ref.at[core], packed_ref.at[pl.ds(0, size)]),
        (diag_ref.at[core, rows], packed_ref.at[pl.ds(size, share)]),
        *((wave_ref.at[s], near_ref.at[pl.ds(s * size, size)]) for s in range(owned)),
        (diag_ref.at[core, rows], near_ref.at[pl.ds(owned * size, share)]),
        (diag_ref.at[core], own_diag_ref),
    ]
    copies = [pltpu.make_async_copy(source, target, sems.at[i]) for i, (source, target) in enumerate(moves)]
    for copy in copies:
        copy.start()
    for copy in copies:
        copy.wait()


def store_vector(slots, at, block):
    size = block.shape[0]
    high, low = split(block)
    slots[at, :size, :size] = high
    slots[at, :size, size:] = low
    slots[at, size:, :size] = high
    slots[at, size:, size:] = jnp.zeros_like(high)


def apply_terms(chosen, n_sec, source_ref, pairs_ref, weights_ref, slots, stacked):
    terms, owned, size, _ = pairs_ref.shape
    plane = lax.axis_index("sec")
    first = position(chosen[0], terms)
    for k in chosen:
        base = 2 * size * (position(k, terms) - first)
        for s in range(owned):
            source = source_ref[s, k]
            at = 2 * jnp.bitwise_xor(source // 2, plane) + jnp.bitwise_and(source, 1)
            inner = jnp.dot(pairs_ref[k, s], slots[jnp.where(source < 0, 2 * n_sec, at)], preferred_element_type=F32)
            high, low = split(inner[:, :size] + inner[:, size:])
            stacked[s * size : (s + 1) * size, base : base + size] = high
            stacked[s * size : (s + 1) * size, base + size : base + 2 * size] = low
    span = pl.ds(2 * size * first, 2 * size * len(chosen))
    both = jnp.dot(stacked[...], weights_ref[span], preferred_element_type=F32)
    return both[:, :size] + both[:, size:]


def join_kernel(keep_ref, got_ref, packed_refs, out_ref):
    rows = keep_ref.shape[0]
    out_ref[:rows] = keep_ref[...] + got_ref[...]
    share = (out_ref.shape[0] - rows) // max(len(packed_refs), 1)
    for i, ref in enumerate(packed_refs):
        out_ref[rows + i * share : rows + (i + 1) * share] = ref[ref.shape[0] - share :]


def plane_kernel(part_refs, sum_ref, *diag_refs):
    rows = sum_ref.shape[0]
    size = rows - PAD
    summed = part_refs[0][:rows]
    for ref in part_refs[1:]:
        summed += ref[:rows]
    sum_ref[...] = summed
    chip = lax.axis_index("ops") // 2
    share = size // len(part_refs)
    for m, ref in enumerate(part_refs):
        first = pl.multiple_of(jnp.bitwise_xor(chip, m) * share, share)
        for i, diag_ref in enumerate(diag_refs):
            diag_ref[pl.ds(first, share)] = ref[rows + i * share : rows + (i + 1) * share]


def first_kernel(n_sec, n_ops, source_ref, coupling_ref, pairs_ref, weights_ref, local_ref, near_ref, mine_refs, theirs_refs,
                 keep_ref, send_ref, norm_ref, slots, stacked):
    size = local_ref.shape[1]
    core = lax.axis_index("ops") % 2
    acc = jnp.zeros((size, size), F32)
    for m in range(n_sec):
        for s in range(2):
            if m < 2:
                at, block = 2 * m + s, (local_ref[s], near_ref[s * size : (s + 1) * size])[m]
            else:
                at, block = 2 * m + (core if s == 0 else 1 - core), (mine_refs, theirs_refs)[s][m - 2][:size]
            acc += block * block
            store_vector(slots, at, block)
    slots[2 * n_sec] = jnp.zeros_like(slots[2 * n_sec])
    norm_ref[...] = jnp.broadcast_to(total(acc), norm_ref.shape)
    part = apply_terms(range(pairs_ref.shape[0]), n_sec, source_ref, pairs_ref, weights_ref, slots, stacked)
    corr = jnp.zeros((1, 1), F32)
    mirror = n_sec // 2
    blocks = []
    for s in range(2):
        if mirror < 2:
            partner = near_ref[s * size : (s + 1) * size]
        else:
            partner = jnp.where(core == s, mine_refs[mirror - 2][:size], theirs_refs[mirror - 2][:size])
        blocks.append(part[s * size : (s + 1) * size] + (coupling_ref[0, s] / n_ops) * partner.T)
        corr += total(local_ref[s] * blocks[s])
    keep_ref[:size] = jnp.where(core == 0, blocks[0], blocks[1])
    send_ref[:size] = jnp.where(core == 0, blocks[1], blocks[0])
    keep_ref[size:] = jnp.broadcast_to(corr, (PAD, size))
    send_ref[size:] = jnp.broadcast_to(corr, (PAD, size))


def correction_kernel(n_sec, norm_ref, whole_ref, near_ref, mine_refs, sum_refs, diag_refs, out_ref):
    size = whole_ref.shape[1]
    core = lax.axis_index("ops") % 2
    norm_sq = norm_ref[:1, :1]
    corr = sum_refs[0][size : size + 1, :1]
    for ref in sum_refs[1:]:
        corr += ref[size : size + 1, :1]
    scale = jnp.sqrt(norm_sq)
    inverse = 1.0 / scale
    rayleigh = corr / norm_sq
    sums = [jnp.zeros((size, size), F32) for _ in range(5)]
    for m in range(n_sec):
        if m < 2:
            ref = (whole_ref, near_ref)[m]
            wave = ref[pl.ds(pl.multiple_of(core * size, size), size)]
        else:
            wave = mine_refs[m - 2][:size]
        sigma = sum_refs[m][:size]
        resid = sigma * inverse - rayleigh * (wave * inverse)
        offset = diag_refs[m][...] - rayleigh
        corrected = resid / (1.0 + offset * offset)
        out_ref[m * size : (m + 1) * size] = corrected
        for i, factor in enumerate((wave, corrected, resid, sigma)):
            sums[i] += corrected * factor
        sums[4] += wave * resid
    out_ref[n_sec * size : (n_sec + 1) * size] = sum_refs[0][:size]
    tail = [spread(scale, size), spread(rayleigh, size)] + [spread(total(values), size) for values in sums]
    for i, row in enumerate(tail):
        out_ref[(n_sec + 1) * size + i : (n_sec + 1) * size + i + 1] = row
    for i in range(len(tail), PAD):
        out_ref[(n_sec + 1) * size + i : (n_sec + 1) * size + i + 1] = jnp.zeros((1, size), F32)


def rows_here(block, core):
    rows = block.shape[0] // 2
    return jnp.where(core == 0, block[:rows], block[rows:])


def even_kernel(n_sec, n_ops, source_ref, coupling_ref, pairs_ref, weights_ref, mine_ref, theirs_ref,
                slots, part_ref, curve_ref, own_ref, scalar_ref, stacked):
    size = pairs_ref.shape[2]
    core = lax.axis_index("ops") % 2
    for m in range(n_sec):
        span = pl.ds(m * size, size)
        store_vector(slots, 2 * m + core, mine_ref[span])
        store_vector(slots, 2 * m + 1 - core, theirs_ref[span])
    slots[2 * n_sec] = jnp.zeros_like(slots[2 * n_sec])
    part = apply_terms(range(0, pairs_ref.shape[0], 2), n_sec, source_ref, pairs_ref, weights_ref, slots, stacked)
    curve = jnp.zeros((1, 1), F32)
    mirror = pl.ds(n_sec // 2 * size, size)
    chip = lax.axis_index("ops") // 2
    share = 2 * own_ref.shape[1]
    for s in range(2):
        mine = core == s
        vec = jnp.where(mine, mine_ref[:size], theirs_ref[:size])
        partner = jnp.where(mine, mine_ref[mirror], theirs_ref[mirror])
        block = part[s * size : (s + 1) * size]
        mirrored = (coupling_ref[0, s] / n_ops) * partner.T
        part_ref[s] = block + mirrored
        for i, first in enumerate((0, n_sec)):
            span = pl.ds(pl.multiple_of(first * size + chip * share, share), share)
            own_ref[2 * i + s] = rows_here(jnp.where(mine, mine_ref[span], theirs_ref[span]), core)
        curve += total(vec * (2.0 * block + mirrored))
    curve_ref[...] = jnp.broadcast_to(curve, curve_ref.shape)
    tail = pl.ds((n_sec + 1) * size, PAD)
    row = lax.broadcasted_iota(jnp.int32, (PAD, size), 0)
    scalar_ref[...] = mine_ref[tail] + jnp.where(row < 2, 0.0, theirs_ref[tail])


def odd_kernel(n_sec, n_ops, source_ref, pairs_ref, weights_ref, slots, part_ref, keep_ref, send_ref, stacked):
    size = pairs_ref.shape[2]
    core = lax.axis_index("ops") % 2
    part = apply_terms(range(1, pairs_ref.shape[0], 2), n_sec, source_ref, pairs_ref, weights_ref, slots, stacked)
    rows = size // n_ops
    for s in range(2):
        block = part[s * size : (s + 1) * size] + part_ref[s]
        for q in range(n_ops // 2):
            at_row = (q * 2 + s) * rows
            even = block[2 * q * rows : (2 * q + 1) * rows]
            odd = block[(2 * q + 1) * rows : (2 * q + 2) * rows]
            keep_ref[at_row : at_row + rows] = jnp.where(core == 0, even, odd)
            send_ref[at_row : at_row + rows] = jnp.where(core == 0, odd, even)


def curve_kernel(keep_ref, send_ref, curve_refs, keep_out, send_out):
    size = keep_ref.shape[0]
    curve = curve_refs[0][...]
    for ref in curve_refs[1:]:
        curve += ref[...]
    for ref, out in ((keep_ref, keep_out), (send_ref, send_out)):
        out[:size] = ref[...]
        out[size:] = curve


def deal_kernel(keep_ref, got_ref, *out_refs):
    share = out_refs[0].shape[0] - PAD
    size = keep_ref.shape[0] - PAD
    chip = lax.axis_index("ops") // 2
    tail = keep_ref[size:] + got_ref[size:]
    for m, out_ref in enumerate(out_refs):
        span = pl.ds(pl.multiple_of(jnp.bitwise_xor(chip, m) * share, share), share)
        out_ref[:share] = keep_ref[span] + got_ref[span]
        out_ref[share:] = tail


def ritz_kernel(scalar_ref, local_ref, own_ref, got_refs, wave_out, sigma_out, energy_out):
    scale, rayleigh, wave_corr, corr_sq, corr_resid, corr_sigma, wave_resid = (scalar_ref[i : i + 1, :1] for i in range(7))
    rows = own_ref.shape[1]
    got = got_refs[0][...]
    for ref in got_refs[1:]:
        got += ref[...]
    curve = got[2 * rows : 2 * rows + 1, :1]
    ops = lax.axis_index("ops")
    core = ops % 2
    span = pl.ds(pl.multiple_of(ops // 2 * (2 * rows), 2 * rows), 2 * rows)
    along = wave_corr / scale
    lift = along / scale
    norm_sq = corr_sq - along * along
    norm = jnp.sqrt(norm_sq)
    coupling = (corr_resid - lift * wave_resid) / norm
    curvature = (curve - 2.0 * lift * corr_sigma + along * along * rayleigh) / norm_sq
    half_gap = 0.5 * (curvature - rayleigh)
    radius = jnp.sqrt(half_gap * half_gap + coupling * coupling)
    energy = 0.5 * (rayleigh + curvature) - radius
    safe = jnp.where(radius > 0.0, radius, 1.0)
    big = jnp.sqrt(0.5 + 0.5 * (jnp.abs(half_gap) / safe))
    small = (0.5 * (jnp.abs(coupling) / safe)) / big
    ahead = half_gap >= 0.0
    cos_part = jnp.where(radius > 0.0, jnp.where(ahead, big, small), 1.0)
    sin_size = jnp.where(radius > 0.0, jnp.where(ahead, small, big), 0.0)
    sin_part = jnp.where(coupling < 0.0, sin_size, -sin_size)
    factor = sin_part * scale / norm
    for s in range(2):
        wave, sigma = rows_here(local_ref[s, span], core), own_ref[2 + s]
        wave_out[s] = cos_part * wave + factor * (own_ref[s] - lift * wave)
        sigma_out[s] = cos_part * sigma + factor * (got[s * rows : (s + 1) * rows] - lift * sigma)
    energy_out[...] = jnp.broadcast_to(energy, energy_out.shape)


def body(n_ops, n_sec, wavefunction, hamiltonian_diag, mirror_coupling, left_env, right_env, term_source):
    owned, size, _ = wavefunction.shape
    terms = left_env.shape[0]
    half = terms // 4 * 2
    chips = n_ops // 2
    rows = size // n_ops
    shape = jax.ShapeDtypeStruct

    def swap(values):
        return lax.ppermute(values, "ops", [(i, i ^ 1) for i in range(n_ops)])

    def to_chip(values, m):
        return lax.ppermute(values, "ops", [(i, i ^ (2 * m)) for i in range(n_ops)])

    def to_plane(values, m):
        return lax.ppermute(values, "sec", [(i, i ^ m) for i in range(n_sec)])

    def gather_planes(values):
        return [values] + [to_plane(values, m) for m in range(1, n_sec)]

    matmul_flops = terms * owned * size * size * size * 12
    slot_shape = (2 * n_sec + 1, 2 * size, 2 * size)
    stack_shape = (owned * size, 2 * terms * size)
    half_shape = (owned * size, terms * size)
    message_shape = shape((size + PAD, size), F32)
    scalar_shape = shape((PAD, size), F32)

    def in_hbm(values):
        return pltpu.with_memory_space_constraint(values, pltpu.HBM)

    with jax.named_scope("gather_wave"):
        packed, whole, own_diag = call(
            pack_kernel,
            (
                shape((size + size // chips, size), F32),
                shape((owned * size + size // chips, size), F32),
                shape((size, size), F32),
            ),
            [HBM] * 2,
            [pltpu.SemaphoreType.DMA((owned + 4,))],
            limit=SMALL,
        )(in_hbm(wavefunction), in_hbm(hamiltonian_diag))
        mine = [to_plane(packed, m) for m in range(2, n_sec)]
        near = to_plane(whole, 1)
    with jax.named_scope("load"):
        held = [left_env, right_env, wavefunction, term_source.T, mirror_coupling[None]]
        loaded = call(
            load_kernel,
            (
                shape((terms, owned, size, 2 * size), BF16),
                shape((2 * terms * size, 2 * size), BF16),
                *(shape(values.shape, values.dtype) for values in held[2:]),
            ),
            [HBM] * len(held),
            [
                pltpu.VMEM(left_env.shape, F32),
                pltpu.VMEM(right_env.shape, F32),
                pltpu.SemaphoreType.DMA((len(held),)),
            ],
            limit=SMALL,
        )(*[in_hbm(values) for values in held])
        loaded, mine = lax.optimization_barrier((loaded, mine))
        pairs, weights, local, source, coupling = loaded
    with jax.named_scope("swap_wave"):
        theirs = [swap(values) for values in mine]
    with jax.named_scope("first_apply"):
        keep, send, norm = call(
            functools.partial(first_kernel, n_sec, n_ops),
            (message_shape, message_shape, scalar_shape),
            [SMEM, SMEM] + [VMEM] * 4 + [[VMEM] * (n_sec - 2)] * 2,
            [pltpu.VMEM(slot_shape, BF16), pltpu.VMEM(stack_shape, BF16)],
            matmul_flops,
        )(source, coupling, pairs, weights, local, near, mine, theirs)
    with jax.named_scope("reduce_sigma"):
        share = size // chips
        joined = call(
            join_kernel,
            shape((size + PAD + (n_sec - 1) * share, size), F32),
            [VMEM, VMEM, [VMEM] * (n_sec - 1)],
            limit=SMALL,
        )(keep, swap(send), [near] + mine)
        summed, *diag = call(
            plane_kernel,
            (message_shape, *[shape((size, size), F32)] * (n_sec - 1)),
            [[VMEM] * chips],
            limit=SMALL,
        )([joined] + [to_chip(joined, m) for m in range(1, chips)])
    with jax.named_scope("gather_sigma"):
        sums = gather_planes(summed)
    with jax.named_scope("correction"):
        found = call(
            functools.partial(correction_kernel, n_sec),
            shape(((n_sec + 1) * size + PAD, size), F32),
            [VMEM] * 3 + [[VMEM] * (n_sec - 2), [VMEM] * n_sec, [VMEM] * n_sec],
            limit=SMALL,
        )(norm, whole, near, mine, sums, [own_diag] + diag)
        other = swap(found)
    with jax.named_scope("even_terms"):
        slots, part, curve, kept, scalars = call(
            functools.partial(even_kernel, n_sec, n_ops),
            (
                shape(slot_shape, BF16),
                shape((owned, size, size), F32),
                scalar_shape,
                shape((2 * owned, rows, size), F32),
                scalar_shape,
            ),
            [SMEM, SMEM] + [VMEM] * 4,
            [pltpu.VMEM(half_shape, BF16)],
            matmul_flops // 2,
        )(source, coupling, pairs, weights, found, other)
        curves = gather_planes(curve)
    with jax.named_scope("odd_terms"):
        keep, send = call(
            functools.partial(odd_kernel, n_sec, n_ops),
            (shape((size, size), F32), shape((size, size), F32)),
            [SMEM] + [VMEM] * 4,
            [pltpu.VMEM(half_shape, BF16)],
            matmul_flops // 2,
        )(source, pairs, weights, slots, part)
    with jax.named_scope("reduce_dir_sigma"):
        keep, send = call(curve_kernel, (message_shape, message_shape), [VMEM, VMEM, [VMEM] * n_sec], limit=SMALL)(
            keep, send, curves
        )
        dealt = call(deal_kernel, [shape((2 * rows + PAD, size), F32)] * chips, [VMEM, VMEM], limit=SMALL)(keep, swap(send))
        got = [dealt[0]] + [to_chip(dealt[m], m) for m in range(1, chips)]
    with jax.named_scope("ritz"):
        new_wave, new_sigma, energy = call(
            ritz_kernel,
            (shape((owned, rows, size), F32), shape((owned, rows, size), F32), shape((1, size), F32)),
            [VMEM] * 3 + [[VMEM] * chips],
        )(scalars, local, kept, got)
    return (new_wave, new_sigma, energy[0, :1])


def solution(mesh):
    placed = (
        P("sec", None, None),
        P("sec", None, None),
        P("sec"),
        P("ops", "sec", None, None),
        P("ops", None, None),
        P("ops", "sec"),
    )
    return jax.shard_map(
        functools.partial(body, mesh.shape["ops"], mesh.shape["sec"]),
        mesh=mesh,
        in_specs=placed,
        out_specs=(P("sec", "ops", None), P("sec", "ops", None), P()),
        check_vma=False,
    )
```

time: 60 us -> 57.2 us (0.953)
  waiting for transfers between devices: 25.2 us -> 21.6 us
  Pallas kernels: 10.6 us -> 11.8 us
    ppermute x9, waiting for transfers between devices: 12.6 us -> 8.62 us  [to_plane(): return lax.ppermute(values, 'sec', [(i, i ^ m) for i in range(n_sec)])]
    pallas_call x5 -> x8, Pallas kernels: 6.45 us -> 7.89 us  [the longest x1 3.28 us: body(): call(load_kernel, (shape((terms, owned, size, 2 * size), BF16), shape((2...]
    ppermute x5, waiting for transfers between devices: 3.86 us -> 4.69 us  [swap(): return lax.ppermute(values, 'ops', [(i, i ^ 1) for i in range(n_ops)])]
  transfers between devices with their start and end apart: 20 -> 20, of which waited for: 17 -> 15; matrix products, arithmetic and copies ran while one was open for 0% -> 0% of each run, Pallas kernels for 4% -> 9%
where the time goes in v3:
time: 57.2 us; the launch traced here: 57 us
  starting transfers between devices  22.9 us (40%)
  waiting for transfers between devices  21.6 us (38%)
  Pallas kernels  11.8 us (21%)
  between operations  0.73 us (1%)
    ppermute x9, starting transfers between devices, to_plane(): return lax.ppermute(values, 'sec', [(i, i ^ m) for i in range(n_sec)])  14.7 us
    ppermute x9, waiting for transfers between devices, to_plane(): return lax.ppermute(values, 'sec', [(i, i ^ m) for i in range(n_sec)])  8.62 us
    ppermute x6, waiting for transfers between devices, to_chip(): return lax.ppermute(values, 'ops', [(i, i ^ 2 * m) for i in range(n_ops)])  8.33 us
    ppermute x6, starting transfers between devices, to_chip(): return lax.ppermute(values, 'ops', [(i, i ^ 2 * m) for i in range(n_ops)])  7.11 us
    ppermute x5, waiting for transfers between devices, swap(): return lax.ppermute(values, 'ops', [(i, i ^ 1) for i in range(n_ops)])  4.69 us
    pallas_call x1, Pallas kernels, body(): call(load_kernel, (shape((terms, owned, size, 2 * size), BF16), shape((2...  3.28 us
    pallas_call x1, Pallas kernels, body(): call(functools.partial(first_kernel, n_sec, n_ops), (message_shape, messa...  2.82 us
    pallas_call x1, Pallas kernels, body(): call(functools.partial(even_kernel, n_sec, n_ops), (shape(slot_shape, BF1...  1.87 us
  transfers between devices with their start and end apart: 20, of which 15 were waited for; matrix products, arithmetic and copies ran while one was open for 0% of the time, Pallas kernels for 9%

profile of v3, /device:TPU:0, one launch (start us, length us, event | category | flops | bytes accessed | tf_op | source)
XLA Modules:
  0.0 57.0 jit_solution(7544976401272881437)
XLA Ops:
  0.6 1.1 %gather_wave.1 = (f32[160,128]{1,0:T(8,128)S(1)}, f32[288,128]{1,0:T(8,128)S(1)}, f32[128,128]{1,0:T(8,128)S(1)}) custom-call(f32[2,128,128]{2,1,0:T(8,128)} %wave_ref.3, f32[2,128,128]{2,1,0:T(8,128)} %diag_ref.1), custom_call_target="tpu_custom_call" | custom-call | bytes 1048576 | tf_op jit(solution)/shard_map/gather_wave/pallas_call | solution.py:342
  1.7 5.1 %collective-permute-start.1 = (f32[160,128]{1,0:T(8,128)S(1)}, f32[160,128]{1,0:T(8,128)S(1)}, u32[]{:S(2)}, u32[]{:S(2)}) collective-permute-start(f32[160,128]{1,0:T(8,128)S(1)} %get-tuple-element.46), channel_id=1, source_target_pairs={{0,3},{1,2},{2,1},{3,0},{4,7},{5,6},{6,5},{7,4},{8,11},{9,10},{10,... | collective-permute-start | bytes 245768 | tf_op jit(solution)/shard_map/gather_wave/ppermute | solution.py:326
  6.8 0.6 %collective-permute-start.2 = (f32[288,128]{1,0:T(8,128)S(1)}, f32[288,128]{1,0:T(8,128)S(1)}, u32[]{:S(2)}, u32[]{:S(2)}) collective-permute-start(f32[288,128]{1,0:T(8,128)S(1)} %get-tuple-element.52.whole_ref), channel_id=1, source_target_pairs={{0,1},{1,0},{2,3},{3,2},{4,5},{5,4},{6,7},{7,6},{8,9},{9,8},{10,11... | collective-permute-start | bytes 442376 | tf_op jit(solution)/shard_map/gather_wave/ppermute | solution.py:326
  7.5 3.3 %load.1 = (bf16[24,2,128,256]{3,2,1,0:T(8,128)(2,1)S(1)}, bf16[6144,256]{1,0:T(8,128)(2,1)S(1)}, f32[2,128,128]{2,1,0:T(8,128)S(1)}, s32[2,24]{1,0:T(2,128)S(1)}, f32[1,2]{1,0:T(1,128)S(1)}) custom-call(f32[24,2,128,128]{3,2,1,0:T(8,128)} %left_ref.1, f32[24,128,128]{2,1,0:T(8,128)} %right_ref.1, f32[2,128,128]{2,1,0:T(8,128)} %wave_ref.3, s32[2,24]{1,0:T(2,128)} %bitcast.4, ...), custom_call_target="tpu_custom_call" | custom-call | bytes 1048576 | tf_op jit(solution)/shard_map/load/pallas_call | solution.py:357
  10.8 3.0 %collective-permute-done.mine_refs_0_.packed_refs_1_ = f32[160,128]{1,0:T(8,128)S(1)} collective-permute-done((f32[160,128]{1,0:T(8,128)S(1)}, f32[160,128]{1,0:T(8,128)S(1)}, u32[]{:S(2)}, u32[]{:S(2)}) %collective-permute-start) | collective-permute-done | bytes 81952 | tf_op jit(solution)/shard_map/gather_wave/ppermute | solution.py:326
  13.8 0.5 collective-permute-start.4
  14.3 0.8 %collective-permute-done.3.theirs_refs_0_ = f32[160,128]{1,0:T(8,128)S(1)} collective-permute-done((f32[160,128]{1,0:T(8,128)S(1)}, f32[160,128]{1,0:T(8,128)S(1)}, u32[]{:S(2)}, u32[]{:S(2)}) %collective-permute-start.3) | collective-permute-done | bytes 81952 | tf_op jit(solution)/shard_map/swap_wave/ppermute | solution.py:320
  15.2 2.8 %first_apply.1 = (f32[136,128]{1,0:T(8,128)S(1)}, f32[136,128]{1,0:T(8,128)S(1)}, f32[8,128]{1,0:T(8,128)S(1)}) custom-call(s32[2,24]{1,0:T(2,128)S(1)} %get-tuple-element.47.source_ref, f32[1,2]{1,0:T(1,128)S(1)} %get-tuple-element.48.coupling_ref, bf16[24,2,128,256]{3,2,1,0:T(8,128)(2,1)S(1)} %get-tuple-element.49.pairs_ref, ...), custom_call_target="tpu_custom_call" | custom-call | flops 1207959552 | bytes 1048576 | tf_op jit(solution)/shard_map/first_apply/pallas_call | solution.py:377
  18.0 0.4 collective-permute-start.5
  18.5 0.9 %collective-permute-done.5.got_ref = f32[136,128]{1,0:T(8,128)S(1)} collective-permute-done((f32[136,128]{1,0:T(8,128)S(1)}, f32[136,128]{1,0:T(8,128)S(1)}, u32[]{:S(2)}, u32[]{:S(2)}) %collective-permute-start.5) | collective-permute-done | bytes 69664 | tf_op jit(solution)/shard_map/reduce_sigma/ppermute | solution.py:320
  19.4 2.5 %collective-permute-start.8 = (f32[232,128]{1,0:T(8,128)S(1)}, f32[232,128]{1,0:T(8,128)S(1)}, u32[]{:S(2)}, u32[]{:S(2)}) collective-permute-start(f32[232,128]{1,0:T(8,128)S(1)} %reduce_sigma.2.part_refs_0_), channel_id=1, source_target_pairs={{0,24},{4,28},{8,16},{12,20},{16,8},{20,12},{24,0},{28,4},{1,25},{... | collective-permute-start | bytes 356360 | tf_op jit(solution)/shard_map/reduce_sigma/ppermute | solution.py:323
  21.9 0.5 collective-permute-start.7
  22.4 0.5 collective-permute-start.6
  22.9 3.0 %collective-permute-done.8.part_refs_3_ = f32[232,128]{1,0:T(8,128)S(1)} collective-permute-done((f32[232,128]{1,0:T(8,128)S(1)}, f32[232,128]{1,0:T(8,128)S(1)}, u32[]{:S(2)}, u32[]{:S(2)}) %collective-permute-start.8) | collective-permute-done | bytes 118816 | tf_op jit(solution)/shard_map/reduce_sigma/ppermute | solution.py:323
  25.9 2.4 %collective-permute-done.7.part_refs_2_ = f32[232,128]{1,0:T(8,128)S(1)} collective-permute-done((f32[232,128]{1,0:T(8,128)S(1)}, f32[232,128]{1,0:T(8,128)S(1)}, u32[]{:S(2)}, u32[]{:S(2)}) %collective-permute-start.7) | collective-permute-done | bytes 118816 | tf_op jit(solution)/shard_map/reduce_sigma/ppermute | solution.py:323
  28.5 2.7 %collective-permute-start.11 = (f32[136,128]{1,0:T(8,128)S(1)}, f32[136,128]{1,0:T(8,128)S(1)}, u32[]{:S(2)}, u32[]{:S(2)}) collective-permute-start(f32[136,128]{1,0:T(8,128)S(1)} %get-tuple-element.58.sum_refs_0_), channel_id=1, source_target_pairs={{0,3},{1,2},{2,1},{3,0},{4,7},{5,6},{6,5},{7,4},{8,11},{9,10},{10,... | collective-permute-start | bytes 208904 | tf_op jit(solution)/shard_map/gather_sigma/ppermute | solution.py:326
  31.2 1.7 %collective-permute-start.9 = (f32[136,128]{1,0:T(8,128)S(1)}, f32[136,128]{1,0:T(8,128)S(1)}, u32[]{:S(2)}, u32[]{:S(2)}) collective-permute-start(f32[136,128]{1,0:T(8,128)S(1)} %get-tuple-element.58.sum_refs_0_), channel_id=1, source_target_pairs={{0,1},{1,0},{2,3},{3,2},{4,5},{5,4},{6,7},{7,6},{8,9},{9,8},{10,11... | collective-permute-start | bytes 208904 | tf_op jit(solution)/shard_map/gather_sigma/ppermute | solution.py:326
  33.0 2.3 %collective-permute-done.11.sum_refs_3_ = f32[136,128]{1,0:T(8,128)S(1)} collective-permute-done((f32[136,128]{1,0:T(8,128)S(1)}, f32[136,128]{1,0:T(8,128)S(1)}, u32[]{:S(2)}, u32[]{:S(2)}) %collective-permute-start.11) | collective-permute-done | bytes 69664 | tf_op jit(solution)/shard_map/gather_sigma/ppermute | solution.py:326
  35.3 2.1 %collective-permute-done.10.sum_refs_2_ = f32[136,128]{1,0:T(8,128)S(1)} collective-permute-done((f32[136,128]{1,0:T(8,128)S(1)}, f32[136,128]{1,0:T(8,128)S(1)}, u32[]{:S(2)}, u32[]{:S(2)}) %collective-permute-start.10) | collective-permute-done | bytes 69664 | tf_op jit(solution)/shard_map/gather_sigma/ppermute | solution.py:326
  37.4 0.4 correction.1.mine_ref
  37.9 1.6 %collective-permute-done.12.theirs_ref = f32[648,128]{1,0:T(8,128)S(1)} collective-permute-done((f32[648,128]{1,0:T(8,128)S(1)}, f32[648,128]{1,0:T(8,128)S(1)}, u32[]{:S(2)}, u32[]{:S(2)}) %collective-permute-start.12) | collective-permute-done | bytes 331808 | tf_op jit(solution)/shard_map/correction/ppermute | solution.py:320
  39.5 1.9 %even_terms.1 = (bf16[9,256,256]{2,1,0:T(8,128)(2,1)S(1)}, f32[2,128,128]{2,1,0:T(8,128)S(1)}, f32[8,128]{1,0:T(8,128)S(1)}, f32[4,16,128]{2,1,0:T(8,128)S(1)}, f32[8,128]{1,0:T(8,128)S(1)}) custom-call(s32[2,24]{1,0:T(2,128)S(1)} %get-tuple-element.47.source_ref, f32[1,2]{1,0:T(1,128)S(1)} %get-tuple-element.48.coupling_ref, ...), custom_call_target="tpu_custom_call" | custom-call | flops 603979776 | bytes 1048576 | tf_op jit(solution)/shard_map/even_terms/pallas_call | solution.py:409
  41.4 2.7 %collective-permute-start.15 = (f32[8,128]{1,0:T(8,128)S(1)}, f32[8,128]{1,0:T(8,128)S(1)}, u32[]{:S(2)}, u32[]{:S(2)}) collective-permute-start(f32[8,128]{1,0:T(8,128)S(1)} %get-tuple-element.69.curve_refs_0_), channel_id=1, source_target_pairs={{0,3},{1,2},{2,1},{3,0},{4,7},{5,6},{6,5},{7,4},{8,11},{9,10},{10,... | collective-permute-start | bytes 12296 | tf_op jit(solution)/shard_map/even_terms/ppermute | solution.py:326
  44.1 1.7 %collective-permute-start.13 = (f32[8,128]{1,0:T(8,128)S(1)}, f32[8,128]{1,0:T(8,128)S(1)}, u32[]{:S(2)}, u32[]{:S(2)}) collective-permute-start(f32[8,128]{1,0:T(8,128)S(1)} %get-tuple-element.69.curve_refs_0_), channel_id=1, source_target_pairs={{0,1},{1,0},{2,3},{3,2},{4,5},{5,4},{6,7},{7,6},{8,9},{9,8},{10,11... | collective-permute-start | bytes 12296 | tf_op jit(solution)/shard_map/even_terms/ppermute | solution.py:326
  45.8 1.6 %odd_terms.1 = (f32[128,128]{1,0:T(8,128)S(1)}, f32[128,128]{1,0:T(8,128)S(1)}) custom-call(s32[2,24]{1,0:T(2,128)S(1)} %get-tuple-element.47.source_ref, bf16[24,2,128,256]{3,2,1,0:T(8,128)(2,1)S(1)} %get-tuple-element.49.pairs_ref, bf16[6144,256]{1,0:T(8,128)(2,1)S(1)} %get-tuple-element.50.weights_ref, bf16[9,256,256]{2,1,0:T(8,128)(2,1)S(1)} %get-tuple-element.65.slots, ...), custom_call_target="tpu_custom_call" | custom-call | flops 603979776 | bytes 1048576 | tf_op jit(solution)/shard_map/odd_terms/pallas_call | solution.py:424
  47.5 1.1 %collective-permute-done.14.curve_refs_2_ = f32[8,128]{1,0:T(8,128)S(1)} collective-permute-done((f32[8,128]{1,0:T(8,128)S(1)}, f32[8,128]{1,0:T(8,128)S(1)}, u32[]{:S(2)}, u32[]{:S(2)}) %collective-permute-start.14) | collective-permute-done | bytes 4128 | tf_op jit(solution)/shard_map/even_terms/ppermute | solution.py:326
  48.7 1.2 %collective-permute-done.16.got_ref = f32[136,128]{1,0:T(8,128)S(1)} collective-permute-done((f32[136,128]{1,0:T(8,128)S(1)}, f32[136,128]{1,0:T(8,128)S(1)}, u32[]{:S(2)}, u32[]{:S(2)}) %collective-permute-start.16) | collective-permute-done | bytes 69664 | tf_op jit(solution)/shard_map/reduce_dir_sigma/ppermute | solution.py:320
  50.0 1.6 %collective-permute-start.17 = (f32[40,128]{1,0:T(8,128)S(1)}, f32[40,128]{1,0:T(8,128)S(1)}, u32[]{:S(2)}, u32[]{:S(2)}) collective-permute-start(f32[40,128]{1,0:T(8,128)S(1)} %get-tuple-element.73), channel_id=1, source_target_pairs={{0,8},{4,12},{8,0},{12,4},{16,24},{20,28},{24,16},{28,20},{1,9},{5... | collective-permute-start | bytes 61448 | tf_op jit(solution)/shard_map/reduce_dir_sigma/ppermute | solution.py:323
  51.6 1.9 %collective-permute-start.19 = (f32[40,128]{1,0:T(8,128)S(1)}, f32[40,128]{1,0:T(8,128)S(1)}, u32[]{:S(2)}, u32[]{:S(2)}) collective-permute-start(f32[40,128]{1,0:T(8,128)S(1)} %get-tuple-element.75), channel_id=1, source_target_pairs={{0,24},{4,28},{8,16},{12,20},{16,8},{20,12},{24,0},{28,4},{1,25},{... | collective-permute-start | bytes 61448 | tf_op jit(solution)/shard_map/reduce_dir_sigma/ppermute | solution.py:323
  53.8 1.6 %collective-permute-done.18.got_refs_2_ = f32[40,128]{1,0:T(8,128)S(1)} collective-permute-done((f32[40,128]{1,0:T(8,128)S(1)}, f32[40,128]{1,0:T(8,128)S(1)}, u32[]{:S(2)}, u32[]{:S(2)}) %collective-permute-start.18) | collective-permute-done | bytes 20512 | tf_op jit(solution)/shard_map/reduce_dir_sigma/ppermute | solution.py:323
  55.4 0.9 %collective-permute-done.19.got_refs_3_ = f32[40,128]{1,0:T(8,128)S(1)} collective-permute-done((f32[40,128]{1,0:T(8,128)S(1)}, f32[40,128]{1,0:T(8,128)S(1)}, u32[]{:S(2)}, u32[]{:S(2)}) %collective-permute-start.19) | collective-permute-done | bytes 20512 | tf_op jit(solution)/shard_map/reduce_dir_sigma/ppermute | solution.py:323
  56.3 0.7 %ritz.1 = (f32[2,16,128]{2,1,0:T(8,128)}, f32[2,16,128]{2,1,0:T(8,128)}, f32[1,128]{1,0:T(1,128)}) custom-call(f32[8,128]{1,0:T(8,128)S(1)} %get-tuple-element.63.scalar_ref, f32[2,128,128]{2,1,0:T(8,128)S(1)} %get-tuple-element.51.local_ref, f32[4,16,128]{2,1,0:T(8,128)S(1)} %get-tuple-element.64.own_ref, f32[40,128]{1,0:T(8,128)S(1)} %get-tuple-element.72.got_refs_0_, ...), custom_call_target="tpu_custom_call" | custom-call | bytes 1048576 | tf_op jit(solution)/shard_map/ritz/pallas_call | solution.py:438
  (19 shorter events, 0.9 us)
Async XLA Ops:
  1.7 9.0 %collective-permute-start.1 = (f32[160,128]{1,0:T(8,128)S(1)}, f32[160,128]{1,0:T(8,128)S(1)}, u32[]{:S(2)}, u32[]{:S(2)}) collective-permute-start(f32[160,128]{1,0:T(8,128)S(1)} %get-tuple-element.46), channel_id=1, source_target_pairs={{0,3},{1,2},{2,1},{3,0},{4,7},{5,6},{6,5},{7,4},{8,11},{9,10},{10,... | collective-permute-start | bytes 245768 | tf_op jit(solution)/shard_map/gather_wave/ppermute | solution.py:326
  6.8 7.0 %collective-permute-start = (f32[160,128]{1,0:T(8,128)S(1)}, f32[160,128]{1,0:T(8,128)S(1)}, u32[]{:S(2)}, u32[]{:S(2)}) collective-permute-start(f32[160,128]{1,0:T(8,128)S(1)} %get-tuple-element.46), channel_id=1, source_target_pairs={{0,2},{1,3},{2,0},{3,1},{4,6},{5,7},{6,4},{7,5},{8,10},{9,11},{10,... | collective-permute-start | bytes 245768 | tf_op jit(solution)/shard_map/gather_wave/ppermute | solution.py:326
  6.8 7.5 %collective-permute-start.2 = (f32[288,128]{1,0:T(8,128)S(1)}, f32[288,128]{1,0:T(8,128)S(1)}, u32[]{:S(2)}, u32[]{:S(2)}) collective-permute-start(f32[288,128]{1,0:T(8,128)S(1)} %get-tuple-element.52.whole_ref), channel_id=1, source_target_pairs={{0,1},{1,0},{2,3},{3,2},{4,5},{5,4},{6,7},{7,6},{8,9},{9,8},{10,11... | collective-permute-start | bytes 442376 | tf_op jit(solution)/shard_map/gather_wave/ppermute | solution.py:326
  13.8 1.3 %collective-permute-start.3 = (f32[160,128]{1,0:T(8,128)S(1)}, f32[160,128]{1,0:T(8,128)S(1)}, u32[]{:S(2)}, u32[]{:S(2)}) collective-permute-start(f32[160,128]{1,0:T(8,128)S(1)} %collective-permute-done.mine_refs_0_.packed_refs_1_), channel_id=1, source_target_pairs={{0,4},{4,0},{8,12},{12,8},{16,20},{20,16},{24,28},{28,24},{1,5},{5... | collective-permute-start | bytes 245768 | tf_op jit(solution)/shard_map/swap_wave/ppermute | solution.py:320
  13.8 1.4 %collective-permute-start.4 = (f32[160,128]{1,0:T(8,128)S(1)}, f32[160,128]{1,0:T(8,128)S(1)}, u32[]{:S(2)}, u32[]{:S(2)}) collective-permute-start(f32[160,128]{1,0:T(8,128)S(1)} %collective-permute-done.1.mine_refs_1_.packed_refs_2_), channel_id=1, source_target_pairs={{0,4},{4,0},{8,12},{12,8},{16,20},{20,16},{24,28},{28,24},{1,5},{5... | collective-permute-start | bytes 245768 | tf_op jit(solution)/shard_map/swap_wave/ppermute | solution.py:320
  18.0 1.3 %collective-permute-start.5 = (f32[136,128]{1,0:T(8,128)S(1)}, f32[136,128]{1,0:T(8,128)S(1)}, u32[]{:S(2)}, u32[]{:S(2)}) collective-permute-start(f32[136,128]{1,0:T(8,128)S(1)} %get-tuple-element.57), channel_id=1, source_target_pairs={{0,4},{4,0},{8,12},{12,8},{16,20},{20,16},{24,28},{28,24},{1,5},{5... | collective-permute-start | bytes 208904 | tf_op jit(solution)/shard_map/reduce_sigma/ppermute | solution.py:320
  19.4 6.6 %collective-permute-start.8 = (f32[232,128]{1,0:T(8,128)S(1)}, f32[232,128]{1,0:T(8,128)S(1)}, u32[]{:S(2)}, u32[]{:S(2)}) collective-permute-start(f32[232,128]{1,0:T(8,128)S(1)} %reduce_sigma.2.part_refs_0_), channel_id=1, source_target_pairs={{0,24},{4,28},{8,16},{12,20},{16,8},{20,12},{24,0},{28,4},{1,25},{... | collective-permute-start | bytes 356360 | tf_op jit(solution)/shard_map/reduce_sigma/ppermute | solution.py:323
  21.9 6.5 %collective-permute-start.7 = (f32[232,128]{1,0:T(8,128)S(1)}, f32[232,128]{1,0:T(8,128)S(1)}, u32[]{:S(2)}, u32[]{:S(2)}) collective-permute-start(f32[232,128]{1,0:T(8,128)S(1)} %reduce_sigma.2.part_refs_0_), channel_id=1, source_target_pairs={{0,16},{4,20},{8,24},{12,28},{16,0},{20,4},{24,8},{28,12},{1,17},{... | collective-permute-start | bytes 356360 | tf_op jit(solution)/shard_map/reduce_sigma/ppermute | solution.py:323
  22.4 6.1 %collective-permute-start.6 = (f32[232,128]{1,0:T(8,128)S(1)}, f32[232,128]{1,0:T(8,128)S(1)}, u32[]{:S(2)}, u32[]{:S(2)}) collective-permute-start(f32[232,128]{1,0:T(8,128)S(1)} %reduce_sigma.2.part_refs_0_), channel_id=1, source_target_pairs={{0,8},{4,12},{8,0},{12,4},{16,24},{20,28},{24,16},{28,20},{1,9},{5... | collective-permute-start | bytes 356360 | tf_op jit(solution)/shard_map/reduce_sigma/ppermute | solution.py:323
  28.5 6.8 %collective-permute-start.11 = (f32[136,128]{1,0:T(8,128)S(1)}, f32[136,128]{1,0:T(8,128)S(1)}, u32[]{:S(2)}, u32[]{:S(2)}) collective-permute-start(f32[136,128]{1,0:T(8,128)S(1)} %get-tuple-element.58.sum_refs_0_), channel_id=1, source_target_pairs={{0,3},{1,2},{2,1},{3,0},{4,7},{5,6},{6,5},{7,4},{8,11},{9,10},{10,... | collective-permute-start | bytes 208904 | tf_op jit(solution)/shard_map/gather_sigma/ppermute | solution.py:326
  31.2 6.2 %collective-permute-start.10 = (f32[136,128]{1,0:T(8,128)S(1)}, f32[136,128]{1,0:T(8,128)S(1)}, u32[]{:S(2)}, u32[]{:S(2)}) collective-permute-start(f32[136,128]{1,0:T(8,128)S(1)} %get-tuple-element.58.sum_refs_0_), channel_id=1, source_target_pairs={{0,2},{1,3},{2,0},{3,1},{4,6},{5,7},{6,4},{7,5},{8,10},{9,11},{10,... | collective-permute-start | bytes 208904 | tf_op jit(solution)/shard_map/gather_sigma/ppermute | solution.py:326
  31.2 6.2 %collective-permute-start.9 = (f32[136,128]{1,0:T(8,128)S(1)}, f32[136,128]{1,0:T(8,128)S(1)}, u32[]{:S(2)}, u32[]{:S(2)}) collective-permute-start(f32[136,128]{1,0:T(8,128)S(1)} %get-tuple-element.58.sum_refs_0_), channel_id=1, source_target_pairs={{0,1},{1,0},{2,3},{3,2},{4,5},{5,4},{6,7},{7,6},{8,9},{9,8},{10,11... | collective-permute-start | bytes 208904 | tf_op jit(solution)/shard_map/gather_sigma/ppermute | solution.py:326
  37.8 1.7 %collective-permute-start.12 = (f32[648,128]{1,0:T(8,128)S(1)}, f32[648,128]{1,0:T(8,128)S(1)}, u32[]{:S(2)}, u32[]{:S(2)}) collective-permute-start(f32[648,128]{1,0:T(8,128)S(1)} %correction.1.mine_ref), channel_id=1, source_target_pairs={{0,4},{4,0},{8,12},{12,8},{16,20},{20,16},{24,28},{28,24},{1,5},{5... | collective-permute-start | bytes 995336 | tf_op jit(solution)/shard_map/correction/ppermute | solution.py:320
  41.4 6.1 %collective-permute-start.15 = (f32[8,128]{1,0:T(8,128)S(1)}, f32[8,128]{1,0:T(8,128)S(1)}, u32[]{:S(2)}, u32[]{:S(2)}) collective-permute-start(f32[8,128]{1,0:T(8,128)S(1)} %get-tuple-element.69.curve_refs_0_), channel_id=1, source_target_pairs={{0,3},{1,2},{2,1},{3,0},{4,7},{5,6},{6,5},{7,4},{8,11},{9,10},{10,... | collective-permute-start | bytes 12296 | tf_op jit(solution)/shard_map/even_terms/ppermute | solution.py:326
  44.1 4.5 %collective-permute-start.14 = (f32[8,128]{1,0:T(8,128)S(1)}, f32[8,128]{1,0:T(8,128)S(1)}, u32[]{:S(2)}, u32[]{:S(2)}) collective-permute-start(f32[8,128]{1,0:T(8,128)S(1)} %get-tuple-element.69.curve_refs_0_), channel_id=1, source_target_pairs={{0,2},{1,3},{2,0},{3,1},{4,6},{5,7},{6,4},{7,5},{8,10},{9,11},{10,... | collective-permute-start | bytes 12296 | tf_op jit(solution)/shard_map/even_terms/ppermute | solution.py:326
  44.1 4.5 %collective-permute-start.13 = (f32[8,128]{1,0:T(8,128)S(1)}, f32[8,128]{1,0:T(8,128)S(1)}, u32[]{:S(2)}, u32[]{:S(2)}) collective-permute-start(f32[8,128]{1,0:T(8,128)S(1)} %get-tuple-element.69.curve_refs_0_), channel_id=1, source_target_pairs={{0,1},{1,0},{2,3},{3,2},{4,5},{5,4},{6,7},{7,6},{8,9},{9,8},{10,11... | collective-permute-start | bytes 12296 | tf_op jit(solution)/shard_map/even_terms/ppermute | solution.py:326
  48.6 1.3 %collective-permute-start.16 = (f32[136,128]{1,0:T(8,128)S(1)}, f32[136,128]{1,0:T(8,128)S(1)}, u32[]{:S(2)}, u32[]{:S(2)}) collective-permute-start(f32[136,128]{1,0:T(8,128)S(1)} %get-tuple-element.71), channel_id=1, source_target_pairs={{0,4},{4,0},{8,12},{12,8},{16,20},{20,16},{24,28},{28,24},{1,5},{5... | collective-permute-start | bytes 208904 | tf_op jit(solution)/shard_map/reduce_dir_sigma/ppermute | solution.py:320
  50.0 3.8 %collective-permute-start.17 = (f32[40,128]{1,0:T(8,128)S(1)}, f32[40,128]{1,0:T(8,128)S(1)}, u32[]{:S(2)}, u32[]{:S(2)}) collective-permute-start(f32[40,128]{1,0:T(8,128)S(1)} %get-tuple-element.73), channel_id=1, source_target_pairs={{0,8},{4,12},{8,0},{12,4},{16,24},{20,28},{24,16},{28,20},{1,9},{5... | collective-permute-start | bytes 61448 | tf_op jit(solution)/shard_map/reduce_dir_sigma/ppermute | solution.py:323
  51.5 3.9 %collective-permute-start.18 = (f32[40,128]{1,0:T(8,128)S(1)}, f32[40,128]{1,0:T(8,128)S(1)}, u32[]{:S(2)}, u32[]{:S(2)}) collective-permute-start(f32[40,128]{1,0:T(8,128)S(1)} %get-tuple-element.74), channel_id=1, source_target_pairs={{0,16},{4,20},{8,24},{12,28},{16,0},{20,4},{24,8},{28,12},{1,17},{... | collective-permute-start | bytes 61448 | tf_op jit(solution)/shard_map/reduce_dir_sigma/ppermute | solution.py:323
  51.6 4.7 %collective-permute-start.19 = (f32[40,128]{1,0:T(8,128)S(1)}, f32[40,128]{1,0:T(8,128)S(1)}, u32[]{:S(2)}, u32[]{:S(2)}) collective-permute-start(f32[40,128]{1,0:T(8,128)S(1)} %get-tuple-element.75), channel_id=1, source_target_pairs={{0,24},{4,28},{8,16},{12,20},{16,8},{20,12},{24,0},{28,4},{1,25},{... | collective-permute-start | bytes 61448 | tf_op jit(solution)/shard_map/reduce_dir_sigma/ppermute | solution.py:323

commit v4 on v3

--- a/solution.py
+++ b/solution.py
@@ -67,8 +67,8 @@
         weights_ref[base + size : base + 2 * size, size:] = jnp.zeros_like(high)
 
 
-def pack_kernel(wave_ref, diag_ref, packed_ref, near_ref, own_diag_ref, sems):
-    owned, size, _ = wave_ref.shape
+def pack_kernel(wave_ref, diag_ref, packed_ref, own_diag_ref, sems):
+    size = wave_ref.shape[1]
     share = packed_ref.shape[0] - size
     ops = lax.axis_index("ops")
     core, chip = ops % 2, ops // 2
@@ -76,8 +76,6 @@
     moves = [
         (wave_ref.at[core], packed_ref.at[pl.ds(0, size)]),
         (diag_ref.at[core, rows], packed_ref.at[pl.ds(size, share)]),
-        *((wave_ref.at[s], near_ref.at[pl.ds(s * size, size)]) for s in range(owned)),
-        (diag_ref.at[core, rows], near_ref.at[pl.ds(owned * size, share)]),
         (diag_ref.at[core], own_diag_ref),
     ]
     copies = [pltpu.make_async_copy(source, target, sems.at[i]) for i, (source, target) in enumerate(moves)]
@@ -85,6 +83,21 @@
         copy.start()
     for copy in copies:
         copy.wait()
+
+
+def other_kernel(source_ref, target_ref):
+    target_ref[...] = source_ref[1 - lax.axis_index("ops") % 2]
+
+
+def partners(n_sec):
+    return [(m, m + 1) for m in range(1, n_sec - 1, 2)], n_sec - 1
+
+
+def from_partner(n_sec, m, core, mine, theirs, last):
+    for i, pair in enumerate(partners(n_sec)[0]):
+        if m in pair:
+            return jnp.where(core == pair.index(m), mine(i), theirs(i))
+    return last()
 
 
 def store_vector(slots, at, block):
@@ -114,53 +127,49 @@
     return both[:, :size] + both[:, size:]
 
 
-def join_kernel(keep_ref, got_ref, packed_refs, out_ref):
-    rows = keep_ref.shape[0]
+def join_kernel(keep_ref, got_ref, last_ref, out_ref):
+    rows, size = keep_ref.shape
     out_ref[:rows] = keep_ref[...] + got_ref[...]
-    share = (out_ref.shape[0] - rows) // max(len(packed_refs), 1)
-    for i, ref in enumerate(packed_refs):
-        out_ref[rows + i * share : rows + (i + 1) * share] = ref[ref.shape[0] - share :]
-
-
-def plane_kernel(part_refs, sum_ref, *diag_refs):
+    out_ref[rows:] = last_ref[size:]
+
+
+def plane_kernel(part_refs, sum_ref, diag_ref):
     rows = sum_ref.shape[0]
-    size = rows - PAD
     summed = part_refs[0][:rows]
     for ref in part_refs[1:]:
         summed += ref[:rows]
     sum_ref[...] = summed
     chip = lax.axis_index("ops") // 2
-    share = size // len(part_refs)
+    share = diag_ref.shape[0] // len(part_refs)
     for m, ref in enumerate(part_refs):
         first = pl.multiple_of(jnp.bitwise_xor(chip, m) * share, share)
-        for i, diag_ref in enumerate(diag_refs):
-            diag_ref[pl.ds(first, share)] = ref[rows + i * share : rows + (i + 1) * share]
-
-
-def first_kernel(n_sec, n_ops, source_ref, coupling_ref, pairs_ref, weights_ref, local_ref, near_ref, mine_refs, theirs_refs,
-                 keep_ref, send_ref, norm_ref, slots, stacked):
+        diag_ref[pl.ds(first, share)] = ref[rows:]
+
+
+def first_kernel(n_sec, n_ops, source_ref, coupling_ref, pairs_ref, weights_ref, local_ref, mine_refs, theirs_refs,
+                 last_ref, other_last_ref, keep_ref, send_ref, norm_ref, slots, stacked):
     size = local_ref.shape[1]
     core = lax.axis_index("ops") % 2
+    pairs, last = partners(n_sec)
+    blocks = [(s, local_ref[s]) for s in range(2)]
+    for i, (even, odd) in enumerate(pairs):
+        for refs, m in ((mine_refs, jnp.where(core == 0, even, odd)), (theirs_refs, jnp.where(core == 0, odd, even))):
+            blocks += [(2 * m + s, refs[i][s]) for s in range(2)]
+    blocks += [(2 * last + core, last_ref[:size]), (2 * last + 1 - core, other_last_ref[:size])]
     acc = jnp.zeros((size, size), F32)
-    for m in range(n_sec):
-        for s in range(2):
-            if m < 2:
-                at, block = 2 * m + s, (local_ref[s], near_ref[s * size : (s + 1) * size])[m]
-            else:
-                at, block = 2 * m + (core if s == 0 else 1 - core), (mine_refs, theirs_refs)[s][m - 2][:size]
-            acc += block * block
-            store_vector(slots, at, block)
+    for at, block in blocks:
+        acc += block * block
+        store_vector(slots, at, block)
     slots[2 * n_sec] = jnp.zeros_like(slots[2 * n_sec])
     norm_ref[...] = jnp.broadcast_to(total(acc), norm_ref.shape)
     part = apply_terms(range(pairs_ref.shape[0]), n_sec, source_ref, pairs_ref, weights_ref, slots, stacked)
     corr = jnp.zeros((1, 1), F32)
-    mirror = n_sec // 2
     blocks = []
     for s in range(2):
-        if mirror < 2:
-            partner = near_ref[s * size : (s + 1) * size]
-        else:
-            partner = jnp.where(core == s, mine_refs[mirror - 2][:size], theirs_refs[mirror - 2][:size])
+        partner = from_partner(
+            n_sec, n_sec // 2, core, lambda i: mine_refs[i][s], lambda i: theirs_refs[i][s],
+            lambda: jnp.where(core == s, last_ref[:size], other_last_ref[:size]),
+        )
         blocks.append(part[s * size : (s + 1) * size] + (coupling_ref[0, s] / n_ops) * partner.T)
         corr += total(local_ref[s] * blocks[s])
     keep_ref[:size] = jnp.where(core == 0, blocks[0], blocks[1])
@@ -169,8 +178,8 @@
     send_ref[size:] = jnp.broadcast_to(corr, (PAD, size))
 
 
-def correction_kernel(n_sec, norm_ref, whole_ref, near_ref, mine_refs, sum_refs, diag_refs, out_ref):
-    size = whole_ref.shape[1]
+def correction_kernel(n_sec, norm_ref, sector_refs, mine_refs, theirs_refs, last_refs, diag_refs, other_diag_refs, sum_refs, out_ref):
+    size = sector_refs[1].shape[0]
     core = lax.axis_index("ops") % 2
     norm_sq = norm_ref[:1, :1]
     corr = sum_refs[0][size : size + 1, :1]
@@ -181,14 +190,18 @@
     rayleigh = corr / norm_sq
     sums = [jnp.zeros((size, size), F32) for _ in range(5)]
     for m in range(n_sec):
-        if m < 2:
-            ref = (whole_ref, near_ref)[m]
-            wave = ref[pl.ds(pl.multiple_of(core * size, size), size)]
+        if m == 0:
+            wave, diag = sector_refs[0][:size], sector_refs[1][...]
         else:
-            wave = mine_refs[m - 2][:size]
+            wave = from_partner(
+                n_sec, m, core, lambda i: mine_refs[i][core], lambda i: theirs_refs[i][core], lambda: last_refs[0][:size]
+            )
+            diag = from_partner(
+                n_sec, m, core, lambda i: diag_refs[i][core], lambda i: other_diag_refs[i][...], lambda: last_refs[1][...]
+            )
         sigma = sum_refs[m][:size]
         resid = sigma * inverse - rayleigh * (wave * inverse)
-        offset = diag_refs[m][...] - rayleigh
+        offset = diag - rayleigh
         corrected = resid / (1.0 + offset * offset)
         out_ref[m * size : (m + 1) * size] = corrected
         for i, factor in enumerate((wave, corrected, resid, sigma)):
@@ -325,6 +338,10 @@
     def to_plane(values, m):
         return lax.ppermute(values, "sec", [(i, i ^ m) for i in range(n_sec)])
 
+    def to_planes(values, pair):
+        moves = [(o * n_sec + z, o * n_sec + (z ^ pair[o % 2])) for o in range(n_ops) for z in range(n_sec)]
+        return lax.ppermute(values, ("ops", "sec"), moves)
+
     def gather_planes(values):
         return [values] + [to_plane(values, m) for m in range(1, n_sec)]
 
@@ -338,20 +355,20 @@
     def in_hbm(values):
         return pltpu.with_memory_space_constraint(values, pltpu.HBM)
 
+    zs, last = partners(n_sec)
+
     with jax.named_scope("gather_wave"):
-        packed, whole, own_diag = call(
+        mine = [to_planes(wavefunction, pair) for pair in zs]
+        sectors = call(
             pack_kernel,
-            (
-                shape((size + size // chips, size), F32),
-                shape((owned * size + size // chips, size), F32),
-                shape((size, size), F32),
-            ),
+            (shape((size + size // chips, size), F32), shape((size, size), F32)),
             [HBM] * 2,
-            [pltpu.SemaphoreType.DMA((owned + 4,))],
+            [pltpu.SemaphoreType.DMA((3,))],
             limit=SMALL,
         )(in_hbm(wavefunction), in_hbm(hamiltonian_diag))
-        mine = [to_plane(packed, m) for m in range(2, n_sec)]
-        near = to_plane(whole, 1)
+        mine.append(to_plane(sectors[0], last))
+    with jax.named_scope("gather_diag"):
+        diag = [to_planes(hamiltonian_diag, pair) for pair in zs]
     with jax.named_scope("load"):
         held = [left_env, right_env, wavefunction, term_source.T, mirror_coupling[None]]
         loaded = call(
@@ -373,37 +390,35 @@
         pairs, weights, local, source, coupling = loaded
     with jax.named_scope("swap_wave"):
         theirs = [swap(values) for values in mine]
+        (*mine, last), (*theirs, other_last) = mine, theirs
     with jax.named_scope("first_apply"):
         keep, send, norm = call(
             functools.partial(first_kernel, n_sec, n_ops),
             (message_shape, message_shape, scalar_shape),
-            [SMEM, SMEM] + [VMEM] * 4 + [[VMEM] * (n_sec - 2)] * 2,
+            [SMEM, SMEM] + [VMEM] * 3 + [[VMEM] * len(zs)] * 2 + [VMEM] * 2,
             [pltpu.VMEM(slot_shape, BF16), pltpu.VMEM(stack_shape, BF16)],
             matmul_flops,
-        )(source, coupling, pairs, weights, local, near, mine, theirs)
+        )(source, coupling, pairs, weights, local, mine, theirs, last, other_last)
     with jax.named_scope("reduce_sigma"):
-        share = size // chips
         joined = call(
-            join_kernel,
-            shape((size + PAD + (n_sec - 1) * share, size), F32),
-            [VMEM, VMEM, [VMEM] * (n_sec - 1)],
-            limit=SMALL,
-        )(keep, swap(send), [near] + mine)
-        summed, *diag = call(
-            plane_kernel,
-            (message_shape, *[shape((size, size), F32)] * (n_sec - 1)),
-            [[VMEM] * chips],
-            limit=SMALL,
+            join_kernel, shape((size + PAD + size // chips, size), F32), [VMEM] * 3, limit=SMALL
+        )(keep, swap(send), last)
+        summed, last_diag = call(
+            plane_kernel, (message_shape, shape((size, size), F32)), [[VMEM] * chips], limit=SMALL
         )([joined] + [to_chip(joined, m) for m in range(1, chips)])
+    with jax.named_scope("swap_diag"):
+        other_diag = [
+            swap(call(other_kernel, shape((size, size), F32), [VMEM], limit=SMALL)(values)) for values in diag
+        ]
     with jax.named_scope("gather_sigma"):
         sums = gather_planes(summed)
     with jax.named_scope("correction"):
         found = call(
             functools.partial(correction_kernel, n_sec),
             shape(((n_sec + 1) * size + PAD, size), F32),
-            [VMEM] * 3 + [[VMEM] * (n_sec - 2), [VMEM] * n_sec, [VMEM] * n_sec],
+            [VMEM, [VMEM] * 2, [VMEM] * len(zs), [VMEM] * len(zs), [VMEM] * 2, [VMEM] * len(zs), [VMEM] * len(zs), [VMEM] * n_sec],
             limit=SMALL,
-        )(norm, whole, near, mine, sums, [own_diag] + diag)
+        )(norm, list(sectors), mine, theirs, [last, last_diag], diag, other_diag, sums)
         other = swap(found)
     with jax.named_scope("even_terms"):
         slots, part, curve, kept, scalars = call(

time: 57.2 us -> 54.2 us (0.948)
  waiting for transfers between devices: 21.6 us -> 17.5 us
  starting transfers between devices: 22.9 us -> 24.1 us
    ppermute x0 -> x2, starting transfers between devices: none -> 4.43 us  [to_planes(): return lax.ppermute(values, ('ops', 'sec'), moves)]
    ppermute x9 -> x7, waiting for transfers between devices: 8.62 us -> 4.66 us  [to_plane(): return lax.ppermute(values, 'sec', [(i, i ^ m) for i in range(n_sec)])]
    ppermute x9 -> x7, starting transfers between devices: 14.7 us -> 11.4 us  [to_plane(): return lax.ppermute(values, 'sec', [(i, i ^ m) for i in range(n_sec)])]
    ppermute x5 -> x6, waiting for transfers between devices: 4.69 us -> 5.07 us  [swap(): return lax.ppermute(values, 'ops', [(i, i ^ 1) for i in range(n_ops)])]
  transfers between devices with their start and end apart: 20 -> 21, of which waited for: 15 -> 14; matrix products, arithmetic and copies ran while one was open for 0% -> 0% of each run, Pallas kernels for 9% -> 11%
where the time goes in v4:
time: 54.2 us; the launch traced here: 54 us
  starting transfers between devices  24.1 us (44%)
  waiting for transfers between devices  17.5 us (32%)
  Pallas kernels  11.7 us (22%)
  between operations  0.74 us (1%)
    ppermute x7, starting transfers between devices, to_plane(): return lax.ppermute(values, 'sec', [(i, i ^ m) for i in range(n_sec)])  11.4 us
    ppermute x6, waiting for transfers between devices, to_chip(): return lax.ppermute(values, 'ops', [(i, i ^ 2 * m) for i in range(n_ops)])  7.78 us
    ppermute x6, starting transfers between devices, to_chip(): return lax.ppermute(values, 'ops', [(i, i ^ 2 * m) for i in range(n_ops)])  7.11 us
    ppermute x6, waiting for transfers between devices, swap(): return lax.ppermute(values, 'ops', [(i, i ^ 1) for i in range(n_ops)])  5.07 us
    ppermute x7, waiting for transfers between devices, to_plane(): return lax.ppermute(values, 'sec', [(i, i ^ m) for i in range(n_sec)])  4.66 us
    ppermute x2, starting transfers between devices, to_planes(): return lax.ppermute(values, ('ops', 'sec'), moves)  4.43 us
    pallas_call x1, Pallas kernels, body(): call(load_kernel, (shape((terms, owned, size, 2 * size), BF16), shape((2...  3.28 us
    pallas_call x1, Pallas kernels, body(): call(functools.partial(first_kernel, n_sec, n_ops), (message_shape, messa...  2.83 us
  transfers between devices with their start and end apart: 21, of which 14 were waited for; matrix products, arithmetic and copies ran while one was open for 0% of the time, Pallas kernels for 11%

profile of v4, /device:TPU:0, one launch (start us, length us, event | category | flops | bytes accessed | tf_op | source)
XLA Modules:
  0.0 54.0 jit_solution(1722937364833339006)
XLA Ops:
  0.6 3.1 %collective-permute-start = (f32[2,128,128]{2,1,0:T(8,128)}, f32[2,128,128]{2,1,0:T(8,128)S(1)}, u32[]{:S(2)}, u32[]{:S(2)}) collective-permute-start(f32[2,128,128]{2,1,0:T(8,128)} %wave_ref.3), channel_id=1, source_target_pairs={{0,1},{1,0},{2,3},{3,2},{4,6},{5,7},{6,4},{7,5},{8,9},{9,8},{10,11... | collective-permute-start | bytes 393224 | tf_op jit(solution)/shard_map/gather_wave/ppermute | solution.py:343
  3.7 0.9 %gather_wave.1 = (f32[160,128]{1,0:T(8,128)S(1)}, f32[128,128]{1,0:T(8,128)S(1)}) custom-call(f32[2,128,128]{2,1,0:T(8,128)} %wave_ref.3, f32[2,128,128]{2,1,0:T(8,128)} %diag_ref.1), custom_call_target="tpu_custom_call" | custom-call | bytes 1048576 | tf_op jit(solution)/shard_map/gather_wave/pallas_call | solution.py:362
  4.7 2.5 %collective-permute-start.1 = (f32[160,128]{1,0:T(8,128)S(1)}, f32[160,128]{1,0:T(8,128)S(1)}, u32[]{:S(2)}, u32[]{:S(2)}) collective-permute-start(f32[160,128]{1,0:T(8,128)S(1)} %get-tuple-element.43.sector_refs_0_), channel_id=1, source_target_pairs={{0,3},{1,2},{2,1},{3,0},{4,7},{5,6},{6,5},{7,4},{8,11},{9,10},{10,... | collective-permute-start | bytes 245768 | tf_op jit(solution)/shard_map/gather_wave/ppermute | solution.py:339
  7.2 3.3 %load.1 = (bf16[24,2,128,256]{3,2,1,0:T(8,128)(2,1)S(1)}, bf16[6144,256]{1,0:T(8,128)(2,1)S(1)}, f32[2,128,128]{2,1,0:T(8,128)S(1)}, s32[2,24]{1,0:T(2,128)S(1)}, f32[1,2]{1,0:T(1,128)S(1)}) custom-call(f32[24,2,128,128]{3,2,1,0:T(8,128)} %left_ref.1, f32[24,128,128]{2,1,0:T(8,128)} %right_ref.1, f32[2,128,128]{2,1,0:T(8,128)} %wave_ref.3, s32[2,24]{1,0:T(2,128)} %bitcast.4, ...), custom_call_target="tpu_custom_call" | custom-call | bytes 1048576 | tf_op jit(solution)/shard_map/load/pallas_call | solution.py:374
  10.5 1.1 %collective-permute-done.1.last_ref.last_refs_0_ = f32[160,128]{1,0:T(8,128)S(1)} collective-permute-done((f32[160,128]{1,0:T(8,128)S(1)}, f32[160,128]{1,0:T(8,128)S(1)}, u32[]{:S(2)}, u32[]{:S(2)}) %collective-permute-start.1) | collective-permute-done | bytes 81952 | tf_op jit(solution)/shard_map/gather_wave/ppermute | solution.py:339
  11.6 0.5 collective-permute-start.3
  12.1 1.0 %collective-permute-done.3.other_last_ref = f32[160,128]{1,0:T(8,128)S(1)} collective-permute-done((f32[160,128]{1,0:T(8,128)S(1)}, f32[160,128]{1,0:T(8,128)S(1)}, u32[]{:S(2)}, u32[]{:S(2)}) %collective-permute-start.3) | collective-permute-done | bytes 81952 | tf_op jit(solution)/shard_map/swap_wave/ppermute | solution.py:333
  13.0 2.8 %first_apply.1 = (f32[136,128]{1,0:T(8,128)S(1)}, f32[136,128]{1,0:T(8,128)S(1)}, f32[8,128]{1,0:T(8,128)S(1)}) custom-call(s32[2,24]{1,0:T(2,128)S(1)} %get-tuple-element.44.source_ref, f32[1,2]{1,0:T(1,128)S(1)} %get-tuple-element.45.coupling_ref, bf16[24,2,128,256]{3,2,1,0:T(8,128)(2,1)S(1)} %get-tuple-element.46.pairs_ref, ...), custom_call_target="tpu_custom_call" | custom-call | flops 1207959552 | bytes 1048576 | tf_op jit(solution)/shard_map/first_apply/pallas_call | solution.py:395
  16.2 1.3 %collective-permute-start.8 = (f32[2,128,128]{2,1,0:T(8,128)S(1)}, f32[2,128,128]{2,1,0:T(8,128)S(1)}, u32[]{:S(2)}, u32[]{:S(2)}) collective-permute-start(f32[2,128,128]{2,1,0:T(8,128)S(1)} %copy-done), channel_id=1, source_target_pairs={{0,1},{1,0},{2,3},{3,2},{4,6},{5,7},{6,4},{7,5},{8,9},{9,8},{10,11... | collective-permute-start | bytes 393224 | tf_op jit(solution)/shard_map/gather_diag/ppermute | solution.py:343
  17.6 2.5 %collective-permute-start.7 = (f32[168,128]{1,0:T(8,128)S(1)}, f32[168,128]{1,0:T(8,128)S(1)}, u32[]{:S(2)}, u32[]{:S(2)}) collective-permute-start(f32[168,128]{1,0:T(8,128)S(1)} %reduce_sigma.2.part_refs_0_), channel_id=1, source_target_pairs={{0,24},{4,28},{8,16},{12,20},{16,8},{20,12},{24,0},{28,4},{1,25},{... | collective-permute-start | bytes 258056 | tf_op jit(solution)/shard_map/reduce_sigma/ppermute | solution.py:336
  20.1 0.5 collective-permute-start.6
  20.6 0.5 collective-permute-start.5
  21.2 2.3 %collective-permute-done.7.part_refs_3_ = f32[168,128]{1,0:T(8,128)S(1)} collective-permute-done((f32[168,128]{1,0:T(8,128)S(1)}, f32[168,128]{1,0:T(8,128)S(1)}, u32[]{:S(2)}, u32[]{:S(2)}) %collective-permute-start.7) | collective-permute-done | bytes 86048 | tf_op jit(solution)/shard_map/reduce_sigma/ppermute | solution.py:336
  23.5 2.3 %collective-permute-done.6.part_refs_2_ = f32[168,128]{1,0:T(8,128)S(1)} collective-permute-done((f32[168,128]{1,0:T(8,128)S(1)}, f32[168,128]{1,0:T(8,128)S(1)}, u32[]{:S(2)}, u32[]{:S(2)}) %collective-permute-start.6) | collective-permute-done | bytes 86048 | tf_op jit(solution)/shard_map/reduce_sigma/ppermute | solution.py:336
  26.0 2.2 %collective-permute-start.12 = (f32[136,128]{1,0:T(8,128)S(1)}, f32[136,128]{1,0:T(8,128)S(1)}, u32[]{:S(2)}, u32[]{:S(2)}) collective-permute-start(f32[136,128]{1,0:T(8,128)S(1)} %get-tuple-element.56.sum_refs_0_), channel_id=1, source_target_pairs={{0,3},{1,2},{2,1},{3,0},{4,7},{5,6},{6,5},{7,4},{8,11},{9,10},{10,... | collective-permute-start | bytes 208904 | tf_op jit(solution)/shard_map/gather_sigma/ppermute | solution.py:339
  28.3 2.2 %collective-permute-start.10 = (f32[136,128]{1,0:T(8,128)S(1)}, f32[136,128]{1,0:T(8,128)S(1)}, u32[]{:S(2)}, u32[]{:S(2)}) collective-permute-start(f32[136,128]{1,0:T(8,128)S(1)} %get-tuple-element.56.sum_refs_0_), channel_id=1, source_target_pairs={{0,1},{1,0},{2,3},{3,2},{4,5},{5,4},{6,7},{7,6},{8,9},{9,8},{10,11... | collective-permute-start | bytes 208904 | tf_op jit(solution)/shard_map/gather_sigma/ppermute | solution.py:339
  30.6 1.2 %collective-permute-done.9.other_diag_refs_0_ = f32[128,128]{1,0:T(8,128)S(1)} collective-permute-done((f32[128,128]{1,0:T(8,128)S(1)}, f32[128,128]{1,0:T(8,128)S(1)}, u32[]{:S(2)}, u32[]{:S(2)}) %collective-permute-start.9) | collective-permute-done | bytes 65568 | tf_op jit(solution)/shard_map/swap_diag/ppermute | solution.py:333
  31.8 1.2 %collective-permute-done.12.sum_refs_3_ = f32[136,128]{1,0:T(8,128)S(1)} collective-permute-done((f32[136,128]{1,0:T(8,128)S(1)}, f32[136,128]{1,0:T(8,128)S(1)}, u32[]{:S(2)}, u32[]{:S(2)}) %collective-permute-start.12) | collective-permute-done | bytes 69664 | tf_op jit(solution)/shard_map/gather_sigma/ppermute | solution.py:339
  33.0 1.8 %collective-permute-done.11.sum_refs_2_ = f32[136,128]{1,0:T(8,128)S(1)} collective-permute-done((f32[136,128]{1,0:T(8,128)S(1)}, f32[136,128]{1,0:T(8,128)S(1)}, u32[]{:S(2)}, u32[]{:S(2)}) %collective-permute-start.11) | collective-permute-done | bytes 69664 | tf_op jit(solution)/shard_map/gather_sigma/ppermute | solution.py:339
  34.8 0.4 correction.1.mine_ref
  35.3 1.6 %collective-permute-done.13.theirs_ref = f32[648,128]{1,0:T(8,128)S(1)} collective-permute-done((f32[648,128]{1,0:T(8,128)S(1)}, f32[648,128]{1,0:T(8,128)S(1)}, u32[]{:S(2)}, u32[]{:S(2)}) %collective-permute-start.13) | collective-permute-done | bytes 331808 | tf_op jit(solution)/shard_map/correction/ppermute | solution.py:333
  36.9 1.9 %even_terms.1 = (bf16[9,256,256]{2,1,0:T(8,128)(2,1)S(1)}, f32[2,128,128]{2,1,0:T(8,128)S(1)}, f32[8,128]{1,0:T(8,128)S(1)}, f32[4,16,128]{2,1,0:T(8,128)S(1)}, f32[8,128]{1,0:T(8,128)S(1)}) custom-call(s32[2,24]{1,0:T(2,128)S(1)} %get-tuple-element.44.source_ref, f32[1,2]{1,0:T(1,128)S(1)} %get-tuple-element.45.coupling_ref, ...), custom_call_target="tpu_custom_call" | custom-call | flops 603979776 | bytes 1048576 | tf_op jit(solution)/shard_map/even_terms/pallas_call | solution.py:424
  38.8 2.2 %collective-permute-start.16 = (f32[8,128]{1,0:T(8,128)S(1)}, f32[8,128]{1,0:T(8,128)S(1)}, u32[]{:S(2)}, u32[]{:S(2)}) collective-permute-start(f32[8,128]{1,0:T(8,128)S(1)} %get-tuple-element.63.curve_refs_0_), channel_id=1, source_target_pairs={{0,3},{1,2},{2,1},{3,0},{4,7},{5,6},{6,5},{7,4},{8,11},{9,10},{10,... | collective-permute-start | bytes 12296 | tf_op jit(solution)/shard_map/even_terms/ppermute | solution.py:339
  41.0 2.3 %collective-permute-start.14 = (f32[8,128]{1,0:T(8,128)S(1)}, f32[8,128]{1,0:T(8,128)S(1)}, u32[]{:S(2)}, u32[]{:S(2)}) collective-permute-start(f32[8,128]{1,0:T(8,128)S(1)} %get-tuple-element.63.curve_refs_0_), channel_id=1, source_target_pairs={{0,1},{1,0},{2,3},{3,2},{4,5},{5,4},{6,7},{7,6},{8,9},{9,8},{10,11... | collective-permute-start | bytes 12296 | tf_op jit(solution)/shard_map/even_terms/ppermute | solution.py:339
  43.2 1.6 %odd_terms.1 = (f32[128,128]{1,0:T(8,128)S(1)}, f32[128,128]{1,0:T(8,128)S(1)}) custom-call(s32[2,24]{1,0:T(2,128)S(1)} %get-tuple-element.44.source_ref, bf16[24,2,128,256]{3,2,1,0:T(8,128)(2,1)S(1)} %get-tuple-element.46.pairs_ref, bf16[6144,256]{1,0:T(8,128)(2,1)S(1)} %get-tuple-element.47.weights_ref, bf16[9,256,256]{2,1,0:T(8,128)(2,1)S(1)} %get-tuple-element.59.slots, ...), custom_call_target="tpu_custom_call" | custom-call | flops 603979776 | bytes 1048576 | tf_op jit(solution)/shard_map/odd_terms/pallas_call | solution.py:439
  44.8 0.6 %collective-permute-done.15.curve_refs_2_ = f32[8,128]{1,0:T(8,128)S(1)} collective-permute-done((f32[8,128]{1,0:T(8,128)S(1)}, f32[8,128]{1,0:T(8,128)S(1)}, u32[]{:S(2)}, u32[]{:S(2)}) %collective-permute-start.15) | collective-permute-done | bytes 4128 | tf_op jit(solution)/shard_map/even_terms/ppermute | solution.py:339
  45.6 1.2 %collective-permute-done.17.got_ref = f32[136,128]{1,0:T(8,128)S(1)} collective-permute-done((f32[136,128]{1,0:T(8,128)S(1)}, f32[136,128]{1,0:T(8,128)S(1)}, u32[]{:S(2)}, u32[]{:S(2)}) %collective-permute-start.17) | collective-permute-done | bytes 69664 | tf_op jit(solution)/shard_map/reduce_dir_sigma/ppermute | solution.py:333
  46.8 1.4 %collective-permute-start.18 = (f32[40,128]{1,0:T(8,128)S(1)}, f32[40,128]{1,0:T(8,128)S(1)}, u32[]{:S(2)}, u32[]{:S(2)}) collective-permute-start(f32[40,128]{1,0:T(8,128)S(1)} %get-tuple-element.67), channel_id=1, source_target_pairs={{0,8},{4,12},{8,0},{12,4},{16,24},{20,28},{24,16},{28,20},{1,9},{5... | collective-permute-start | bytes 61448 | tf_op jit(solution)/shard_map/reduce_dir_sigma/ppermute | solution.py:336
  48.6 1.7 %collective-permute-start.20 = (f32[40,128]{1,0:T(8,128)S(1)}, f32[40,128]{1,0:T(8,128)S(1)}, u32[]{:S(2)}, u32[]{:S(2)}) collective-permute-start(f32[40,128]{1,0:T(8,128)S(1)} %get-tuple-element.69), channel_id=1, source_target_pairs={{0,24},{4,28},{8,16},{12,20},{16,8},{20,12},{24,0},{28,4},{1,25},{... | collective-permute-start | bytes 61448 | tf_op jit(solution)/shard_map/reduce_dir_sigma/ppermute | solution.py:336
  50.7 1.6 %collective-permute-done.19.got_refs_2_ = f32[40,128]{1,0:T(8,128)S(1)} collective-permute-done((f32[40,128]{1,0:T(8,128)S(1)}, f32[40,128]{1,0:T(8,128)S(1)}, u32[]{:S(2)}, u32[]{:S(2)}) %collective-permute-start.19) | collective-permute-done | bytes 20512 | tf_op jit(solution)/shard_map/reduce_dir_sigma/ppermute | solution.py:336
  52.2 1.1 %collective-permute-done.20.got_refs_3_ = f32[40,128]{1,0:T(8,128)S(1)} collective-permute-done((f32[40,128]{1,0:T(8,128)S(1)}, f32[40,128]{1,0:T(8,128)S(1)}, u32[]{:S(2)}, u32[]{:S(2)}) %collective-permute-start.20) | collective-permute-done | bytes 20512 | tf_op jit(solution)/shard_map/reduce_dir_sigma/ppermute | solution.py:336
  53.3 0.7 %ritz.1 = (f32[2,16,128]{2,1,0:T(8,128)}, f32[2,16,128]{2,1,0:T(8,128)}, f32[1,128]{1,0:T(1,128)}) custom-call(f32[8,128]{1,0:T(8,128)S(1)} %get-tuple-element.57.scalar_ref, f32[2,128,128]{2,1,0:T(8,128)S(1)} %get-tuple-element.48.local_ref, f32[4,16,128]{2,1,0:T(8,128)S(1)} %get-tuple-element.58.own_ref, f32[40,128]{1,0:T(8,128)S(1)} %get-tuple-element.66.got_refs_0_, ...), custom_call_target="tpu_custom_call" | custom-call | bytes 1048576 | tf_op jit(solution)/shard_map/ritz/pallas_call | solution.py:453
  (24 shorter events, 1.6 us)
Async XLA Ops:
  0.6 10.9 %collective-permute-start = (f32[2,128,128]{2,1,0:T(8,128)}, f32[2,128,128]{2,1,0:T(8,128)S(1)}, u32[]{:S(2)}, u32[]{:S(2)}) collective-permute-start(f32[2,128,128]{2,1,0:T(8,128)} %wave_ref.3), channel_id=1, source_target_pairs={{0,1},{1,0},{2,3},{3,2},{4,6},{5,7},{6,4},{7,5},{8,9},{9,8},{10,11... | collective-permute-start | bytes 393224 | tf_op jit(solution)/shard_map/gather_wave/ppermute | solution.py:343
  4.7 6.9 %collective-permute-start.1 = (f32[160,128]{1,0:T(8,128)S(1)}, f32[160,128]{1,0:T(8,128)S(1)}, u32[]{:S(2)}, u32[]{:S(2)}) collective-permute-start(f32[160,128]{1,0:T(8,128)S(1)} %get-tuple-element.43.sector_refs_0_), channel_id=1, source_target_pairs={{0,3},{1,2},{2,1},{3,0},{4,7},{5,6},{6,5},{7,4},{8,11},{9,10},{10,... | collective-permute-start | bytes 245768 | tf_op jit(solution)/shard_map/gather_wave/ppermute | solution.py:339
  11.6 4.7 %copy-start = (f32[2,128,128]{2,1,0:T(8,128)S(1)}, f32[2,128,128]{2,1,0:T(8,128)}, u32[]{:S(2)}) copy-start(f32[2,128,128]{2,1,0:T(8,128)} %diag_ref.1) | copy-start | bytes 393220
  11.6 1.5 %collective-permute-start.2 = (f32[2,128,128]{2,1,0:T(8,128)S(1)}, f32[2,128,128]{2,1,0:T(8,128)S(1)}, u32[]{:S(2)}, u32[]{:S(2)}) collective-permute-start(f32[2,128,128]{2,1,0:T(8,128)S(1)} %collective-permute-done.mine_refs_0_), channel_id=1, source_target_pairs={{0,4},{4,0},{8,12},{12,8},{16,20},{20,16},{24,28},{28,24},{1,5},{5... | collective-permute-start | bytes 393224 | tf_op jit(solution)/shard_map/swap_wave/ppermute | solution.py:333
  11.6 1.5 %collective-permute-start.3 = (f32[160,128]{1,0:T(8,128)S(1)}, f32[160,128]{1,0:T(8,128)S(1)}, u32[]{:S(2)}, u32[]{:S(2)}) collective-permute-start(f32[160,128]{1,0:T(8,128)S(1)} %collective-permute-done.1.last_ref.last_refs_0_), channel_id=1, source_target_pairs={{0,4},{4,0},{8,12},{12,8},{16,20},{20,16},{24,28},{28,24},{1,5},{5... | collective-permute-start | bytes 245768 | tf_op jit(solution)/shard_map/swap_wave/ppermute | solution.py:333
  15.9 1.7 %collective-permute-start.4 = (f32[136,128]{1,0:T(8,128)S(1)}, f32[136,128]{1,0:T(8,128)S(1)}, u32[]{:S(2)}, u32[]{:S(2)}) collective-permute-start(f32[136,128]{1,0:T(8,128)S(1)} %get-tuple-element.54), channel_id=1, source_target_pairs={{0,4},{4,0},{8,12},{12,8},{16,20},{20,16},{24,28},{28,24},{1,5},{5... | collective-permute-start | bytes 208904 | tf_op jit(solution)/shard_map/reduce_sigma/ppermute | solution.py:333
  16.2 14.3 %collective-permute-start.8 = (f32[2,128,128]{2,1,0:T(8,128)S(1)}, f32[2,128,128]{2,1,0:T(8,128)S(1)}, u32[]{:S(2)}, u32[]{:S(2)}) collective-permute-start(f32[2,128,128]{2,1,0:T(8,128)S(1)} %copy-done), channel_id=1, source_target_pairs={{0,1},{1,0},{2,3},{3,2},{4,6},{5,7},{6,4},{7,5},{8,9},{9,8},{10,11... | collective-permute-start | bytes 393224 | tf_op jit(solution)/shard_map/gather_diag/ppermute | solution.py:343
  17.6 5.9 %collective-permute-start.7 = (f32[168,128]{1,0:T(8,128)S(1)}, f32[168,128]{1,0:T(8,128)S(1)}, u32[]{:S(2)}, u32[]{:S(2)}) collective-permute-start(f32[168,128]{1,0:T(8,128)S(1)} %reduce_sigma.2.part_refs_0_), channel_id=1, source_target_pairs={{0,24},{4,28},{8,16},{12,20},{16,8},{20,12},{24,0},{28,4},{1,25},{... | collective-permute-start | bytes 258056 | tf_op jit(solution)/shard_map/reduce_sigma/ppermute | solution.py:336
  20.1 5.7 %collective-permute-start.6 = (f32[168,128]{1,0:T(8,128)S(1)}, f32[168,128]{1,0:T(8,128)S(1)}, u32[]{:S(2)}, u32[]{:S(2)}) collective-permute-start(f32[168,128]{1,0:T(8,128)S(1)} %reduce_sigma.2.part_refs_0_), channel_id=1, source_target_pairs={{0,16},{4,20},{8,24},{12,28},{16,0},{20,4},{24,8},{28,12},{1,17},{... | collective-permute-start | bytes 258056 | tf_op jit(solution)/shard_map/reduce_sigma/ppermute | solution.py:336
  20.6 5.4 %collective-permute-start.5 = (f32[168,128]{1,0:T(8,128)S(1)}, f32[168,128]{1,0:T(8,128)S(1)}, u32[]{:S(2)}, u32[]{:S(2)}) collective-permute-start(f32[168,128]{1,0:T(8,128)S(1)} %reduce_sigma.2.part_refs_0_), channel_id=1, source_target_pairs={{0,8},{4,12},{8,0},{12,4},{16,24},{20,28},{24,16},{28,20},{1,9},{5... | collective-permute-start | bytes 258056 | tf_op jit(solution)/shard_map/reduce_sigma/ppermute | solution.py:336
  26.0 6.9 %collective-permute-start.12 = (f32[136,128]{1,0:T(8,128)S(1)}, f32[136,128]{1,0:T(8,128)S(1)}, u32[]{:S(2)}, u32[]{:S(2)}) collective-permute-start(f32[136,128]{1,0:T(8,128)S(1)} %get-tuple-element.56.sum_refs_0_), channel_id=1, source_target_pairs={{0,3},{1,2},{2,1},{3,0},{4,7},{5,6},{6,5},{7,4},{8,11},{9,10},{10,... | collective-permute-start | bytes 208904 | tf_op jit(solution)/shard_map/gather_sigma/ppermute | solution.py:339
  28.3 6.5 %collective-permute-start.11 = (f32[136,128]{1,0:T(8,128)S(1)}, f32[136,128]{1,0:T(8,128)S(1)}, u32[]{:S(2)}, u32[]{:S(2)}) collective-permute-start(f32[136,128]{1,0:T(8,128)S(1)} %get-tuple-element.56.sum_refs_0_), channel_id=1, source_target_pairs={{0,2},{1,3},{2,0},{3,1},{4,6},{5,7},{6,4},{7,5},{8,10},{9,11},{10,... | collective-permute-start | bytes 208904 | tf_op jit(solution)/shard_map/gather_sigma/ppermute | solution.py:339
  28.3 6.5 %collective-permute-start.10 = (f32[136,128]{1,0:T(8,128)S(1)}, f32[136,128]{1,0:T(8,128)S(1)}, u32[]{:S(2)}, u32[]{:S(2)}) collective-permute-start(f32[136,128]{1,0:T(8,128)S(1)} %get-tuple-element.56.sum_refs_0_), channel_id=1, source_target_pairs={{0,1},{1,0},{2,3},{3,2},{4,5},{5,4},{6,7},{7,6},{8,9},{9,8},{10,11... | collective-permute-start | bytes 208904 | tf_op jit(solution)/shard_map/gather_sigma/ppermute | solution.py:339
  30.5 1.3 %collective-permute-start.9 = (f32[128,128]{1,0:T(8,128)S(1)}, f32[128,128]{1,0:T(8,128)S(1)}, u32[]{:S(2)}, u32[]{:S(2)}) collective-permute-start(f32[128,128]{1,0:T(8,128)S(1)} %swap_diag.1), channel_id=1, source_target_pairs={{0,4},{4,0},{8,12},{12,8},{16,20},{20,16},{24,28},{28,24},{1,5},{5... | collective-permute-start | bytes 196616 | tf_op jit(solution)/shard_map/swap_diag/ppermute | solution.py:333
  35.2 1.7 %collective-permute-start.13 = (f32[648,128]{1,0:T(8,128)S(1)}, f32[648,128]{1,0:T(8,128)S(1)}, u32[]{:S(2)}, u32[]{:S(2)}) collective-permute-start(f32[648,128]{1,0:T(8,128)S(1)} %correction.1.mine_ref), channel_id=1, source_target_pairs={{0,4},{4,0},{8,12},{12,8},{16,20},{20,16},{24,28},{28,24},{1,5},{5... | collective-permute-start | bytes 995336 | tf_op jit(solution)/shard_map/correction/ppermute | solution.py:333
  38.8 6.0 %collective-permute-start.16 = (f32[8,128]{1,0:T(8,128)S(1)}, f32[8,128]{1,0:T(8,128)S(1)}, u32[]{:S(2)}, u32[]{:S(2)}) collective-permute-start(f32[8,128]{1,0:T(8,128)S(1)} %get-tuple-element.63.curve_refs_0_), channel_id=1, source_target_pairs={{0,3},{1,2},{2,1},{3,0},{4,7},{5,6},{6,5},{7,4},{8,11},{9,10},{10,... | collective-permute-start | bytes 12296 | tf_op jit(solution)/shard_map/even_terms/ppermute | solution.py:339
  41.0 4.5 %collective-permute-start.15 = (f32[8,128]{1,0:T(8,128)S(1)}, f32[8,128]{1,0:T(8,128)S(1)}, u32[]{:S(2)}, u32[]{:S(2)}) collective-permute-start(f32[8,128]{1,0:T(8,128)S(1)} %get-tuple-element.63.curve_refs_0_), channel_id=1, source_target_pairs={{0,2},{1,3},{2,0},{3,1},{4,6},{5,7},{6,4},{7,5},{8,10},{9,11},{10,... | collective-permute-start | bytes 12296 | tf_op jit(solution)/shard_map/even_terms/ppermute | solution.py:339
  41.0 4.5 %collective-permute-start.14 = (f32[8,128]{1,0:T(8,128)S(1)}, f32[8,128]{1,0:T(8,128)S(1)}, u32[]{:S(2)}, u32[]{:S(2)}) collective-permute-start(f32[8,128]{1,0:T(8,128)S(1)} %get-tuple-element.63.curve_refs_0_), channel_id=1, source_target_pairs={{0,1},{1,0},{2,3},{3,2},{4,5},{5,4},{6,7},{7,6},{8,9},{9,8},{10,11... | collective-permute-start | bytes 12296 | tf_op jit(solution)/shard_map/even_terms/ppermute | solution.py:339
  45.5 1.3 %collective-permute-start.17 = (f32[136,128]{1,0:T(8,128)S(1)}, f32[136,128]{1,0:T(8,128)S(1)}, u32[]{:S(2)}, u32[]{:S(2)}) collective-permute-start(f32[136,128]{1,0:T(8,128)S(1)} %get-tuple-element.65), channel_id=1, source_target_pairs={{0,4},{4,0},{8,12},{12,8},{16,20},{20,16},{24,28},{28,24},{1,5},{5... | collective-permute-start | bytes 208904 | tf_op jit(solution)/shard_map/reduce_dir_sigma/ppermute | solution.py:333
  46.8 3.8 %collective-permute-start.18 = (f32[40,128]{1,0:T(8,128)S(1)}, f32[40,128]{1,0:T(8,128)S(1)}, u32[]{:S(2)}, u32[]{:S(2)}) collective-permute-start(f32[40,128]{1,0:T(8,128)S(1)} %get-tuple-element.67), channel_id=1, source_target_pairs={{0,8},{4,12},{8,0},{12,4},{16,24},{20,28},{24,16},{28,20},{1,9},{5... | collective-permute-start | bytes 61448 | tf_op jit(solution)/shard_map/reduce_dir_sigma/ppermute | solution.py:336
  48.3 4.0 %collective-permute-start.19 = (f32[40,128]{1,0:T(8,128)S(1)}, f32[40,128]{1,0:T(8,128)S(1)}, u32[]{:S(2)}, u32[]{:S(2)}) collective-permute-start(f32[40,128]{1,0:T(8,128)S(1)} %get-tuple-element.68), channel_id=1, source_target_pairs={{0,16},{4,20},{8,24},{12,28},{16,0},{20,4},{24,8},{28,12},{1,17},{... | collective-permute-start | bytes 61448 | tf_op jit(solution)/shard_map/reduce_dir_sigma/ppermute | solution.py:336
  48.6 4.7 %collective-permute-start.20 = (f32[40,128]{1,0:T(8,128)S(1)}, f32[40,128]{1,0:T(8,128)S(1)}, u32[]{:S(2)}, u32[]{:S(2)}) collective-permute-start(f32[40,128]{1,0:T(8,128)S(1)} %get-tuple-element.69), channel_id=1, source_target_pairs={{0,24},{4,28},{8,16},{12,20},{16,8},{20,12},{24,0},{28,4},{1,25},{... | collective-permute-start | bytes 61448 | tf_op jit(solution)/shard_map/reduce_dir_sigma/ppermute | solution.py:336

commit v5 on v4

--- a/solution.py
+++ b/solution.py
@@ -170,7 +170,7 @@
             n_sec, n_sec // 2, core, lambda i: mine_refs[i][s], lambda i: theirs_refs[i][s],
             lambda: jnp.where(core == s, last_ref[:size], other_last_ref[:size]),
         )
-        blocks.append(part[s * size : (s + 1) * size] + (coupling_ref[0, s] / n_ops) * partner.T)
+        blocks.append(part[s * size : (s + 1) * size] + (coupling_ref[:, s : s + 1] * (1.0 / n_ops)) * partner.T)
         corr += total(local_ref[s] * blocks[s])
     keep_ref[:size] = jnp.where(core == 0, blocks[0], blocks[1])
     send_ref[:size] = jnp.where(core == 0, blocks[1], blocks[0])
@@ -239,7 +239,7 @@
         vec = jnp.where(mine, mine_ref[:size], theirs_ref[:size])
         partner = jnp.where(mine, mine_ref[mirror], theirs_ref[mirror])
         block = part[s * size : (s + 1) * size]
-        mirrored = (coupling_ref[0, s] / n_ops) * partner.T
+        mirrored = (coupling_ref[:, s : s + 1] * (1.0 / n_ops)) * partner.T
         part_ref[s] = block + mirrored
         for i, first in enumerate((0, n_sec)):
             span = pl.ds(pl.multiple_of(first * size + chip * share, share), share)
@@ -386,7 +386,7 @@
             ],
             limit=SMALL,
         )(*[in_hbm(values) for values in held])
-        loaded, mine = lax.optimization_barrier((loaded, mine))
+        loaded, mine[:-1] = lax.optimization_barrier((loaded, mine[:-1]))
         pairs, weights, local, source, coupling = loaded
     with jax.named_scope("swap_wave"):
         theirs = [swap(values) for values in mine]
@@ -395,7 +395,7 @@
         keep, send, norm = call(
             functools.partial(first_kernel, n_sec, n_ops),
             (message_shape, message_shape, scalar_shape),
-            [SMEM, SMEM] + [VMEM] * 3 + [[VMEM] * len(zs)] * 2 + [VMEM] * 2,
+            [SMEM, VMEM] + [VMEM] * 3 + [[VMEM] * len(zs)] * 2 + [VMEM] * 2,
             [pltpu.VMEM(slot_shape, BF16), pltpu.VMEM(stack_shape, BF16)],
             matmul_flops,
         )(source, coupling, pairs, weights, local, mine, theirs, last, other_last)
@@ -430,7 +430,7 @@
                 shape((2 * owned, rows, size), F32),
                 scalar_shape,
             ),
-            [SMEM, SMEM] + [VMEM] * 4,
+            [SMEM, VMEM] + [VMEM] * 4,
             [pltpu.VMEM(half_shape, BF16)],
             matmul_flops // 2,
         )(source, coupling, pairs, weights, found, other)

time: 54.2 us -> 54.2 us (level)
  starting transfers between devices: 24.1 us -> 23.5 us
    ppermute x6, starting transfers between devices: 1.11 us -> 0.5 us  [swap(): return lax.ppermute(values, 'ops', [(i, i ^ 1) for i in range(n_ops)])]
where the time goes in v5:
time: 54.2 us; the launch traced here: 54 us
  starting transfers between devices  23.5 us (43%)
  waiting for transfers between devices  18 us (33%)
  Pallas kernels  11.7 us (22%)
  between operations  0.76 us (1%)
    ppermute x7, starting transfers between devices, to_plane(): return lax.ppermute(values, 'sec', [(i, i ^ m) for i in range(n_sec)])  11.4 us
    ppermute x6, waiting for transfers between devices, to_chip(): return lax.ppermute(values, 'ops', [(i, i ^ 2 * m) for i in range(n_ops)])  7.94 us
    ppermute x6, starting transfers between devices, to_chip(): return lax.ppermute(values, 'ops', [(i, i ^ 2 * m) for i in range(n_ops)])  7.11 us
    ppermute x6, waiting for transfers between devices, swap(): return lax.ppermute(values, 'ops', [(i, i ^ 1) for i in range(n_ops)])  5.39 us
    ppermute x7, waiting for transfers between devices, to_plane(): return lax.ppermute(values, 'sec', [(i, i ^ m) for i in range(n_sec)])  4.71 us
    ppermute x2, starting transfers between devices, to_planes(): return lax.ppermute(values, ('ops', 'sec'), moves)  4.43 us
    pallas_call x1, Pallas kernels, body(): call(load_kernel, (shape((terms, owned, size, 2 * size), BF16), shape((2...  3.28 us
    pallas_call x1, Pallas kernels, body(): call(functools.partial(first_kernel, n_sec, n_ops), (message_shape, messa...  2.83 us
  transfers between devices with their start and end apart: 21, of which 14 were waited for; matrix products, arithmetic and copies ran while one was open for 0% of the time, Pallas kernels for 11%

profile of v5, /device:TPU:0, one launch (start us, length us, event | category | flops | bytes accessed | tf_op | source)
XLA Modules:
  0.0 54.0 jit_solution(2059413738392171784)
XLA Ops:
  0.6 3.1 %collective-permute-start = (f32[2,128,128]{2,1,0:T(8,128)}, f32[2,128,128]{2,1,0:T(8,128)S(1)}, u32[]{:S(2)}, u32[]{:S(2)}) collective-permute-start(f32[2,128,128]{2,1,0:T(8,128)} %wave_ref.3), channel_id=1, source_target_pairs={{0,1},{1,0},{2,3},{3,2},{4,6},{5,7},{6,4},{7,5},{8,9},{9,8},{10,11... | collective-permute-start | bytes 393224 | tf_op jit(solution)/shard_map/gather_wave/ppermute | solution.py:343
  3.7 0.9 %gather_wave.1 = (f32[160,128]{1,0:T(8,128)S(1)}, f32[128,128]{1,0:T(8,128)S(1)}) custom-call(f32[2,128,128]{2,1,0:T(8,128)} %wave_ref.3, f32[2,128,128]{2,1,0:T(8,128)} %diag_ref.1), custom_call_target="tpu_custom_call" | custom-call | bytes 1048576 | tf_op jit(solution)/shard_map/gather_wave/pallas_call | solution.py:362
  4.7 2.5 %collective-permute-start.2 = (f32[160,128]{1,0:T(8,128)S(1)}, f32[160,128]{1,0:T(8,128)S(1)}, u32[]{:S(2)}, u32[]{:S(2)}) collective-permute-start(f32[160,128]{1,0:T(8,128)S(1)} %get-tuple-element.48.sector_refs_0_), channel_id=1, source_target_pairs={{0,3},{1,2},{2,1},{3,0},{4,7},{5,6},{6,5},{7,4},{8,11},{9,10},{10,... | collective-permute-start | bytes 245768 | tf_op jit(solution)/shard_map/gather_wave/ppermute | solution.py:339
  7.2 3.3 %load.1 = (bf16[24,2,128,256]{3,2,1,0:T(8,128)(2,1)S(1)}, bf16[6144,256]{1,0:T(8,128)(2,1)S(1)}, f32[2,128,128]{2,1,0:T(8,128)S(1)}, s32[2,24]{1,0:T(2,128)S(1)}, f32[1,2]{1,0:T(1,128)S(1)}) custom-call(f32[24,2,128,128]{3,2,1,0:T(8,128)} %left_ref.1, f32[24,128,128]{2,1,0:T(8,128)} %right_ref.1, f32[2,128,128]{2,1,0:T(8,128)} %wave_ref.3, s32[2,24]{1,0:T(2,128)} %bitcast.4, ...), custom_call_target="tpu_custom_call" | custom-call | bytes 1048576 | tf_op jit(solution)/shard_map/load/pallas_call | solution.py:374
  10.6 1.0 %collective-permute-done.2.last_ref.last_refs_0_ = f32[160,128]{1,0:T(8,128)S(1)} collective-permute-done((f32[160,128]{1,0:T(8,128)S(1)}, f32[160,128]{1,0:T(8,128)S(1)}, u32[]{:S(2)}, u32[]{:S(2)}) %collective-permute-start.2) | collective-permute-done | bytes 81952 | tf_op jit(solution)/shard_map/gather_wave/ppermute | solution.py:339
  11.6 1.3 %collective-permute-done.3.other_last_ref = f32[160,128]{1,0:T(8,128)S(1)} collective-permute-done((f32[160,128]{1,0:T(8,128)S(1)}, f32[160,128]{1,0:T(8,128)S(1)}, u32[]{:S(2)}, u32[]{:S(2)}) %collective-permute-start.3) | collective-permute-done | bytes 81952 | tf_op jit(solution)/shard_map/swap_wave/ppermute | solution.py:333
  12.8 2.8 %first_apply.1 = (f32[136,128]{1,0:T(8,128)S(1)}, f32[136,128]{1,0:T(8,128)S(1)}, f32[8,128]{1,0:T(8,128)S(1)}) custom-call(s32[2,24]{1,0:T(2,128)S(1)} %get-tuple-element.42.source_ref, f32[1,2]{1,0:T(1,128)S(1)} %get-tuple-element.43.coupling_ref, bf16[24,2,128,256]{3,2,1,0:T(8,128)(2,1)S(1)} %get-tuple-element.44.pairs_ref, ...), custom_call_target="tpu_custom_call" | custom-call | flops 1207959552 | bytes 1048576 | tf_op jit(solution)/shard_map/first_apply/pallas_call | solution.py:395
  15.9 1.3 %collective-permute-start.8 = (f32[2,128,128]{2,1,0:T(8,128)S(1)}, f32[2,128,128]{2,1,0:T(8,128)S(1)}, u32[]{:S(2)}, u32[]{:S(2)}) collective-permute-start(f32[2,128,128]{2,1,0:T(8,128)S(1)} %copy-done), channel_id=1, source_target_pairs={{0,1},{1,0},{2,3},{3,2},{4,6},{5,7},{6,4},{7,5},{8,9},{9,8},{10,11... | collective-permute-start | bytes 393224 | tf_op jit(solution)/shard_map/gather_diag/ppermute | solution.py:343
  17.3 2.5 %collective-permute-start.7 = (f32[168,128]{1,0:T(8,128)S(1)}, f32[168,128]{1,0:T(8,128)S(1)}, u32[]{:S(2)}, u32[]{:S(2)}) collective-permute-start(f32[168,128]{1,0:T(8,128)S(1)} %reduce_sigma.2.part_refs_0_), channel_id=1, source_target_pairs={{0,24},{4,28},{8,16},{12,20},{16,8},{20,12},{24,0},{28,4},{1,25},{... | collective-permute-start | bytes 258056 | tf_op jit(solution)/shard_map/reduce_sigma/ppermute | solution.py:336
  19.8 0.5 collective-permute-start.6
  20.3 0.5 collective-permute-start.5
  20.8 2.2 %collective-permute-done.7.part_refs_3_ = f32[168,128]{1,0:T(8,128)S(1)} collective-permute-done((f32[168,128]{1,0:T(8,128)S(1)}, f32[168,128]{1,0:T(8,128)S(1)}, u32[]{:S(2)}, u32[]{:S(2)}) %collective-permute-start.7) | collective-permute-done | bytes 86048 | tf_op jit(solution)/shard_map/reduce_sigma/ppermute | solution.py:336
  23.0 2.4 %collective-permute-done.6.part_refs_2_ = f32[168,128]{1,0:T(8,128)S(1)} collective-permute-done((f32[168,128]{1,0:T(8,128)S(1)}, f32[168,128]{1,0:T(8,128)S(1)}, u32[]{:S(2)}, u32[]{:S(2)}) %collective-permute-start.6) | collective-permute-done | bytes 86048 | tf_op jit(solution)/shard_map/reduce_sigma/ppermute | solution.py:336
  25.6 2.3 %collective-permute-start.12 = (f32[136,128]{1,0:T(8,128)S(1)}, f32[136,128]{1,0:T(8,128)S(1)}, u32[]{:S(2)}, u32[]{:S(2)}) collective-permute-start(f32[136,128]{1,0:T(8,128)S(1)} %get-tuple-element.54.sum_refs_0_), channel_id=1, source_target_pairs={{0,3},{1,2},{2,1},{3,0},{4,7},{5,6},{6,5},{7,4},{8,11},{9,10},{10,... | collective-permute-start | bytes 208904 | tf_op jit(solution)/shard_map/gather_sigma/ppermute | solution.py:339
  28.0 2.0 %collective-permute-start.10 = (f32[136,128]{1,0:T(8,128)S(1)}, f32[136,128]{1,0:T(8,128)S(1)}, u32[]{:S(2)}, u32[]{:S(2)}) collective-permute-start(f32[136,128]{1,0:T(8,128)S(1)} %get-tuple-element.54.sum_refs_0_), channel_id=1, source_target_pairs={{0,1},{1,0},{2,3},{3,2},{4,5},{5,4},{6,7},{7,6},{8,9},{9,8},{10,11... | collective-permute-start | bytes 208904 | tf_op jit(solution)/shard_map/gather_sigma/ppermute | solution.py:339
  30.1 1.2 %collective-permute-done.9.other_diag_refs_0_ = f32[128,128]{1,0:T(8,128)S(1)} collective-permute-done((f32[128,128]{1,0:T(8,128)S(1)}, f32[128,128]{1,0:T(8,128)S(1)}, u32[]{:S(2)}, u32[]{:S(2)}) %collective-permute-start.9) | collective-permute-done | bytes 65568 | tf_op jit(solution)/shard_map/swap_diag/ppermute | solution.py:333
  31.4 1.2 %collective-permute-done.12.sum_refs_3_ = f32[136,128]{1,0:T(8,128)S(1)} collective-permute-done((f32[136,128]{1,0:T(8,128)S(1)}, f32[136,128]{1,0:T(8,128)S(1)}, u32[]{:S(2)}, u32[]{:S(2)}) %collective-permute-start.12) | collective-permute-done | bytes 69664 | tf_op jit(solution)/shard_map/gather_sigma/ppermute | solution.py:339
  32.5 2.3 %collective-permute-done.11.sum_refs_2_ = f32[136,128]{1,0:T(8,128)S(1)} collective-permute-done((f32[136,128]{1,0:T(8,128)S(1)}, f32[136,128]{1,0:T(8,128)S(1)}, u32[]{:S(2)}, u32[]{:S(2)}) %collective-permute-start.11) | collective-permute-done | bytes 69664 | tf_op jit(solution)/shard_map/gather_sigma/ppermute | solution.py:339
  34.8 0.4 correction.1.mine_ref
  35.3 1.6 %collective-permute-done.13.theirs_ref = f32[648,128]{1,0:T(8,128)S(1)} collective-permute-done((f32[648,128]{1,0:T(8,128)S(1)}, f32[648,128]{1,0:T(8,128)S(1)}, u32[]{:S(2)}, u32[]{:S(2)}) %collective-permute-start.13) | collective-permute-done | bytes 331808 | tf_op jit(solution)/shard_map/correction/ppermute | solution.py:333
  36.9 1.9 %even_terms.1 = (bf16[9,256,256]{2,1,0:T(8,128)(2,1)S(1)}, f32[2,128,128]{2,1,0:T(8,128)S(1)}, f32[8,128]{1,0:T(8,128)S(1)}, f32[4,16,128]{2,1,0:T(8,128)S(1)}, f32[8,128]{1,0:T(8,128)S(1)}) custom-call(s32[2,24]{1,0:T(2,128)S(1)} %get-tuple-element.42.source_ref, f32[1,2]{1,0:T(1,128)S(1)} %get-tuple-element.43.coupling_ref, ...), custom_call_target="tpu_custom_call" | custom-call | flops 603979776 | bytes 1048576 | tf_op jit(solution)/shard_map/even_terms/pallas_call | solution.py:424
  38.8 1.9 %collective-permute-start.16 = (f32[8,128]{1,0:T(8,128)S(1)}, f32[8,128]{1,0:T(8,128)S(1)}, u32[]{:S(2)}, u32[]{:S(2)}) collective-permute-start(f32[8,128]{1,0:T(8,128)S(1)} %get-tuple-element.61.curve_refs_0_), channel_id=1, source_target_pairs={{0,3},{1,2},{2,1},{3,0},{4,7},{5,6},{6,5},{7,4},{8,11},{9,10},{10,... | collective-permute-start | bytes 12296 | tf_op jit(solution)/shard_map/even_terms/ppermute | solution.py:339
  40.7 2.6 %collective-permute-start.14 = (f32[8,128]{1,0:T(8,128)S(1)}, f32[8,128]{1,0:T(8,128)S(1)}, u32[]{:S(2)}, u32[]{:S(2)}) collective-permute-start(f32[8,128]{1,0:T(8,128)S(1)} %get-tuple-element.61.curve_refs_0_), channel_id=1, source_target_pairs={{0,1},{1,0},{2,3},{3,2},{4,5},{5,4},{6,7},{7,6},{8,9},{9,8},{10,11... | collective-permute-start | bytes 12296 | tf_op jit(solution)/shard_map/even_terms/ppermute | solution.py:339
  43.2 1.6 %odd_terms.1 = (f32[128,128]{1,0:T(8,128)S(1)}, f32[128,128]{1,0:T(8,128)S(1)}) custom-call(s32[2,24]{1,0:T(2,128)S(1)} %get-tuple-element.42.source_ref, bf16[24,2,128,256]{3,2,1,0:T(8,128)(2,1)S(1)} %get-tuple-element.44.pairs_ref, bf16[6144,256]{1,0:T(8,128)(2,1)S(1)} %get-tuple-element.45.weights_ref, bf16[9,256,256]{2,1,0:T(8,128)(2,1)S(1)} %get-tuple-element.57.slots, ...), custom_call_target="tpu_custom_call" | custom-call | flops 603979776 | bytes 1048576 | tf_op jit(solution)/shard_map/odd_terms/pallas_call | solution.py:439
  44.8 0.3 collective-permute-done.15.curve_refs_2_
  45.3 1.2 %collective-permute-done.17.got_ref = f32[136,128]{1,0:T(8,128)S(1)} collective-permute-done((f32[136,128]{1,0:T(8,128)S(1)}, f32[136,128]{1,0:T(8,128)S(1)}, u32[]{:S(2)}, u32[]{:S(2)}) %collective-permute-start.17) | collective-permute-done | bytes 69664 | tf_op jit(solution)/shard_map/reduce_dir_sigma/ppermute | solution.py:333
  46.5 1.9 %collective-permute-start.18 = (f32[40,128]{1,0:T(8,128)S(1)}, f32[40,128]{1,0:T(8,128)S(1)}, u32[]{:S(2)}, u32[]{:S(2)}) collective-permute-start(f32[40,128]{1,0:T(8,128)S(1)} %get-tuple-element.65), channel_id=1, source_target_pairs={{0,8},{4,12},{8,0},{12,4},{16,24},{20,28},{24,16},{28,20},{1,9},{5... | collective-permute-start | bytes 61448 | tf_op jit(solution)/shard_map/reduce_dir_sigma/ppermute | solution.py:336
  48.6 1.5 %collective-permute-start.20 = (f32[40,128]{1,0:T(8,128)S(1)}, f32[40,128]{1,0:T(8,128)S(1)}, u32[]{:S(2)}, u32[]{:S(2)}) collective-permute-start(f32[40,128]{1,0:T(8,128)S(1)} %get-tuple-element.67), channel_id=1, source_target_pairs={{0,24},{4,28},{8,16},{12,20},{16,8},{20,12},{24,0},{28,4},{1,25},{... | collective-permute-start | bytes 61448 | tf_op jit(solution)/shard_map/reduce_dir_sigma/ppermute | solution.py:336
  50.1 0.3 collective-permute-done.18.got_refs_1_
  50.4 2.0 %collective-permute-done.19.got_refs_2_ = f32[40,128]{1,0:T(8,128)S(1)} collective-permute-done((f32[40,128]{1,0:T(8,128)S(1)}, f32[40,128]{1,0:T(8,128)S(1)}, u32[]{:S(2)}, u32[]{:S(2)}) %collective-permute-start.19) | collective-permute-done | bytes 20512 | tf_op jit(solution)/shard_map/reduce_dir_sigma/ppermute | solution.py:336
  52.3 1.0 %collective-permute-done.20.got_refs_3_ = f32[40,128]{1,0:T(8,128)S(1)} collective-permute-done((f32[40,128]{1,0:T(8,128)S(1)}, f32[40,128]{1,0:T(8,128)S(1)}, u32[]{:S(2)}, u32[]{:S(2)}) %collective-permute-start.20) | collective-permute-done | bytes 20512 | tf_op jit(solution)/shard_map/reduce_dir_sigma/ppermute | solution.py:336
  53.3 0.7 %ritz.1 = (f32[2,16,128]{2,1,0:T(8,128)}, f32[2,16,128]{2,1,0:T(8,128)}, f32[1,128]{1,0:T(1,128)}) custom-call(f32[8,128]{1,0:T(8,128)S(1)} %get-tuple-element.55.scalar_ref, f32[2,128,128]{2,1,0:T(8,128)S(1)} %get-tuple-element.46.local_ref, f32[4,16,128]{2,1,0:T(8,128)S(1)} %get-tuple-element.56.own_ref, f32[40,128]{1,0:T(8,128)S(1)} %get-tuple-element.64.got_refs_0_, ...), custom_call_target="tpu_custom_call" | custom-call | bytes 1048576 | tf_op jit(solution)/shard_map/ritz/pallas_call | solution.py:453
  (24 shorter events, 1.1 us)
Async XLA Ops:
  0.6 9.9 %collective-permute-start = (f32[2,128,128]{2,1,0:T(8,128)}, f32[2,128,128]{2,1,0:T(8,128)S(1)}, u32[]{:S(2)}, u32[]{:S(2)}) collective-permute-start(f32[2,128,128]{2,1,0:T(8,128)} %wave_ref.3), channel_id=1, source_target_pairs={{0,1},{1,0},{2,3},{3,2},{4,6},{5,7},{6,4},{7,5},{8,9},{9,8},{10,11... | collective-permute-start | bytes 393224 | tf_op jit(solution)/shard_map/gather_wave/ppermute | solution.py:343
  4.7 6.9 %collective-permute-start.2 = (f32[160,128]{1,0:T(8,128)S(1)}, f32[160,128]{1,0:T(8,128)S(1)}, u32[]{:S(2)}, u32[]{:S(2)}) collective-permute-start(f32[160,128]{1,0:T(8,128)S(1)} %get-tuple-element.48.sector_refs_0_), channel_id=1, source_target_pairs={{0,3},{1,2},{2,1},{3,0},{4,7},{5,6},{6,5},{7,4},{8,11},{9,10},{10,... | collective-permute-start | bytes 245768 | tf_op jit(solution)/shard_map/gather_wave/ppermute | solution.py:339
  10.5 5.4 %copy-start = (f32[2,128,128]{2,1,0:T(8,128)S(1)}, f32[2,128,128]{2,1,0:T(8,128)}, u32[]{:S(2)}) copy-start(f32[2,128,128]{2,1,0:T(8,128)} %diag_ref.1) | copy-start | bytes 393220
  10.5 2.3 %collective-permute-start.1 = (f32[2,128,128]{2,1,0:T(8,128)S(1)}, f32[2,128,128]{2,1,0:T(8,128)S(1)}, u32[]{:S(2)}, u32[]{:S(2)}) collective-permute-start(f32[2,128,128]{2,1,0:T(8,128)S(1)} %collective-permute-done.mine_refs_0_), channel_id=1, source_target_pairs={{0,4},{4,0},{8,12},{12,8},{16,20},{20,16},{24,28},{28,24},{1,5},{5... | collective-permute-start | bytes 393224 | tf_op jit(solution)/shard_map/swap_wave/ppermute | solution.py:333
  11.6 1.3 %collective-permute-start.3 = (f32[160,128]{1,0:T(8,128)S(1)}, f32[160,128]{1,0:T(8,128)S(1)}, u32[]{:S(2)}, u32[]{:S(2)}) collective-permute-start(f32[160,128]{1,0:T(8,128)S(1)} %collective-permute-done.2.last_ref.last_refs_0_), channel_id=1, source_target_pairs={{0,4},{4,0},{8,12},{12,8},{16,20},{20,16},{24,28},{28,24},{1,5},{5... | collective-permute-start | bytes 245768 | tf_op jit(solution)/shard_map/swap_wave/ppermute | solution.py:333
  15.7 1.6 %collective-permute-start.4 = (f32[136,128]{1,0:T(8,128)S(1)}, f32[136,128]{1,0:T(8,128)S(1)}, u32[]{:S(2)}, u32[]{:S(2)}) collective-permute-start(f32[136,128]{1,0:T(8,128)S(1)} %get-tuple-element.52), channel_id=1, source_target_pairs={{0,4},{4,0},{8,12},{12,8},{16,20},{20,16},{24,28},{28,24},{1,5},{5... | collective-permute-start | bytes 208904 | tf_op jit(solution)/shard_map/reduce_sigma/ppermute | solution.py:333
  15.9 14.1 %collective-permute-start.8 = (f32[2,128,128]{2,1,0:T(8,128)S(1)}, f32[2,128,128]{2,1,0:T(8,128)S(1)}, u32[]{:S(2)}, u32[]{:S(2)}) collective-permute-start(f32[2,128,128]{2,1,0:T(8,128)S(1)} %copy-done), channel_id=1, source_target_pairs={{0,1},{1,0},{2,3},{3,2},{4,6},{5,7},{6,4},{7,5},{8,9},{9,8},{10,11... | collective-permute-start | bytes 393224 | tf_op jit(solution)/shard_map/gather_diag/ppermute | solution.py:343
  17.3 5.7 %collective-permute-start.7 = (f32[168,128]{1,0:T(8,128)S(1)}, f32[168,128]{1,0:T(8,128)S(1)}, u32[]{:S(2)}, u32[]{:S(2)}) collective-permute-start(f32[168,128]{1,0:T(8,128)S(1)} %reduce_sigma.2.part_refs_0_), channel_id=1, source_target_pairs={{0,24},{4,28},{8,16},{12,20},{16,8},{20,12},{24,0},{28,4},{1,25},{... | collective-permute-start | bytes 258056 | tf_op jit(solution)/shard_map/reduce_sigma/ppermute | solution.py:336
  19.8 5.6 %collective-permute-start.6 = (f32[168,128]{1,0:T(8,128)S(1)}, f32[168,128]{1,0:T(8,128)S(1)}, u32[]{:S(2)}, u32[]{:S(2)}) collective-permute-start(f32[168,128]{1,0:T(8,128)S(1)} %reduce_sigma.2.part_refs_0_), channel_id=1, source_target_pairs={{0,16},{4,20},{8,24},{12,28},{16,0},{20,4},{24,8},{28,12},{1,17},{... | collective-permute-start | bytes 258056 | tf_op jit(solution)/shard_map/reduce_sigma/ppermute | solution.py:336
  20.3 5.3 %collective-permute-start.5 = (f32[168,128]{1,0:T(8,128)S(1)}, f32[168,128]{1,0:T(8,128)S(1)}, u32[]{:S(2)}, u32[]{:S(2)}) collective-permute-start(f32[168,128]{1,0:T(8,128)S(1)} %reduce_sigma.2.part_refs_0_), channel_id=1, source_target_pairs={{0,8},{4,12},{8,0},{12,4},{16,24},{20,28},{24,16},{28,20},{1,9},{5... | collective-permute-start | bytes 258056 | tf_op jit(solution)/shard_map/reduce_sigma/ppermute | solution.py:336
  25.6 6.9 %collective-permute-start.12 = (f32[136,128]{1,0:T(8,128)S(1)}, f32[136,128]{1,0:T(8,128)S(1)}, u32[]{:S(2)}, u32[]{:S(2)}) collective-permute-start(f32[136,128]{1,0:T(8,128)S(1)} %get-tuple-element.54.sum_refs_0_), channel_id=1, source_target_pairs={{0,3},{1,2},{2,1},{3,0},{4,7},{5,6},{6,5},{7,4},{8,11},{9,10},{10,... | collective-permute-start | bytes 208904 | tf_op jit(solution)/shard_map/gather_sigma/ppermute | solution.py:339
  27.9 6.9 %collective-permute-start.11 = (f32[136,128]{1,0:T(8,128)S(1)}, f32[136,128]{1,0:T(8,128)S(1)}, u32[]{:S(2)}, u32[]{:S(2)}) collective-permute-start(f32[136,128]{1,0:T(8,128)S(1)} %get-tuple-element.54.sum_refs_0_), channel_id=1, source_target_pairs={{0,2},{1,3},{2,0},{3,1},{4,6},{5,7},{6,4},{7,5},{8,10},{9,11},{10,... | collective-permute-start | bytes 208904 | tf_op jit(solution)/shard_map/gather_sigma/ppermute | solution.py:339
  28.0 6.8 %collective-permute-start.10 = (f32[136,128]{1,0:T(8,128)S(1)}, f32[136,128]{1,0:T(8,128)S(1)}, u32[]{:S(2)}, u32[]{:S(2)}) collective-permute-start(f32[136,128]{1,0:T(8,128)S(1)} %get-tuple-element.54.sum_refs_0_), channel_id=1, source_target_pairs={{0,1},{1,0},{2,3},{3,2},{4,5},{5,4},{6,7},{7,6},{8,9},{9,8},{10,11... | collective-permute-start | bytes 208904 | tf_op jit(solution)/shard_map/gather_sigma/ppermute | solution.py:339
  30.0 1.3 %collective-permute-start.9 = (f32[128,128]{1,0:T(8,128)S(1)}, f32[128,128]{1,0:T(8,128)S(1)}, u32[]{:S(2)}, u32[]{:S(2)}) collective-permute-start(f32[128,128]{1,0:T(8,128)S(1)} %swap_diag.1), channel_id=1, source_target_pairs={{0,4},{4,0},{8,12},{12,8},{16,20},{20,16},{24,28},{28,24},{1,5},{5... | collective-permute-start | bytes 196616 | tf_op jit(solution)/shard_map/swap_diag/ppermute | solution.py:333
  35.2 1.7 %collective-permute-start.13 = (f32[648,128]{1,0:T(8,128)S(1)}, f32[648,128]{1,0:T(8,128)S(1)}, u32[]{:S(2)}, u32[]{:S(2)}) collective-permute-start(f32[648,128]{1,0:T(8,128)S(1)} %correction.1.mine_ref), channel_id=1, source_target_pairs={{0,4},{4,0},{8,12},{12,8},{16,20},{20,16},{24,28},{28,24},{1,5},{5... | collective-permute-start | bytes 995336 | tf_op jit(solution)/shard_map/correction/ppermute | solution.py:333
  38.8 6.1 %collective-permute-start.16 = (f32[8,128]{1,0:T(8,128)S(1)}, f32[8,128]{1,0:T(8,128)S(1)}, u32[]{:S(2)}, u32[]{:S(2)}) collective-permute-start(f32[8,128]{1,0:T(8,128)S(1)} %get-tuple-element.61.curve_refs_0_), channel_id=1, source_target_pairs={{0,3},{1,2},{2,1},{3,0},{4,7},{5,6},{6,5},{7,4},{8,11},{9,10},{10,... | collective-permute-start | bytes 12296 | tf_op jit(solution)/shard_map/even_terms/ppermute | solution.py:339
  40.6 4.5 %collective-permute-start.15 = (f32[8,128]{1,0:T(8,128)S(1)}, f32[8,128]{1,0:T(8,128)S(1)}, u32[]{:S(2)}, u32[]{:S(2)}) collective-permute-start(f32[8,128]{1,0:T(8,128)S(1)} %get-tuple-element.61.curve_refs_0_), channel_id=1, source_target_pairs={{0,2},{1,3},{2,0},{3,1},{4,6},{5,7},{6,4},{7,5},{8,10},{9,11},{10,... | collective-permute-start | bytes 12296 | tf_op jit(solution)/shard_map/even_terms/ppermute | solution.py:339
  40.7 4.5 %collective-permute-start.14 = (f32[8,128]{1,0:T(8,128)S(1)}, f32[8,128]{1,0:T(8,128)S(1)}, u32[]{:S(2)}, u32[]{:S(2)}) collective-permute-start(f32[8,128]{1,0:T(8,128)S(1)} %get-tuple-element.61.curve_refs_0_), channel_id=1, source_target_pairs={{0,1},{1,0},{2,3},{3,2},{4,5},{5,4},{6,7},{7,6},{8,9},{9,8},{10,11... | collective-permute-start | bytes 12296 | tf_op jit(solution)/shard_map/even_terms/ppermute | solution.py:339
  45.2 1.3 %collective-permute-start.17 = (f32[136,128]{1,0:T(8,128)S(1)}, f32[136,128]{1,0:T(8,128)S(1)}, u32[]{:S(2)}, u32[]{:S(2)}) collective-permute-start(f32[136,128]{1,0:T(8,128)S(1)} %get-tuple-element.63), channel_id=1, source_target_pairs={{0,4},{4,0},{8,12},{12,8},{16,20},{20,16},{24,28},{28,24},{1,5},{5... | collective-permute-start | bytes 208904 | tf_op jit(solution)/shard_map/reduce_dir_sigma/ppermute | solution.py:333
  46.5 3.8 %collective-permute-start.18 = (f32[40,128]{1,0:T(8,128)S(1)}, f32[40,128]{1,0:T(8,128)S(1)}, u32[]{:S(2)}, u32[]{:S(2)}) collective-permute-start(f32[40,128]{1,0:T(8,128)S(1)} %get-tuple-element.65), channel_id=1, source_target_pairs={{0,8},{4,12},{8,0},{12,4},{16,24},{20,28},{24,16},{28,20},{1,9},{5... | collective-permute-start | bytes 61448 | tf_op jit(solution)/shard_map/reduce_dir_sigma/ppermute | solution.py:336
  48.4 3.9 %collective-permute-start.19 = (f32[40,128]{1,0:T(8,128)S(1)}, f32[40,128]{1,0:T(8,128)S(1)}, u32[]{:S(2)}, u32[]{:S(2)}) collective-permute-start(f32[40,128]{1,0:T(8,128)S(1)} %get-tuple-element.66), channel_id=1, source_target_pairs={{0,16},{4,20},{8,24},{12,28},{16,0},{20,4},{24,8},{28,12},{1,17},{... | collective-permute-start | bytes 61448 | tf_op jit(solution)/shard_map/reduce_dir_sigma/ppermute | solution.py:336
  48.6 4.7 %collective-permute-start.20 = (f32[40,128]{1,0:T(8,128)S(1)}, f32[40,128]{1,0:T(8,128)S(1)}, u32[]{:S(2)}, u32[]{:S(2)}) collective-permute-start(f32[40,128]{1,0:T(8,128)S(1)} %get-tuple-element.67), channel_id=1, source_target_pairs={{0,24},{4,28},{8,16},{12,20},{16,8},{20,12},{24,0},{28,4},{1,25},{... | collective-permute-start | bytes 61448 | tf_op jit(solution)/shard_map/reduce_dir_sigma/ppermute | solution.py:336

commit v6 on v4

--- a/solution.py
+++ b/solution.py
@@ -68,14 +68,14 @@
 
 
 def pack_kernel(wave_ref, diag_ref, packed_ref, own_diag_ref, sems):
-    size = wave_ref.shape[1]
-    share = packed_ref.shape[0] - size
+    owned, size, _ = wave_ref.shape
+    share = packed_ref.shape[0] - owned * size
     ops = lax.axis_index("ops")
     core, chip = ops % 2, ops // 2
     rows = pl.ds(pl.multiple_of(chip * share, share), share)
     moves = [
-        (wave_ref.at[core], packed_ref.at[pl.ds(0, size)]),
-        (diag_ref.at[core, rows], packed_ref.at[pl.ds(size, share)]),
+        *((wave_ref.at[s], packed_ref.at[pl.ds(s * size, size)]) for s in range(owned)),
+        (diag_ref.at[core, rows], packed_ref.at[pl.ds(owned * size, share)]),
         (diag_ref.at[core], own_diag_ref),
     ]
     copies = [pltpu.make_async_copy(source, target, sems.at[i]) for i, (source, target) in enumerate(moves)]
@@ -90,7 +90,7 @@
 
 
 def partners(n_sec):
-    return [(m, m + 1) for m in range(1, n_sec - 1, 2)], n_sec - 1
+    return [(m, m + 1) for m in range(2, n_sec, 2)], 1
 
 
 def from_partner(n_sec, m, core, mine, theirs, last):
@@ -130,7 +130,7 @@
 def join_kernel(keep_ref, got_ref, last_ref, out_ref):
     rows, size = keep_ref.shape
     out_ref[:rows] = keep_ref[...] + got_ref[...]
-    out_ref[rows:] = last_ref[size:]
+    out_ref[rows:] = last_ref[2 * size :]
 
 
 def plane_kernel(part_refs, sum_ref, diag_ref):
@@ -147,7 +147,7 @@
 
 
 def first_kernel(n_sec, n_ops, source_ref, coupling_ref, pairs_ref, weights_ref, local_ref, mine_refs, theirs_refs,
-                 last_ref, other_last_ref, keep_ref, send_ref, norm_ref, slots, stacked):
+                 last_ref, keep_ref, send_ref, norm_ref, slots, stacked):
     size = local_ref.shape[1]
     core = lax.axis_index("ops") % 2
     pairs, last = partners(n_sec)
@@ -155,7 +155,7 @@
     for i, (even, odd) in enumerate(pairs):
         for refs, m in ((mine_refs, jnp.where(core == 0, even, odd)), (theirs_refs, jnp.where(core == 0, odd, even))):
             blocks += [(2 * m + s, refs[i][s]) for s in range(2)]
-    blocks += [(2 * last + core, last_ref[:size]), (2 * last + 1 - core, other_last_ref[:size])]
+    blocks += [(2 * last + s, last_ref[s * size : (s + 1) * size]) for s in range(2)]
     acc = jnp.zeros((size, size), F32)
     for at, block in blocks:
         acc += block * block
@@ -168,7 +168,7 @@
     for s in range(2):
         partner = from_partner(
             n_sec, n_sec // 2, core, lambda i: mine_refs[i][s], lambda i: theirs_refs[i][s],
-            lambda: jnp.where(core == s, last_ref[:size], other_last_ref[:size]),
+            lambda: last_ref[s * size : (s + 1) * size],
         )
         blocks.append(part[s * size : (s + 1) * size] + (coupling_ref[0, s] / n_ops) * partner.T)
         corr += total(local_ref[s] * blocks[s])
@@ -181,6 +181,7 @@
 def correction_kernel(n_sec, norm_ref, sector_refs, mine_refs, theirs_refs, last_refs, diag_refs, other_diag_refs, sum_refs, out_ref):
     size = sector_refs[1].shape[0]
     core = lax.axis_index("ops") % 2
+    sector = pl.ds(pl.multiple_of(core * size, size), size)
     norm_sq = norm_ref[:1, :1]
     corr = sum_refs[0][size : size + 1, :1]
     for ref in sum_refs[1:]:
@@ -191,10 +192,10 @@
     sums = [jnp.zeros((size, size), F32) for _ in range(5)]
     for m in range(n_sec):
         if m == 0:
-            wave, diag = sector_refs[0][:size], sector_refs[1][...]
+            wave, diag = sector_refs[0][sector], sector_refs[1][...]
         else:
             wave = from_partner(
-                n_sec, m, core, lambda i: mine_refs[i][core], lambda i: theirs_refs[i][core], lambda: last_refs[0][:size]
+                n_sec, m, core, lambda i: mine_refs[i][core], lambda i: theirs_refs[i][core], lambda: last_refs[0][sector]
             )
             diag = from_partner(
                 n_sec, m, core, lambda i: diag_refs[i][core], lambda i: other_diag_refs[i][...], lambda: last_refs[1][...]
@@ -361,9 +362,9 @@
         mine = [to_planes(wavefunction, pair) for pair in zs]
         sectors = call(
             pack_kernel,
-            (shape((size + size // chips, size), F32), shape((size, size), F32)),
+            (shape((owned * size + size // chips, size), F32), shape((size, size), F32)),
             [HBM] * 2,
-            [pltpu.SemaphoreType.DMA((3,))],
+            [pltpu.SemaphoreType.DMA((owned + 2,))],
             limit=SMALL,
         )(in_hbm(wavefunction), in_hbm(hamiltonian_diag))
         mine.append(to_plane(sectors[0], last))
@@ -386,19 +387,19 @@
             ],
             limit=SMALL,
         )(*[in_hbm(values) for values in held])
-        loaded, mine = lax.optimization_barrier((loaded, mine))
+        loaded, mine[:-1] = lax.optimization_barrier((loaded, mine[:-1]))
         pairs, weights, local, source, coupling = loaded
     with jax.named_scope("swap_wave"):
+        *mine, last = mine
         theirs = [swap(values) for values in mine]
-        (*mine, last), (*theirs, other_last) = mine, theirs
     with jax.named_scope("first_apply"):
         keep, send, norm = call(
             functools.partial(first_kernel, n_sec, n_ops),
             (message_shape, message_shape, scalar_shape),
-            [SMEM, SMEM] + [VMEM] * 3 + [[VMEM] * len(zs)] * 2 + [VMEM] * 2,
+            [SMEM, SMEM] + [VMEM] * 3 + [[VMEM] * len(zs)] * 2 + [VMEM],
             [pltpu.VMEM(slot_shape, BF16), pltpu.VMEM(stack_shape, BF16)],
             matmul_flops,
-        )(source, coupling, pairs, weights, local, mine, theirs, last, other_last)
+        )(source, coupling, pairs, weights, local, mine, theirs, last)
     with jax.named_scope("reduce_sigma"):
         joined = call(
             join_kernel, shape((size + PAD + size // chips, size), F32), [VMEM] * 3, limit=SMALL

time: 54.2 us -> 54.4 us (level)
  waiting for transfers between devices: 17.5 us -> 19.2 us
  starting transfers between devices: 24.1 us -> 22.6 us
    ppermute x7, starting transfers between devices: 11.4 us -> 10.5 us  [to_plane(): return lax.ppermute(values, 'sec', [(i, i ^ m) for i in range(n_sec)])]
    ppermute x2, waiting for transfers between devices: 0.01 us -> 0.9 us  [to_planes(): return lax.ppermute(values, ('ops', 'sec'), moves)]
    ppermute x6 -> x5, starting transfers between devices: 1.11 us -> 0.29 us  [swap(): return lax.ppermute(values, 'ops', [(i, i ^ 1) for i in range(n_ops)])]
    ppermute x7, waiting for transfers between devices: 4.66 us -> 5.29 us  [to_plane(): return lax.ppermute(values, 'sec', [(i, i ^ m) for i in range(n_sec)])]
    ppermute x6 -> x5, waiting for transfers between devices: 5.07 us -> 4.83 us  [swap(): return lax.ppermute(values, 'ops', [(i, i ^ 1) for i in range(n_ops)])]
  transfers between devices with their start and end apart: 21 -> 20, of which waited for: 14 -> 14; matrix products, arithmetic and copies ran while one was open for 0% -> 0% of each run, Pallas kernels for 11% -> 11%
where the time goes in v6:
time: 54.4 us; the launch traced here: 54.2 us
  starting transfers between devices  22.6 us (42%)
  waiting for transfers between devices  19.2 us (35%)
  Pallas kernels  11.7 us (22%)
  between operations  0.77 us (1%)
    ppermute x7, starting transfers between devices, to_plane(): return lax.ppermute(values, 'sec', [(i, i ^ m) for i in range(n_sec)])  10.5 us
    ppermute x6, waiting for transfers between devices, to_chip(): return lax.ppermute(values, 'ops', [(i, i ^ 2 * m) for i in range(n_ops)])  8.15 us
    ppermute x6, starting transfers between devices, to_chip(): return lax.ppermute(values, 'ops', [(i, i ^ 2 * m) for i in range(n_ops)])  7.11 us
    ppermute x7, waiting for transfers between devices, to_plane(): return lax.ppermute(values, 'sec', [(i, i ^ m) for i in range(n_sec)])  5.29 us
    ppermute x5, waiting for transfers between devices, swap(): return lax.ppermute(values, 'ops', [(i, i ^ 1) for i in range(n_ops)])  4.83 us
    ppermute x2, starting transfers between devices, to_planes(): return lax.ppermute(values, ('ops', 'sec'), moves)  4.62 us
    pallas_call x1, Pallas kernels, body(): call(load_kernel, (shape((terms, owned, size, 2 * size), BF16), shape((2...  3.28 us
    pallas_call x1, Pallas kernels, body(): call(functools.partial(first_kernel, n_sec, n_ops), (message_shape, messa...  2.83 us
  transfers between devices with their start and end apart: 20, of which 14 were waited for; matrix products, arithmetic and copies ran while one was open for 0% of the time, Pallas kernels for 11%

profile of v6, /device:TPU:0, one launch (start us, length us, event | category | flops | bytes accessed | tf_op | source)
XLA Modules:
  0.0 54.2 jit_solution(703052656919678071)
XLA Ops:
  0.6 4.1 %collective-permute-start = (f32[2,128,128]{2,1,0:T(8,128)}, f32[2,128,128]{2,1,0:T(8,128)S(1)}, u32[]{:S(2)}, u32[]{:S(2)}) collective-permute-start(f32[2,128,128]{2,1,0:T(8,128)} %wave_ref.3), channel_id=1, source_target_pairs={{0,2},{1,3},{2,0},{3,1},{4,7},{5,6},{6,5},{7,4},{8,10},{9,11},{10,... | collective-permute-start | bytes 393224 | tf_op jit(solution)/shard_map/gather_wave/ppermute | solution.py:344
  4.7 1.0 %gather_wave.1 = (f32[288,128]{1,0:T(8,128)S(1)}, f32[128,128]{1,0:T(8,128)S(1)}) custom-call(f32[2,128,128]{2,1,0:T(8,128)} %wave_ref.3, f32[2,128,128]{2,1,0:T(8,128)} %diag_ref.1), custom_call_target="tpu_custom_call" | custom-call | bytes 1048576 | tf_op jit(solution)/shard_map/gather_wave/pallas_call | solution.py:363
  5.7 1.6 %collective-permute-start.2 = (f32[288,128]{1,0:T(8,128)S(1)}, f32[288,128]{1,0:T(8,128)S(1)}, u32[]{:S(2)}, u32[]{:S(2)}) collective-permute-start(f32[288,128]{1,0:T(8,128)S(1)} %get-tuple-element.48.sector_refs_0_), channel_id=1, source_target_pairs={{0,1},{1,0},{2,3},{3,2},{4,5},{5,4},{6,7},{7,6},{8,9},{9,8},{10,11... | collective-permute-start | bytes 442376 | tf_op jit(solution)/shard_map/gather_wave/ppermute | solution.py:340
  7.3 3.3 %load.1 = (bf16[24,2,128,256]{3,2,1,0:T(8,128)(2,1)S(1)}, bf16[6144,256]{1,0:T(8,128)(2,1)S(1)}, f32[2,128,128]{2,1,0:T(8,128)S(1)}, s32[2,24]{1,0:T(2,128)S(1)}, f32[1,2]{1,0:T(1,128)S(1)}) custom-call(f32[24,2,128,128]{3,2,1,0:T(8,128)} %left_ref.1, f32[24,128,128]{2,1,0:T(8,128)} %right_ref.1, f32[2,128,128]{2,1,0:T(8,128)} %wave_ref.3, s32[2,24]{1,0:T(2,128)} %bitcast.4, ...), custom_call_target="tpu_custom_call" | custom-call | bytes 1048576 | tf_op jit(solution)/shard_map/load/pallas_call | solution.py:375
  10.6 0.9 %collective-permute-done.mine_refs_0_ = f32[2,128,128]{2,1,0:T(8,128)S(1)} collective-permute-done((f32[2,128,128]{2,1,0:T(8,128)}, f32[2,128,128]{2,1,0:T(8,128)S(1)}, u32[]{:S(2)}, u32[]{:S(2)}) %collective-permute-start) | collective-permute-done | bytes 131104 | tf_op jit(solution)/shard_map/gather_wave/ppermute | solution.py:344
  11.5 1.7 %collective-permute-done.2.last_ref.last_refs_0_ = f32[288,128]{1,0:T(8,128)S(1)} collective-permute-done((f32[288,128]{1,0:T(8,128)S(1)}, f32[288,128]{1,0:T(8,128)S(1)}, u32[]{:S(2)}, u32[]{:S(2)}) %collective-permute-start.2) | collective-permute-done | bytes 147488 | tf_op jit(solution)/shard_map/gather_wave/ppermute | solution.py:340
  13.2 2.8 %first_apply.1 = (f32[136,128]{1,0:T(8,128)S(1)}, f32[136,128]{1,0:T(8,128)S(1)}, f32[8,128]{1,0:T(8,128)S(1)}) custom-call(s32[2,24]{1,0:T(2,128)S(1)} %get-tuple-element.42.source_ref, f32[1,2]{1,0:T(1,128)S(1)} %get-tuple-element.43.coupling_ref, bf16[24,2,128,256]{3,2,1,0:T(8,128)(2,1)S(1)} %get-tuple-element.44.pairs_ref, ...), custom_call_target="tpu_custom_call" | custom-call | flops 1207959552 | bytes 1048576 | tf_op jit(solution)/shard_map/first_apply/pallas_call | solution.py:396
  16.1 0.5 collective-permute-start.7
  16.7 0.7 %collective-permute-done.3.got_ref = f32[136,128]{1,0:T(8,128)S(1)} collective-permute-done((f32[136,128]{1,0:T(8,128)S(1)}, f32[136,128]{1,0:T(8,128)S(1)}, u32[]{:S(2)}, u32[]{:S(2)}) %collective-permute-start.3) | collective-permute-done | bytes 69664 | tf_op jit(solution)/shard_map/reduce_sigma/ppermute | solution.py:334
  17.4 2.7 %collective-permute-start.6 = (f32[168,128]{1,0:T(8,128)S(1)}, f32[168,128]{1,0:T(8,128)S(1)}, u32[]{:S(2)}, u32[]{:S(2)}) collective-permute-start(f32[168,128]{1,0:T(8,128)S(1)} %reduce_sigma.2.part_refs_0_), channel_id=1, source_target_pairs={{0,24},{4,28},{8,16},{12,20},{16,8},{20,12},{24,0},{28,4},{1,25},{... | collective-permute-start | bytes 258056 | tf_op jit(solution)/shard_map/reduce_sigma/ppermute | solution.py:337
  20.1 0.5 collective-permute-start.5
  20.9 2.3 %collective-permute-done.6.part_refs_3_ = f32[168,128]{1,0:T(8,128)S(1)} collective-permute-done((f32[168,128]{1,0:T(8,128)S(1)}, f32[168,128]{1,0:T(8,128)S(1)}, u32[]{:S(2)}, u32[]{:S(2)}) %collective-permute-start.6) | collective-permute-done | bytes 86048 | tf_op jit(solution)/shard_map/reduce_sigma/ppermute | solution.py:337
  23.2 2.4 %collective-permute-done.5.part_refs_2_ = f32[168,128]{1,0:T(8,128)S(1)} collective-permute-done((f32[168,128]{1,0:T(8,128)S(1)}, f32[168,128]{1,0:T(8,128)S(1)}, u32[]{:S(2)}, u32[]{:S(2)}) %collective-permute-start.5) | collective-permute-done | bytes 86048 | tf_op jit(solution)/shard_map/reduce_sigma/ppermute | solution.py:337
  25.9 1.9 %collective-permute-start.11 = (f32[136,128]{1,0:T(8,128)S(1)}, f32[136,128]{1,0:T(8,128)S(1)}, u32[]{:S(2)}, u32[]{:S(2)}) collective-permute-start(f32[136,128]{1,0:T(8,128)S(1)} %get-tuple-element.54.sum_refs_0_), channel_id=1, source_target_pairs={{0,3},{1,2},{2,1},{3,0},{4,7},{5,6},{6,5},{7,4},{8,11},{9,10},{10,... | collective-permute-start | bytes 208904 | tf_op jit(solution)/shard_map/gather_sigma/ppermute | solution.py:340
  27.7 0.8 %collective-permute-start.10 = (f32[136,128]{1,0:T(8,128)S(1)}, f32[136,128]{1,0:T(8,128)S(1)}, u32[]{:S(2)}, u32[]{:S(2)}) collective-permute-start(f32[136,128]{1,0:T(8,128)S(1)} %get-tuple-element.54.sum_refs_0_), channel_id=1, source_target_pairs={{0,2},{1,3},{2,0},{3,1},{4,6},{5,7},{6,4},{7,5},{8,10},{9,11},{10,... | collective-permute-start | bytes 208904 | tf_op jit(solution)/shard_map/gather_sigma/ppermute | solution.py:340
  28.5 1.8 %collective-permute-start.9 = (f32[136,128]{1,0:T(8,128)S(1)}, f32[136,128]{1,0:T(8,128)S(1)}, u32[]{:S(2)}, u32[]{:S(2)}) collective-permute-start(f32[136,128]{1,0:T(8,128)S(1)} %get-tuple-element.54.sum_refs_0_), channel_id=1, source_target_pairs={{0,1},{1,0},{2,3},{3,2},{4,5},{5,4},{6,7},{7,6},{8,9},{9,8},{10,11... | collective-permute-start | bytes 208904 | tf_op jit(solution)/shard_map/gather_sigma/ppermute | solution.py:340
  30.4 1.2 %collective-permute-done.8.other_diag_refs_0_ = f32[128,128]{1,0:T(8,128)S(1)} collective-permute-done((f32[128,128]{1,0:T(8,128)S(1)}, f32[128,128]{1,0:T(8,128)S(1)}, u32[]{:S(2)}, u32[]{:S(2)}) %collective-permute-start.8) | collective-permute-done | bytes 65568 | tf_op jit(solution)/shard_map/swap_diag/ppermute | solution.py:334
  31.7 1.2 %collective-permute-done.11.sum_refs_3_ = f32[136,128]{1,0:T(8,128)S(1)} collective-permute-done((f32[136,128]{1,0:T(8,128)S(1)}, f32[136,128]{1,0:T(8,128)S(1)}, u32[]{:S(2)}, u32[]{:S(2)}) %collective-permute-start.11) | collective-permute-done | bytes 69664 | tf_op jit(solution)/shard_map/gather_sigma/ppermute | solution.py:340
  32.8 2.4 %collective-permute-done.10.sum_refs_2_ = f32[136,128]{1,0:T(8,128)S(1)} collective-permute-done((f32[136,128]{1,0:T(8,128)S(1)}, f32[136,128]{1,0:T(8,128)S(1)}, u32[]{:S(2)}, u32[]{:S(2)}) %collective-permute-start.10) | collective-permute-done | bytes 69664 | tf_op jit(solution)/shard_map/gather_sigma/ppermute | solution.py:340
  35.3 0.4 correction.1.mine_ref
  35.7 1.6 %collective-permute-done.12.theirs_ref = f32[648,128]{1,0:T(8,128)S(1)} collective-permute-done((f32[648,128]{1,0:T(8,128)S(1)}, f32[648,128]{1,0:T(8,128)S(1)}, u32[]{:S(2)}, u32[]{:S(2)}) %collective-permute-start.12) | collective-permute-done | bytes 331808 | tf_op jit(solution)/shard_map/correction/ppermute | solution.py:334
  37.4 1.9 %even_terms.1 = (bf16[9,256,256]{2,1,0:T(8,128)(2,1)S(1)}, f32[2,128,128]{2,1,0:T(8,128)S(1)}, f32[8,128]{1,0:T(8,128)S(1)}, f32[4,16,128]{2,1,0:T(8,128)S(1)}, f32[8,128]{1,0:T(8,128)S(1)}) custom-call(s32[2,24]{1,0:T(2,128)S(1)} %get-tuple-element.42.source_ref, f32[1,2]{1,0:T(1,128)S(1)} %get-tuple-element.43.coupling_ref, ...), custom_call_target="tpu_custom_call" | custom-call | flops 603979776 | bytes 1048576 | tf_op jit(solution)/shard_map/even_terms/pallas_call | solution.py:425
  39.2 1.4 %collective-permute-start.15 = (f32[8,128]{1,0:T(8,128)S(1)}, f32[8,128]{1,0:T(8,128)S(1)}, u32[]{:S(2)}, u32[]{:S(2)}) collective-permute-start(f32[8,128]{1,0:T(8,128)S(1)} %get-tuple-element.61.curve_refs_0_), channel_id=1, source_target_pairs={{0,3},{1,2},{2,1},{3,0},{4,7},{5,6},{6,5},{7,4},{8,11},{9,10},{10,... | collective-permute-start | bytes 12296 | tf_op jit(solution)/shard_map/even_terms/ppermute | solution.py:340
  40.6 3.1 %collective-permute-start.13 = (f32[8,128]{1,0:T(8,128)S(1)}, f32[8,128]{1,0:T(8,128)S(1)}, u32[]{:S(2)}, u32[]{:S(2)}) collective-permute-start(f32[8,128]{1,0:T(8,128)S(1)} %get-tuple-element.61.curve_refs_0_), channel_id=1, source_target_pairs={{0,1},{1,0},{2,3},{3,2},{4,5},{5,4},{6,7},{7,6},{8,9},{9,8},{10,11... | collective-permute-start | bytes 12296 | tf_op jit(solution)/shard_map/even_terms/ppermute | solution.py:340
  43.7 1.6 %odd_terms.1 = (f32[128,128]{1,0:T(8,128)S(1)}, f32[128,128]{1,0:T(8,128)S(1)}) custom-call(s32[2,24]{1,0:T(2,128)S(1)} %get-tuple-element.42.source_ref, bf16[24,2,128,256]{3,2,1,0:T(8,128)(2,1)S(1)} %get-tuple-element.44.pairs_ref, bf16[6144,256]{1,0:T(8,128)(2,1)S(1)} %get-tuple-element.45.weights_ref, bf16[9,256,256]{2,1,0:T(8,128)(2,1)S(1)} %get-tuple-element.57.slots, ...), custom_call_target="tpu_custom_call" | custom-call | flops 603979776 | bytes 1048576 | tf_op jit(solution)/shard_map/odd_terms/pallas_call | solution.py:440
  45.4 1.2 %collective-permute-done.16.got_ref = f32[136,128]{1,0:T(8,128)S(1)} collective-permute-done((f32[136,128]{1,0:T(8,128)S(1)}, f32[136,128]{1,0:T(8,128)S(1)}, u32[]{:S(2)}, u32[]{:S(2)}) %collective-permute-start.16) | collective-permute-done | bytes 69664 | tf_op jit(solution)/shard_map/reduce_dir_sigma/ppermute | solution.py:334
  46.7 1.4 %collective-permute-start.17 = (f32[40,128]{1,0:T(8,128)S(1)}, f32[40,128]{1,0:T(8,128)S(1)}, u32[]{:S(2)}, u32[]{:S(2)}) collective-permute-start(f32[40,128]{1,0:T(8,128)S(1)} %get-tuple-element.65), channel_id=1, source_target_pairs={{0,8},{4,12},{8,0},{12,4},{16,24},{20,28},{24,16},{28,20},{1,9},{5... | collective-permute-start | bytes 61448 | tf_op jit(solution)/shard_map/reduce_dir_sigma/ppermute | solution.py:337
  48.1 0.8 %collective-permute-start.18 = (f32[40,128]{1,0:T(8,128)S(1)}, f32[40,128]{1,0:T(8,128)S(1)}, u32[]{:S(2)}, u32[]{:S(2)}) collective-permute-start(f32[40,128]{1,0:T(8,128)S(1)} %get-tuple-element.66), channel_id=1, source_target_pairs={{0,16},{4,20},{8,24},{12,28},{16,0},{20,4},{24,8},{28,12},{1,17},{... | collective-permute-start | bytes 61448 | tf_op jit(solution)/shard_map/reduce_dir_sigma/ppermute | solution.py:337
  48.8 1.4 %collective-permute-start.19 = (f32[40,128]{1,0:T(8,128)S(1)}, f32[40,128]{1,0:T(8,128)S(1)}, u32[]{:S(2)}, u32[]{:S(2)}) collective-permute-start(f32[40,128]{1,0:T(8,128)S(1)} %get-tuple-element.67), channel_id=1, source_target_pairs={{0,24},{4,28},{8,16},{12,20},{16,8},{20,12},{24,0},{28,4},{1,25},{... | collective-permute-start | bytes 61448 | tf_op jit(solution)/shard_map/reduce_dir_sigma/ppermute | solution.py:337
  50.5 1.3 %collective-permute-done.18.got_refs_2_ = f32[40,128]{1,0:T(8,128)S(1)} collective-permute-done((f32[40,128]{1,0:T(8,128)S(1)}, f32[40,128]{1,0:T(8,128)S(1)}, u32[]{:S(2)}, u32[]{:S(2)}) %collective-permute-start.18) | collective-permute-done | bytes 20512 | tf_op jit(solution)/shard_map/reduce_dir_sigma/ppermute | solution.py:337
  51.8 1.7 %collective-permute-done.19.got_refs_3_ = f32[40,128]{1,0:T(8,128)S(1)} collective-permute-done((f32[40,128]{1,0:T(8,128)S(1)}, f32[40,128]{1,0:T(8,128)S(1)}, u32[]{:S(2)}, u32[]{:S(2)}) %collective-permute-start.19) | collective-permute-done | bytes 20512 | tf_op jit(solution)/shard_map/reduce_dir_sigma/ppermute | solution.py:337
  53.5 0.7 %ritz.1 = (f32[2,16,128]{2,1,0:T(8,128)}, f32[2,16,128]{2,1,0:T(8,128)}, f32[1,128]{1,0:T(1,128)}) custom-call(f32[8,128]{1,0:T(8,128)S(1)} %get-tuple-element.55.scalar_ref, f32[2,128,128]{2,1,0:T(8,128)S(1)} %get-tuple-element.46.local_ref, f32[4,16,128]{2,1,0:T(8,128)S(1)} %get-tuple-element.56.own_ref, f32[40,128]{1,0:T(8,128)S(1)} %get-tuple-element.64.got_refs_0_, ...), custom_call_target="tpu_custom_call" | custom-call | bytes 1048576 | tf_op jit(solution)/shard_map/ritz/pallas_call | solution.py:454
  (22 shorter events, 1.3 us)
Async XLA Ops:
  0.6 10.9 %collective-permute-start = (f32[2,128,128]{2,1,0:T(8,128)}, f32[2,128,128]{2,1,0:T(8,128)S(1)}, u32[]{:S(2)}, u32[]{:S(2)}) collective-permute-start(f32[2,128,128]{2,1,0:T(8,128)} %wave_ref.3), channel_id=1, source_target_pairs={{0,2},{1,3},{2,0},{3,1},{4,7},{5,6},{6,5},{7,4},{8,10},{9,11},{10,... | collective-permute-start | bytes 393224 | tf_op jit(solution)/shard_map/gather_wave/ppermute | solution.py:344
  5.7 7.5 %collective-permute-start.2 = (f32[288,128]{1,0:T(8,128)S(1)}, f32[288,128]{1,0:T(8,128)S(1)}, u32[]{:S(2)}, u32[]{:S(2)}) collective-permute-start(f32[288,128]{1,0:T(8,128)S(1)} %get-tuple-element.48.sector_refs_0_), channel_id=1, source_target_pairs={{0,1},{1,0},{2,3},{3,2},{4,5},{5,4},{6,7},{7,6},{8,9},{9,8},{10,11... | collective-permute-start | bytes 442376 | tf_op jit(solution)/shard_map/gather_wave/ppermute | solution.py:340
  11.5 4.6 %copy-start = (f32[2,128,128]{2,1,0:T(8,128)S(1)}, f32[2,128,128]{2,1,0:T(8,128)}, u32[]{:S(2)}) copy-start(f32[2,128,128]{2,1,0:T(8,128)} %diag_ref.1) | copy-start | bytes 393220
  11.5 1.7 %collective-permute-start.1 = (f32[2,128,128]{2,1,0:T(8,128)S(1)}, f32[2,128,128]{2,1,0:T(8,128)S(1)}, u32[]{:S(2)}, u32[]{:S(2)}) collective-permute-start(f32[2,128,128]{2,1,0:T(8,128)S(1)} %collective-permute-done.mine_refs_0_), channel_id=1, source_target_pairs={{0,4},{4,0},{8,12},{12,8},{16,20},{20,16},{24,28},{28,24},{1,5},{5... | collective-permute-start | bytes 393224 | tf_op jit(solution)/shard_map/swap_wave/ppermute | solution.py:334
  16.1 1.3 %collective-permute-start.3 = (f32[136,128]{1,0:T(8,128)S(1)}, f32[136,128]{1,0:T(8,128)S(1)}, u32[]{:S(2)}, u32[]{:S(2)}) collective-permute-start(f32[136,128]{1,0:T(8,128)S(1)} %get-tuple-element.52), channel_id=1, source_target_pairs={{0,4},{4,0},{8,12},{12,8},{16,20},{20,16},{24,28},{28,24},{1,5},{5... | collective-permute-start | bytes 208904 | tf_op jit(solution)/shard_map/reduce_sigma/ppermute | solution.py:334
  16.1 14.2 %collective-permute-start.7 = (f32[2,128,128]{2,1,0:T(8,128)S(1)}, f32[2,128,128]{2,1,0:T(8,128)S(1)}, u32[]{:S(2)}, u32[]{:S(2)}) collective-permute-start(f32[2,128,128]{2,1,0:T(8,128)S(1)} %copy-done), channel_id=1, source_target_pairs={{0,2},{1,3},{2,0},{3,1},{4,7},{5,6},{6,5},{7,4},{8,10},{9,11},{10,... | collective-permute-start | bytes 393224 | tf_op jit(solution)/shard_map/gather_diag/ppermute | solution.py:344
  17.4 5.8 %collective-permute-start.6 = (f32[168,128]{1,0:T(8,128)S(1)}, f32[168,128]{1,0:T(8,128)S(1)}, u32[]{:S(2)}, u32[]{:S(2)}) collective-permute-start(f32[168,128]{1,0:T(8,128)S(1)} %reduce_sigma.2.part_refs_0_), channel_id=1, source_target_pairs={{0,24},{4,28},{8,16},{12,20},{16,8},{20,12},{24,0},{28,4},{1,25},{... | collective-permute-start | bytes 258056 | tf_op jit(solution)/shard_map/reduce_sigma/ppermute | solution.py:337
  20.1 5.5 %collective-permute-start.5 = (f32[168,128]{1,0:T(8,128)S(1)}, f32[168,128]{1,0:T(8,128)S(1)}, u32[]{:S(2)}, u32[]{:S(2)}) collective-permute-start(f32[168,128]{1,0:T(8,128)S(1)} %reduce_sigma.2.part_refs_0_), channel_id=1, source_target_pairs={{0,16},{4,20},{8,24},{12,28},{16,0},{20,4},{24,8},{28,12},{1,17},{... | collective-permute-start | bytes 258056 | tf_op jit(solution)/shard_map/reduce_sigma/ppermute | solution.py:337
  20.6 5.3 %collective-permute-start.4 = (f32[168,128]{1,0:T(8,128)S(1)}, f32[168,128]{1,0:T(8,128)S(1)}, u32[]{:S(2)}, u32[]{:S(2)}) collective-permute-start(f32[168,128]{1,0:T(8,128)S(1)} %reduce_sigma.2.part_refs_0_), channel_id=1, source_target_pairs={{0,8},{4,12},{8,0},{12,4},{16,24},{20,28},{24,16},{28,20},{1,9},{5... | collective-permute-start | bytes 258056 | tf_op jit(solution)/shard_map/reduce_sigma/ppermute | solution.py:337
  25.9 6.9 %collective-permute-start.11 = (f32[136,128]{1,0:T(8,128)S(1)}, f32[136,128]{1,0:T(8,128)S(1)}, u32[]{:S(2)}, u32[]{:S(2)}) collective-permute-start(f32[136,128]{1,0:T(8,128)S(1)} %get-tuple-element.54.sum_refs_0_), channel_id=1, source_target_pairs={{0,3},{1,2},{2,1},{3,0},{4,7},{5,6},{6,5},{7,4},{8,11},{9,10},{10,... | collective-permute-start | bytes 208904 | tf_op jit(solution)/shard_map/gather_sigma/ppermute | solution.py:340
  27.7 7.5 %collective-permute-start.10 = (f32[136,128]{1,0:T(8,128)S(1)}, f32[136,128]{1,0:T(8,128)S(1)}, u32[]{:S(2)}, u32[]{:S(2)}) collective-permute-start(f32[136,128]{1,0:T(8,128)S(1)} %get-tuple-element.54.sum_refs_0_), channel_id=1, source_target_pairs={{0,2},{1,3},{2,0},{3,1},{4,6},{5,7},{6,4},{7,5},{8,10},{9,11},{10,... | collective-permute-start | bytes 208904 | tf_op jit(solution)/shard_map/gather_sigma/ppermute | solution.py:340
  28.5 6.8 %collective-permute-start.9 = (f32[136,128]{1,0:T(8,128)S(1)}, f32[136,128]{1,0:T(8,128)S(1)}, u32[]{:S(2)}, u32[]{:S(2)}) collective-permute-start(f32[136,128]{1,0:T(8,128)S(1)} %get-tuple-element.54.sum_refs_0_), channel_id=1, source_target_pairs={{0,1},{1,0},{2,3},{3,2},{4,5},{5,4},{6,7},{7,6},{8,9},{9,8},{10,11... | collective-permute-start | bytes 208904 | tf_op jit(solution)/shard_map/gather_sigma/ppermute | solution.py:340
  30.3 1.3 %collective-permute-start.8 = (f32[128,128]{1,0:T(8,128)S(1)}, f32[128,128]{1,0:T(8,128)S(1)}, u32[]{:S(2)}, u32[]{:S(2)}) collective-permute-start(f32[128,128]{1,0:T(8,128)S(1)} %swap_diag.1), channel_id=1, source_target_pairs={{0,4},{4,0},{8,12},{12,8},{16,20},{20,16},{24,28},{28,24},{1,5},{5... | collective-permute-start | bytes 196616 | tf_op jit(solution)/shard_map/swap_diag/ppermute | solution.py:334
  35.7 1.7 %collective-permute-start.12 = (f32[648,128]{1,0:T(8,128)S(1)}, f32[648,128]{1,0:T(8,128)S(1)}, u32[]{:S(2)}, u32[]{:S(2)}) collective-permute-start(f32[648,128]{1,0:T(8,128)S(1)} %correction.1.mine_ref), channel_id=1, source_target_pairs={{0,4},{4,0},{8,12},{12,8},{16,20},{20,16},{24,28},{28,24},{1,5},{5... | collective-permute-start | bytes 995336 | tf_op jit(solution)/shard_map/correction/ppermute | solution.py:334
  39.2 6.0 %collective-permute-start.15 = (f32[8,128]{1,0:T(8,128)S(1)}, f32[8,128]{1,0:T(8,128)S(1)}, u32[]{:S(2)}, u32[]{:S(2)}) collective-permute-start(f32[8,128]{1,0:T(8,128)S(1)} %get-tuple-element.61.curve_refs_0_), channel_id=1, source_target_pairs={{0,3},{1,2},{2,1},{3,0},{4,7},{5,6},{6,5},{7,4},{8,11},{9,10},{10,... | collective-permute-start | bytes 12296 | tf_op jit(solution)/shard_map/even_terms/ppermute | solution.py:340
  40.6 4.7 %collective-permute-start.14 = (f32[8,128]{1,0:T(8,128)S(1)}, f32[8,128]{1,0:T(8,128)S(1)}, u32[]{:S(2)}, u32[]{:S(2)}) collective-permute-start(f32[8,128]{1,0:T(8,128)S(1)} %get-tuple-element.61.curve_refs_0_), channel_id=1, source_target_pairs={{0,2},{1,3},{2,0},{3,1},{4,6},{5,7},{6,4},{7,5},{8,10},{9,11},{10,... | collective-permute-start | bytes 12296 | tf_op jit(solution)/shard_map/even_terms/ppermute | solution.py:340
  40.6 4.7 %collective-permute-start.13 = (f32[8,128]{1,0:T(8,128)S(1)}, f32[8,128]{1,0:T(8,128)S(1)}, u32[]{:S(2)}, u32[]{:S(2)}) collective-permute-start(f32[8,128]{1,0:T(8,128)S(1)} %get-tuple-element.61.curve_refs_0_), channel_id=1, source_target_pairs={{0,1},{1,0},{2,3},{3,2},{4,5},{5,4},{6,7},{7,6},{8,9},{9,8},{10,11... | collective-permute-start | bytes 12296 | tf_op jit(solution)/shard_map/even_terms/ppermute | solution.py:340
  45.3 1.3 %collective-permute-start.16 = (f32[136,128]{1,0:T(8,128)S(1)}, f32[136,128]{1,0:T(8,128)S(1)}, u32[]{:S(2)}, u32[]{:S(2)}) collective-permute-start(f32[136,128]{1,0:T(8,128)S(1)} %get-tuple-element.63), channel_id=1, source_target_pairs={{0,4},{4,0},{8,12},{12,8},{16,20},{20,16},{24,28},{28,24},{1,5},{5... | collective-permute-start | bytes 208904 | tf_op jit(solution)/shard_map/reduce_dir_sigma/ppermute | solution.py:334
  46.7 3.8 %collective-permute-start.17 = (f32[40,128]{1,0:T(8,128)S(1)}, f32[40,128]{1,0:T(8,128)S(1)}, u32[]{:S(2)}, u32[]{:S(2)}) collective-permute-start(f32[40,128]{1,0:T(8,128)S(1)} %get-tuple-element.65), channel_id=1, source_target_pairs={{0,8},{4,12},{8,0},{12,4},{16,24},{20,28},{24,16},{28,20},{1,9},{5... | collective-permute-start | bytes 61448 | tf_op jit(solution)/shard_map/reduce_dir_sigma/ppermute | solution.py:337
  48.1 3.8 %collective-permute-start.18 = (f32[40,128]{1,0:T(8,128)S(1)}, f32[40,128]{1,0:T(8,128)S(1)}, u32[]{:S(2)}, u32[]{:S(2)}) collective-permute-start(f32[40,128]{1,0:T(8,128)S(1)} %get-tuple-element.66), channel_id=1, source_target_pairs={{0,16},{4,20},{8,24},{12,28},{16,0},{20,4},{24,8},{28,12},{1,17},{... | collective-permute-start | bytes 61448 | tf_op jit(solution)/shard_map/reduce_dir_sigma/ppermute | solution.py:337
  48.8 4.7 %collective-permute-start.19 = (f32[40,128]{1,0:T(8,128)S(1)}, f32[40,128]{1,0:T(8,128)S(1)}, u32[]{:S(2)}, u32[]{:S(2)}) collective-permute-start(f32[40,128]{1,0:T(8,128)S(1)} %get-tuple-element.67), channel_id=1, source_target_pairs={{0,24},{4,28},{8,16},{12,20},{16,8},{20,12},{24,0},{28,4},{1,25},{... | collective-permute-start | bytes 61448 | tf_op jit(solution)/shard_map/reduce_dir_sigma/ppermute | solution.py:337
